TPU v7x, 32 devices: a whole 2x2x4 slice. The times are simulated.
32 devices in a mesh: tm: 4 (over y, x), gx: 8 (over z, core).
Axes of the slice: x: 2, y: 2, z: 4, core: 2. Of those that a mesh axis runs over, the one named last changes fastest.
Arguments:
- start_states: float32 [4, 128, 128, 128], P('tm', 'gx'), may hold values from -1.2 to 1.2
- mobility: float32 [128, 128, 128], P('gx'), may hold values from 0.25 to 1
Outputs:
- end_state: float32 [4, 128, 128, 128], P('tm', 'gx')
- next_start: float32 [4, 128, 128, 128], P('tm', 'gx')
All inputs are finite; a program needn't handle non-finite values.
Results may differ from a plain program's by a relative error of at most 0.0001.
Values sent between devices are 32-bit elements; how exact they have to be, the bound alone decides.
No kernel may reach another device: no remote copies, remote signals or barrier semaphores. Data moves between devices by JAX's collectives and lax.ppermute only.
A program may use at most 128 MiB of HBM per device.

v0:
```python
import math

import jax
import jax.numpy as jnp
from jax import lax
from jax.sharding import PartitionSpec as P

KY = 64
KZ = 64
ITERS = 2


time_step = 0.05


def with_halo(cells, sides, width):
    for axis, dim in sides:
        count = lax.axis_size(axis)
        ends = count - 1
        head = lax.slice_in_dim(cells, 0, width, axis=dim)
        tail = lax.slice_in_dim(cells, cells.shape[dim] - width, cells.shape[dim], axis=dim)
        cells = jnp.concatenate(
            [
                lax.ppermute(tail, axis, [(i, (i + 1) % count) for i in range(ends)]),
                cells,
                lax.ppermute(head, axis, [((i + 1) % count, i) for i in range(ends)]),
            ],
            axis=dim,
        )
    return cells


def shifted(value, axis, steps):
    count = lax.axis_size(axis)
    initial, last = (max(0, -steps), min(count, count - steps))
    return lax.ppermute(value, axis, [(source, source + steps) for source in range(initial, last)])


def basis_value(node_times, source, point):
    total = 1.0
    for other in range(5):
        if other != source:
            total = total * (point - node_times[other]) / (node_times[source] - node_times[other])
    return total


def picard_table():
    root = math.sqrt(3.0 / 7.0)
    node_times = [0.0, (1.0 - root) / 2.0, 0.5, (1.0 + root) / 2.0, 1.0]
    gauss_points = [-math.sqrt(0.6), 0.0, math.sqrt(0.6)]
    gauss_weights = [5.0 / 9.0, 8.0 / 9.0, 5.0 / 9.0]
    picard_rows = []
    for target in range(1, 5):
        upper = node_times[target]
        row_values = []
        for source in range(5):
            integral = 0.0
            for point, weight in zip(gauss_points, gauss_weights):
                integral = integral + 0.5 * upper * weight * basis_value(
                    node_times, source, 0.5 * upper * (1.0 + point)
                )
            row_values.append(integral)
        picard_rows.append(row_values)
    return picard_rows


def dct_rows(count, kept):
    freq = jnp.arange(kept, dtype=jnp.float32)[:, None]
    place = jnp.arange(count, dtype=jnp.float32)[None, :]
    matrix = jnp.cos(jnp.pi * (place + 0.5) * freq / count) * jnp.sqrt(2.0 / count)
    return jnp.where(freq == 0, matrix * jnp.sqrt(0.5), matrix)


def analyse(values):
    low_y = dct_rows(values.shape[1], KY)
    low_z = dct_rows(values.shape[2], KZ)
    hp = lax.Precision.HIGHEST
    coeffs = jnp.einsum("ky,xyz->xkz", low_y, values, precision=hp)
    coeffs = jnp.einsum("xkz,lz->xkl", coeffs, low_z, precision=hp)
    return coeffs.reshape(values.shape[0], KY * KZ)


def synthesise(coeffs, width_y, width_z):
    low_y = dct_rows(width_y, KY)
    low_z = dct_rows(width_z, KZ)
    hp = lax.Precision.HIGHEST
    blocks = coeffs.reshape(coeffs.shape[0], KY, KZ)
    back = jnp.einsum("xkl,lz->xkz", blocks, low_z, precision=hp)
    return jnp.einsum("ky,xkz->xyz", low_y, back, precision=hp)


def evaluate(padded, mobility):
    padded = jnp.pad(padded, ((0, 0), (0, 0), (1, 1), (1, 1)))
    values = padded[:, 1:-1, 1:-1, 1:-1]
    laplace = padded[:, 2:, 1:-1, 1:-1] + padded[:, :-2, 1:-1, 1:-1]
    laplace = laplace + padded[:, 1:-1, 2:, 1:-1] + padded[:, 1:-1, :-2, 1:-1]
    laplace = laplace + padded[:, 1:-1, 1:-1, 2:] + padded[:, 1:-1, 1:-1, :-2] - 6.0 * values
    return mobility * (laplace + values - values * values * values)


def sweep(start_value, nodes, mobility, picard_rows):
    fields = jnp.concatenate([start_value[None], nodes], axis=0)
    padded = with_halo(fields, (("gx", 1),), 1)
    node_rates = evaluate(padded, mobility)
    updated = []
    for target in range(4):
        total = picard_rows[target][0] * node_rates[0]
        for source in range(1, 5):
            total = total + picard_rows[target][source] * node_rates[source]
        updated.append(start_value + time_step * total)
    return jnp.stack(updated, axis=0)


def forward(end_value, start_value, receive_mask):
    width_y = start_value.shape[1]
    width_z = start_value.shape[2]
    arrived = shifted(end_value, "tm", 1)
    change = synthesise(analyse(arrived - start_value), width_y, width_z)
    return start_value + receive_mask * change


def body(start_states, mobility):
    picard_rows = picard_table()
    receive_mask = (lax.axis_index("tm") > 0).astype(jnp.float32)
    start_value = start_states[0]
    nodes = jnp.broadcast_to(start_value[None], (4,) + start_value.shape)
    end_value = start_value
    for iteration in range(ITERS):
        if iteration == 0:
            nodes = sweep(start_value, nodes, mobility, picard_rows)
        else:
            nodes = sweep(start_value, nodes, mobility, picard_rows)
        end_value = nodes[3]
        start_value = forward(end_value, start_value, receive_mask)
    return (end_value[None], start_value[None])


def solution(mesh):
    placed = (P("tm", "gx", None, None), P("gx", None, None))
    return jax.shard_map(
        body,
        mesh=mesh,
        in_specs=placed,
        out_specs=(P("tm", "gx", None, None), P("tm", "gx", None, None)),
        check_vma=False,
    )
```

profile of v0, /device:TPU:21, one launch (start us, length us, event | category | flops | bytes accessed | tf_op | source)
XLA Modules:
  0.0 152.4 jit_solution(6626093922065219752)
XLA Ops:
  0.6 1.6 %copy.4 = f32[1,16,128,128]{2,3,1,0:T(8,128)S(1)} copy(f32[1,16,128,128]{3,2,1,0:T(8,128)} %param.2) | data formatting | bytes 2097152 | tf_op args[0]
  2.7 2.0 %copy-done.2 = f32[4,16,128,128]{2,3,1,0:T(8,128)} copy-done((f32[4,16,128,128]{2,3,1,0:T(8,128)}, f32[4,16,128,128]{2,3,1,0:T(8,128)S(1)}, u32[]{:S(2)}) %copy-start.2) | copy-done | bytes 4194328
  4.7 3.8 %collective-permute-start.1 = (f32[5,1,128,128]{2,3,1,0:T(8,128)S(1)}, f32[5,1,128,128]{2,3,1,0:T(8,128)S(1)}, u32[]{:S(2)}, u32[]{:S(2)}) collective-permute-start(f32[5,1,128,128]{2,3,1,0:T(8,128)S(1)} %get-tuple-element.8), channel_id=1, source_target_pairs={{0,1},{1,2},{2,3},{3,4},{4,5},{5,6},{6,7},{8,9},{9,10},{10,11},{11... | collective-permute-start | bytes 983048 | tf_op jit(solution)/shard_map/ppermute | solution.py:24
  8.5 1.9 %collective-permute-start = (f32[5,1,128,128]{2,3,1,0:T(8,128)S(1)}, f32[5,1,128,128]{2,3,1,0:T(8,128)S(1)}, u32[]{:S(2)}, u32[]{:S(2)}) collective-permute-start(f32[5,1,128,128]{2,3,1,0:T(8,128)S(1)} %get-tuple-element.9), channel_id=1, source_target_pairs={{1,0},{2,1},{3,2},{4,3},{5,4},{6,5},{7,6},{9,8},{10,9},{11,10},{12... | collective-permute-start | bytes 983048 | tf_op jit(solution)/shard_map/ppermute | solution.py:26
  10.4 1.6 %copy.5 = f32[16,128,128]{1,2,0:T(8,128)S(1)} copy(f32[16,128,128]{2,1,0:T(8,128)} %param.3) | data formatting | bytes 2097152 | tf_op args[1]
  12.5 4.4 %collective-permute-done = f32[5,1,128,128]{2,3,1,0:T(8,128)S(1)} collective-permute-done((f32[5,1,128,128]{2,3,1,0:T(8,128)S(1)}, f32[5,1,128,128]{2,3,1,0:T(8,128)S(1)}, u32[]{:S(2)}, u32[]{:S(2)}) %collective-permute-start) | collective-permute-done | bytes 327712 | tf_op jit(solution)/shard_map/ppermute | solution.py:26
  17.6 9.5 %select_maximum_fusion.2 = f32[5,18,130,130]{2,3,1,0:T(8,128)S(1)} fusion(f32[5,1,128,128]{2,3,1,0:T(8,128)S(1)} %collective-permute-done, f32[5,1,128,128]{2,3,1,0:T(8,128)S(1)} %collective-permute-done.1, f32[4,16,128,128]{2,3,1,0:T(8,128)} %copy-done.2, f32[1,16,128,128]{2,3,1,0:T(8,128)S(1)} %copy.4), kind=kLoop, calls=%fused_computation.6 | loop fusion | flops 27378000 | bytes 11982240 | tf_op jit(solution)/shard_map/concatenate | solution.py:22
  27.2 6.9 %fusion.11 = f32[5,16,128,128]{2,3,1,0:T(8,128)S(1)} fusion(f32[4,16,128,128]{2,3,1,0:T(8,128)S(1)} %copy-done.3, f32[1,16,128,128]{2,3,1,0:T(8,128)S(1)} %copy.4, f32[5,18,130,130]{2,3,1,0:T(8,128)S(1)} %select_maximum_fusion.2, f32[5,1,128,128]{2,3,1,0:T(8,128)} %copy-done.6, f32[5,1,128,128]{2,3,1,0:T(8,128)} %copy-done.7, f32[16,128,128]{1,2,0:T(8,128)S(1)} %copy.5), kind=kLoop, calls=%fused_computation.26 | loop fusion | flops 22282240 | bytes 33161216 | tf_op jit(solution)/shard_map/mul | solution.py:98
  34.0 2.3 %copy-done = f32[5,16,128,128]{2,3,1,0:T(8,128)} copy-done((f32[5,16,128,128]{2,3,1,0:T(8,128)}, f32[5,16,128,128]{2,3,1,0:T(8,128)S(1)}, u32[]{:S(2)}) %copy-start) | copy-done | bytes 5242904
  36.3 2.0 %bitcast_add_fusion = (f32[16,128,128]{1,2,0:T(8,128)}, f32[1,16,128,128]{2,3,1,0:T(8,128)}) fusion(f32[1,16,128,128]{2,3,1,0:T(8,128)S(1)} %copy.4, f32[5,16,128,128]{2,3,1,0:T(8,128)S(1)} %fusion.11), kind=kLoop, calls=%fused_computation.67 | loop fusion | flops 2883584 | bytes 8388608 | tf_op jit(solution)/shard_map/add | solution.py:110
  38.3 3.3 %collective-permute-start.2 = (f32[16,128,128]{1,2,0:T(8,128)}, f32[16,128,128]{1,2,0:T(8,128)S(1)}, u32[]{:S(2)}, u32[]{:S(2)}) collective-permute-start(f32[16,128,128]{1,2,0:T(8,128)} %get-tuple-element.4), channel_id=1, source_target_pairs={{0,8},{8,16},{16,24},{1,9},{9,17},{17,25},{2,10},{10,18},{18,26},{... | collective-permute-start | bytes 3145736 | tf_op jit(solution)/shard_map/ppermute | solution.py:36
  41.7 23.7 %collective-permute-done.2 = f32[16,128,128]{1,2,0:T(8,128)S(1)} collective-permute-done((f32[16,128,128]{1,2,0:T(8,128)}, f32[16,128,128]{1,2,0:T(8,128)S(1)}, u32[]{:S(2)}, u32[]{:S(2)}) %collective-permute-start.2) | collective-permute-done | bytes 1048608 | tf_op jit(solution)/shard_map/ppermute | solution.py:36
  66.4 1.8 %fusion.41 = f32[16,64,64]{2,1,0:T(8,128)S(1)} fusion(f32[16,64,128]{1,2,0:T(8,128)S(1)} %convolution_bitcast_fusion.1, f32[128]{0:T(128)S(1)} %add_multiply_fusion.1, pred[64]{0:T(512)(128)(4,1)S(1)} %iota_compare_fusion.4), kind=kOutput, calls=%fused_computation.86 | convolution fusion | flops 100704256 | bytes 787008 | tf_op jit(solution)/shard_map/xkz,lz->xkl/dot_general | solution.py:79
  69.0 1.9 %bitcast_dynamic-update-slice_fusion = (f32[5,16,128,128]{2,3,1,0:T(8,128)S(1)}, f32[16,128,128]{1,2,0:T(8,128)S(1)}) fusion(f32[16,64,128]{2,1,0:T(8,128)S(1)} %fusion.39, f32[128]{0:T(128)S(1)} %add_multiply_fusion.1, pred[64]{0:T(512)(128)(4,1)S(1)} %iota_compare_fusion.4, f32[]{:T(128)S(6)} %convert_element_type.6, f32[1,16,128,128]{2,3,1,0:T(8,128)S(1)} %copy.4), kind=kOutput, calls=%fused_computation.66 | convolution fusion | flops 201891840 | bytes 3670596 | tf_op jit(solution)/shard_map/ky,xkz->xyz/dot_general | solution.py:89
  73.6 1.9 %collective-permute-start.4 = (f32[5,1,128,128]{2,3,1,0:T(8,128)S(1)}, f32[5,1,128,128]{2,3,1,0:T(8,128)S(1)}, u32[]{:S(2)}, u32[]{:S(2)}) collective-permute-start(f32[5,1,128,128]{2,3,1,0:T(8,128)S(1)} %get-tuple-element.6), channel_id=1, source_target_pairs={{0,1},{1,2},{2,3},{3,4},{4,5},{5,6},{6,7},{8,9},{9,10},{10,11},{11... | collective-permute-start | bytes 983048 | tf_op jit(solution)/shard_map/ppermute | solution.py:24
  75.5 2.6 %collective-permute-start.3 = (f32[5,1,128,128]{2,3,1,0:T(8,128)S(1)}, f32[5,1,128,128]{2,3,1,0:T(8,128)S(1)}, u32[]{:S(2)}, u32[]{:S(2)}) collective-permute-start(f32[5,1,128,128]{2,3,1,0:T(8,128)S(1)} %get-tuple-element.7), channel_id=1, source_target_pairs={{1,0},{2,1},{3,2},{4,3},{5,4},{6,5},{7,6},{9,8},{10,9},{11,10},{12... | collective-permute-start | bytes 983048 | tf_op jit(solution)/shard_map/ppermute | solution.py:26
  79.5 4.4 %collective-permute-done.3 = f32[5,1,128,128]{2,3,1,0:T(8,128)S(1)} collective-permute-done((f32[5,1,128,128]{2,3,1,0:T(8,128)S(1)}, f32[5,1,128,128]{2,3,1,0:T(8,128)S(1)}, u32[]{:S(2)}, u32[]{:S(2)}) %collective-permute-start.3) | collective-permute-done | bytes 327712 | tf_op jit(solution)/shard_map/ppermute | solution.py:26
  83.9 9.3 %select_maximum_fusion = f32[5,18,130,130]{2,3,1,0:T(8,128)} fusion(f32[5,1,128,128]{2,3,1,0:T(8,128)S(1)} %collective-permute-done.3, f32[5,16,128,128]{2,3,1,0:T(8,128)S(1)} %add_dynamic-update-slice_fusion, f32[5,1,128,128]{2,3,1,0:T(8,128)S(1)} %collective-permute-done.4), kind=kLoop, calls=%fused_computation.4 | loop fusion | flops 22815000 | bytes 11982240 | tf_op jit(solution)/shard_map/concatenate | solution.py:22
  93.2 21.4 %fusion.8 = f32[5,16,128,128]{2,3,1,0:T(8,128)} fusion(f32[5,16,128,128]{2,3,1,0:T(8,128)} %copy-done.4, f32[5,18,130,130]{2,3,1,0:T(8,128)} %select_maximum_fusion, f32[5,1,128,128]{2,3,1,0:T(8,128)S(1)} %collective-permute-done.4, f32[5,1,128,128]{2,3,1,0:T(8,128)S(1)} %collective-permute-done.3, f32[16,128,128]{1,2,0:T(8,128)S(1)} %copy.5), kind=kLoop, calls=%fused_computation.23 | loop fusion | flops 18350080 | bytes 33161216 | tf_op jit(solution)/shard_map/mul | solution.py:98
  114.6 3.1 %fusion.24 = f32[16,128,128]{1,2,0:T(8,128)S(1)} fusion(f32[16,128,128]{1,2,0:T(8,128)S(1)} %get-tuple-element.11, f32[5,16,128,128]{2,3,1,0:T(8,128)} %fusion.8), kind=kLoop, calls=%fused_computation.58 | loop fusion | flops 2883584 | bytes 7340032 | tf_op jit(solution)/shard_map/add | solution.py:110
  117.7 2.5 %collective-permute-start.5 = (f32[16,128,128]{1,2,0:T(8,128)S(1)}, f32[16,128,128]{1,2,0:T(8,128)S(1)}, u32[]{:S(2)}, u32[]{:S(2)}) collective-permute-start(f32[16,128,128]{1,2,0:T(8,128)S(1)} %fusion.24), channel_id=1, source_target_pairs={{0,8},{8,16},{16,24},{1,9},{9,17},{17,25},{2,10},{10,18},{18,26},{... | collective-permute-start | bytes 3145736 | tf_op jit(solution)/shard_map/ppermute | solution.py:36
  121.5 24.1 %collective-permute-done.5 = f32[16,128,128]{1,2,0:T(8,128)S(1)} collective-permute-done((f32[16,128,128]{1,2,0:T(8,128)S(1)}, f32[16,128,128]{1,2,0:T(8,128)S(1)}, u32[]{:S(2)}, u32[]{:S(2)}) %collective-permute-start.5) | collective-permute-done | bytes 1048608 | tf_op jit(solution)/shard_map/ppermute | solution.py:36
  146.7 1.8 %fusion.35 = f32[16,64,64]{2,1,0:T(8,128)S(1)} fusion(f32[16,64,128]{1,2,0:T(8,128)S(1)} %convolution_bitcast_fusion, f32[128]{0:T(128)S(1)} %add_multiply_fusion.1, pred[64]{0:T(512)(128)(4,1)S(1)} %iota_compare_fusion.4), kind=kOutput, calls=%fused_computation.80 | convolution fusion | flops 100704256 | bytes 787008 | tf_op jit(solution)/shard_map/xkz,lz->xkl/dot_general | solution.py:79
  149.2 1.8 %fusion.18 = f32[1,16,128,128]{2,3,1,0:T(8,128)S(1)} fusion(f32[16,128,128]{1,2,0:T(8,128)S(1)} %get-tuple-element.11, f32[16,64,128]{2,1,0:T(8,128)S(1)} %fusion.33, f32[]{:T(128)S(6)} %convert_element_type.6, f32[128]{0:T(128)S(1)} %add_multiply_fusion.1, pred[64]{0:T(512)(128)(4,1)S(1)} %iota_compare_fusion.4), kind=kOutput, calls=%fused_computation.50 | convolution fusion | flops 201891840 | bytes 2622020 | tf_op jit(solution)/shard_map/ky,xkz->xyz/dot_general | solution.py:89
  (31 shorter events, 12.1 us)
Async XLA Ops:
  2.7 2.0 %copy-start.2 = (f32[4,16,128,128]{2,3,1,0:T(8,128)}, f32[4,16,128,128]{2,3,1,0:T(8,128)S(1)}, u32[]{:S(2)}) copy-start(f32[4,16,128,128]{2,3,1,0:T(8,128)S(1)} %broadcast_in_dim.72) | copy-start | bytes 12582916
  4.7 7.8 %collective-permute-start.1 = (f32[5,1,128,128]{2,3,1,0:T(8,128)S(1)}, f32[5,1,128,128]{2,3,1,0:T(8,128)S(1)}, u32[]{:S(2)}, u32[]{:S(2)}) collective-permute-start(f32[5,1,128,128]{2,3,1,0:T(8,128)S(1)} %get-tuple-element.8), channel_id=1, source_target_pairs={{0,1},{1,2},{2,3},{3,4},{4,5},{5,6},{6,7},{8,9},{9,10},{10,11},{11... | collective-permute-start | bytes 983048 | tf_op jit(solution)/shard_map/ppermute | solution.py:24
  8.5 8.4 %collective-permute-start = (f32[5,1,128,128]{2,3,1,0:T(8,128)S(1)}, f32[5,1,128,128]{2,3,1,0:T(8,128)S(1)}, u32[]{:S(2)}, u32[]{:S(2)}) collective-permute-start(f32[5,1,128,128]{2,3,1,0:T(8,128)S(1)} %get-tuple-element.9), channel_id=1, source_target_pairs={{1,0},{2,1},{3,2},{4,3},{5,4},{6,5},{7,6},{9,8},{10,9},{11,10},{12... | collective-permute-start | bytes 983048 | tf_op jit(solution)/shard_map/ppermute | solution.py:26
  12.0 15.2 %copy-start.3 = (f32[4,16,128,128]{2,3,1,0:T(8,128)S(1)}, f32[4,16,128,128]{2,3,1,0:T(8,128)}, u32[]{:S(2)}) copy-start(f32[4,16,128,128]{2,3,1,0:T(8,128)} %copy-done.2) | copy-start | bytes 12582916
  12.5 4.4 %copy-start.6 = (f32[5,1,128,128]{2,3,1,0:T(8,128)}, f32[5,1,128,128]{2,3,1,0:T(8,128)S(1)}, u32[]{:S(2)}) copy-start(f32[5,1,128,128]{2,3,1,0:T(8,128)S(1)} %collective-permute-done.1) | copy-start | bytes 983044
  16.9 0.7 copy-start.7
  34.0 2.3 %copy-start = (f32[5,16,128,128]{2,3,1,0:T(8,128)}, f32[5,16,128,128]{2,3,1,0:T(8,128)S(1)}, u32[]{:S(2)}) copy-start(f32[5,16,128,128]{2,3,1,0:T(8,128)S(1)} %fusion.11) | copy-start | bytes 15728644
  38.3 27.0 %collective-permute-start.2 = (f32[16,128,128]{1,2,0:T(8,128)}, f32[16,128,128]{1,2,0:T(8,128)S(1)}, u32[]{:S(2)}, u32[]{:S(2)}) collective-permute-start(f32[16,128,128]{1,2,0:T(8,128)} %get-tuple-element.4), channel_id=1, source_target_pairs={{0,8},{8,16},{16,24},{1,9},{9,17},{17,25},{2,10},{10,18},{18,26},{... | collective-permute-start | bytes 3145736 | tf_op jit(solution)/shard_map/ppermute | solution.py:36
  41.6 29.2 %copy-start.1 = (f32[5,16,128,128]{2,3,1,0:T(8,128)S(1)}, f32[5,16,128,128]{2,3,1,0:T(8,128)}, u32[]{:S(2)}) copy-start(f32[5,16,128,128]{2,3,1,0:T(8,128)} %copy-done) | copy-start | bytes 15728644
  72.1 1.2 copy-start.5
  73.5 10.4 %copy-start.4 = (f32[5,16,128,128]{2,3,1,0:T(8,128)}, f32[5,16,128,128]{2,3,1,0:T(8,128)S(1)}, u32[]{:S(2)}) copy-start(f32[5,16,128,128]{2,3,1,0:T(8,128)S(1)} %add_dynamic-update-slice_fusion) | copy-start | bytes 15728644
  73.6 5.9 %collective-permute-start.4 = (f32[5,1,128,128]{2,3,1,0:T(8,128)S(1)}, f32[5,1,128,128]{2,3,1,0:T(8,128)S(1)}, u32[]{:S(2)}, u32[]{:S(2)}) collective-permute-start(f32[5,1,128,128]{2,3,1,0:T(8,128)S(1)} %get-tuple-element.6), channel_id=1, source_target_pairs={{0,1},{1,2},{2,3},{3,4},{4,5},{5,6},{6,7},{8,9},{9,10},{10,11},{11... | collective-permute-start | bytes 983048 | tf_op jit(solution)/shard_map/ppermute | solution.py:24
  75.5 8.4 %collective-permute-start.3 = (f32[5,1,128,128]{2,3,1,0:T(8,128)S(1)}, f32[5,1,128,128]{2,3,1,0:T(8,128)S(1)}, u32[]{:S(2)}, u32[]{:S(2)}) collective-permute-start(f32[5,1,128,128]{2,3,1,0:T(8,128)S(1)} %get-tuple-element.7), channel_id=1, source_target_pairs={{1,0},{2,1},{3,2},{4,3},{5,4},{6,5},{7,6},{9,8},{10,9},{11,10},{12... | collective-permute-start | bytes 983048 | tf_op jit(solution)/shard_map/ppermute | solution.py:26
  117.7 27.9 %collective-permute-start.5 = (f32[16,128,128]{1,2,0:T(8,128)S(1)}, f32[16,128,128]{1,2,0:T(8,128)S(1)}, u32[]{:S(2)}, u32[]{:S(2)}) collective-permute-start(f32[16,128,128]{1,2,0:T(8,128)S(1)} %fusion.24), channel_id=1, source_target_pairs={{0,8},{8,16},{16,24},{1,9},{9,17},{17,25},{2,10},{10,18},{18,26},{... | collective-permute-start | bytes 3145736 | tf_op jit(solution)/shard_map/ppermute | solution.py:36
where the time goes:
time: 153 us; the launch traced here: 152 us
  waiting for transfers between devices  58.4 us (38%)
  other arithmetic  54.4 us (36%)
  starting transfers between devices  16 us (10%)
  local copies, waits for them, and re-layouts  11.8 us (8%)
  matrix products  10.9 us (7%)
    ppermute x2, waiting for transfers between devices, shifted(): lax.ppermute(value, axis, [(source, source + steps) for source in range(i...  47.7 us
    mul x2, other arithmetic, evaluate(): return mobility * (laplace + values - values * values * values)  28.2 us
    concatenate x2, other arithmetic, with_halo(): jnp.concatenate([lax.ppermute(tail, axis, [(i, (i + 1) % count) for i in...  18.9 us
    unnamed x20, local copies, waits for them, and re-layouts  11.3 us
    ppermute x2, waiting for transfers between devices, with_halo(): lax.ppermute(head, axis, [((i + 1) % count, i) for i in range(ends)])  8.79 us
    ppermute x2, starting transfers between devices, shifted(): lax.ppermute(value, axis, [(source, source + steps) for source in range(i...  5.77 us
    ppermute x2, starting transfers between devices, with_halo(): lax.ppermute(tail, axis, [(i, (i + 1) % count) for i in range(ends)])  5.69 us
    add x2, other arithmetic, sweep(): updated.append(start_value + time_step * total)  5.12 us
  transfers between devices with their start and end apart: 6, of which 6 were waited for; matrix products, arithmetic and copies ran while one was open for 2% of the time, Pallas kernels for 0%

commit v1 on v0

v1 whole, which is shorter than its diff:
```python
import functools
import math

import jax
import jax.numpy as jnp
import numpy as np
from jax import lax
from jax.experimental import pallas as pl
from jax.experimental.pallas import tpu as pltpu
from jax.sharding import PartitionSpec as P

KY = 64
KZ = 64
time_step = 0.05
F32 = jnp.float32
BF16 = jnp.bfloat16
VMEM_LIMIT = 24 * 2**20


def basis_value(node_times, source, point):
    total = 1.0
    for other in range(5):
        if other != source:
            total = total * (point - node_times[other]) / (node_times[source] - node_times[other])
    return total


def lobatto():
    root = math.sqrt(3.0 / 7.0)
    node_times = [0.0, (1.0 - root) / 2.0, 0.5, (1.0 + root) / 2.0, 1.0]
    gauss_points = [-math.sqrt(0.6), 0.0, math.sqrt(0.6)]
    gauss_weights = [5.0 / 9.0, 8.0 / 9.0, 5.0 / 9.0]
    last_row = []
    for source in range(5):
        integral = 0.0
        for point, weight in zip(gauss_points, gauss_weights):
            integral += 0.5 * weight * basis_value(node_times, source, 0.5 * (1.0 + point))
        last_row.append(integral)
    return node_times, last_row


NODE_TIMES, LAST_ROW = lobatto()
W = [sum(LAST_ROW[j] * NODE_TIMES[j] ** k for j in range(1, 5)) for k in range(4)]


def dct_rows(count, kept):
    freq = np.arange(kept, dtype=np.float64)[:, None]
    place = np.arange(count, dtype=np.float64)[None, :]
    matrix = np.cos(np.pi * (place + 0.5) * freq / count) * np.sqrt(2.0 / count)
    return np.where(freq == 0, matrix * np.sqrt(0.5), matrix)


def halves(matrix):
    high = matrix.astype(jnp.bfloat16)
    low = (matrix - high.astype(np.float64)).astype(jnp.bfloat16)
    return high, low


def tables(ny, nz):
    cy = dct_rows(ny, KY)
    cz = dct_rows(nz, KZ)
    twice = np.zeros((2 * nz, 2 * KZ))
    twice[:nz, :KZ] = cz.T
    twice[nz:, KZ:] = cz.T
    zh, zl = halves(twice)
    fz = np.concatenate([zh, zh, zl], axis=0)
    yh, yl = halves(cy)
    fy = np.concatenate([yh, yh, yl], axis=1)
    by = np.concatenate([yh.T, yh.T, yl.T], axis=1)
    bz = np.concatenate([zh.T, zh.T, zl.T], axis=0)
    return fz, fy, by, bz


def split(x):
    high = x.astype(BF16)
    return high, (x - high.astype(F32)).astype(BF16)


def dot(a, b):
    return jnp.dot(a, b, preferred_element_type=F32)


def neighbours(v):
    ny, nz = v.shape
    rows = lax.broadcasted_iota(jnp.int32, v.shape, 0)
    lanes = lax.broadcasted_iota(jnp.int32, v.shape, 1)
    total = jnp.where(rows == 0, 0.0, pltpu.roll(v, 1, 0))
    total = total + jnp.where(rows == ny - 1, 0.0, pltpu.roll(v, ny - 1, 0))
    total = total + jnp.where(lanes == 0, 0.0, pltpu.roll(v, 1, 1))
    return total + jnp.where(lanes == nz - 1, 0.0, pltpu.roll(v, nz - 1, 1))


def rate(below, v, above, mobility):
    return mobility * (neighbours(v) + (below + above) - v * (5.0 + v * v))


def analyse(pairs, fz_ref, fy_ref):
    rows = []
    for first, second in pairs:
        first_high, first_low = split(first)
        second_high, second_low = split(second)
        rows.append(
            jnp.concatenate([first_high, second_high, first_low, second_low, first_high, second_high], axis=1)
        )
    half = dot(jnp.concatenate(rows, axis=0), fz_ref[...])
    ny = pairs[0][0].shape[0]
    columns = []
    for i in range(len(pairs)):
        high, low = split(half[i * ny : (i + 1) * ny])
        columns.append(jnp.concatenate([high, low, high], axis=0))
    return dot(fy_ref[...], jnp.concatenate(columns, axis=1))


def synthesise(coeffs, by_ref, bz_ref):
    high, low = split(coeffs)
    half = dot(by_ref[...], jnp.concatenate([high, low, high], axis=0))
    width = 2 * KZ
    count = coeffs.shape[1] // width
    rows = []
    for i in range(count):
        high, low = split(half[:, i * width : (i + 1) * width])
        rows.append(jnp.concatenate([high, low, high], axis=1))
    planes = dot(jnp.concatenate(rows, axis=0), bz_ref[...])
    ny = half.shape[0]
    return [planes[i * ny : (i + 1) * ny] for i in range(count)]


def call(kernel, outs, name, flops=10**7, nbytes=10**6, scratch=(), specs=None, out_specs=None, aliases={}):
    def run(*args):
        return pl.pallas_call(
            kernel,
            out_shape=outs,
            in_specs=specs or [pl.BlockSpec(memory_space=pltpu.VMEM)] * len(args),
            out_specs=out_specs or jax.tree.map(lambda _: pl.BlockSpec(memory_space=pltpu.VMEM), outs),
            scratch_shapes=scratch,
            input_output_aliases=aliases,
            compiler_params=pltpu.CompilerParams(vmem_limit_bytes=VMEM_LIMIT),
            cost_estimate=pl.CostEstimate(flops=flops, bytes_accessed=nbytes, transcendentals=0),
            name=name,
        )(*args)

    return run


ANY = pl.BlockSpec(memory_space=pl.ANY)


def is_even():
    return lax.rem(lax.axis_index("gx"), 2) == 0


def pack_kernel(a_ref, mu_ref, even_ref, odd_ref, sems):
    nx = a_ref.shape[0]
    even = is_even()
    tail_a, tail_m = nx - 2, nx - 1
    copies = []
    for i, (out, is_tail) in enumerate([(even_ref, even), (odd_ref, jnp.logical_not(even))]):
        start = jnp.where(is_tail, tail_a, 0)
        plane = jnp.where(is_tail, tail_m, 0)
        copies.append(pltpu.make_async_copy(a_ref.at[pl.ds(start, 2)], out.at[pl.ds(0, 2)], sems.at[2 * i]))
        copies.append(pltpu.make_async_copy(mu_ref.at[pl.ds(plane, 1)], out.at[pl.ds(2, 1)], sems.at[2 * i + 1]))
    for copy in copies:
        copy.start()
    for copy in copies:
        copy.wait()


def inner_kernel(a_ref, mu_ref, fz_ref, fy_ref, g_ref, c_ref):
    nx = a_ref.shape[0]
    pairs = []
    for p in range(1, nx - 1, 2):
        pair = []
        for q in (p, p + 1):
            g = rate(a_ref[q - 1], a_ref[q], a_ref[q + 1], mu_ref[q])
            g_ref[q - 1] = g
            pair.append(a_ref[q] + time_step * g)
        pairs.append(pair)
    c_ref[...] = analyse(pairs, fz_ref, fy_ref)


def own_kernel(a_ref, fz_ref, fy_ref, c_ref):
    nx = a_ref.shape[0]
    c_ref[...] = analyse([(a_ref[p], a_ref[p + 1]) for p in range(1, nx - 1, 2)], fz_ref, fy_ref)


def outer_kernel(a_ref, mu_ref, even_ref, odd_ref, fz_ref, fy_ref, a_out, g_out, c_ref):
    nx = a_ref.shape[0]
    even = is_even()
    place = lax.axis_index("gx")
    count = lax.axis_size("gx")
    keep_low = (place > 0).astype(F32)
    keep_high = (place < count - 1).astype(F32)
    low = [jnp.where(even, odd_ref[i], even_ref[i]) * keep_low for i in range(3)]
    high = [jnp.where(even, even_ref[i], odd_ref[i]) * keep_high for i in range(3)]
    values = [low[0], low[1], a_ref[0], a_ref[1]]
    g_low = [
        rate(values[0], values[1], values[2], low[2]),
        rate(values[1], values[2], values[3], mu_ref[0]),
    ]
    ends = [a_ref[nx - 2], a_ref[nx - 1], high[0], high[1]]
    g_high = [
        rate(ends[0], ends[1], ends[2], mu_ref[nx - 1]),
        rate(ends[1], ends[2], ends[3], high[2]),
    ]
    for i, (v, g) in enumerate(zip(values[1:3] + ends[1:3], g_low + g_high)):
        a_out[i] = v
        g_out[i] = g
    pairs = [
        [v + time_step * g for v, g in zip(values[1:3], g_low)],
        [v + time_step * g for v, g in zip(ends[1:3], g_high)],
    ]
    c_ref[...] = analyse(pairs, fz_ref, fy_ref)


def later_kernel(a_ref, mu_ref, g_ref, ab_ref, gb_ref, fz_ref, fy_ref, acc_ref, c_ref):
    nx = a_ref.shape[0]
    h = time_step

    def plane(p):
        if p in (-1, 0):
            return gb_ref[p + 1]
        if p in (nx - 1, nx):
            return gb_ref[p - nx + 3]
        return g_ref[p - 1]

    c_ref[...] = analyse([(ab_ref[0], ab_ref[1]), (ab_ref[2], ab_ref[3])], fz_ref, fy_ref)
    for p in range(nx):
        g = plane(p)
        a = a_ref[p]
        laplace = neighbours(g) + (plane(p - 1) + plane(p + 1)) - 5.0 * g
        hg = h * g
        cube = hg * (3.0 * W[1] * a * a + hg * (3.0 * W[2] * a + W[3] * hg))
        acc_ref[p] = h * (W[0] * g + mu_ref[p] * (h * W[1] * laplace - cube))


def received(c, own):
    return jnp.where(lax.axis_index("tm") > 0, c - own, 0.0)


def second_inner_kernel(a_ref, mu_ref, acc_ref, c1_ref, own_ref, fz_ref, fy_ref, by_ref, bz_ref, a1_ref, e_ref, c2_ref):
    nx = a_ref.shape[0]
    nz = a_ref.shape[2]
    change = synthesise(received(c1_ref[...], own_ref[...]), by_ref, bz_ref)
    for p in range(1, nx - 1):
        i, k = (p - 1) // 2, (p - 1) % 2
        a1_ref[p - 1] = a_ref[p] + change[i][:, k * nz : (k + 1) * nz]
    pairs = []
    for p in range(2, nx - 2, 2):
        pair = []
        for q in (p, p + 1):
            v = a1_ref[q - 1]
            f = rate(a1_ref[q - 2], v, a1_ref[q], mu_ref[q])
            e = v + time_step * LAST_ROW[0] * f + acc_ref[q]
            e_ref[q - 2] = e
            pair.append(e)
        pairs.append(pair)
    c2_ref[...] = analyse(pairs, fz_ref, fy_ref)


def second_outer_kernel(
    ab_ref, mu_ref, acc_ref, a1_ref, c1_ref, own_ref, fz_ref, fy_ref, by_ref, bz_ref, a1b_ref, e_ref, c2_ref
):
    nx = mu_ref.shape[0]
    nz = mu_ref.shape[2]
    change = synthesise(received(c1_ref[...], own_ref[...]), by_ref, bz_ref)
    outer = [ab_ref[i] + change[i // 2][:, (i % 2) * nz : (i % 2 + 1) * nz] for i in range(4)]
    a1b_ref[0] = outer[1]
    a1b_ref[1] = outer[2]
    pairs = []
    for start, planes in (
        (0, [outer[0], outer[1], a1_ref[0], a1_ref[1]]),
        (nx - 2, [a1_ref[nx - 4], a1_ref[nx - 3], outer[2], outer[3]]),
    ):
        pair = []
        for k in range(2):
            q = start + k
            f = rate(planes[k], planes[k + 1], planes[k + 2], mu_ref[q])
            e = planes[k + 1] + time_step * LAST_ROW[0] * f + acc_ref[q]
            e_ref[2 * (start > 0) + k] = e
            pair.append(e)
        pairs.append(pair)
    c2_ref[...] = analyse(pairs, fz_ref, fy_ref)


def last_kernel(a1_ref, a1b_ref, c1_ref, c1b_ref, c2_ref, c2b_ref, by_ref, bz_ref, out_ref):
    nx = a1_ref.shape[0] + 2
    nz = a1_ref.shape[2]
    k = KZ
    c1 = c1_ref[...]
    c1b = c1b_ref[...]
    inner = received(c2_ref[...], c1[:, k : c1.shape[1] - k])
    ends = jnp.concatenate([c1b[:, k : 2 * k], c1[:, :k], c1[:, c1.shape[1] - k :], c1b[:, 2 * k : 3 * k]], axis=1)
    outer = received(c2b_ref[...], ends)
    change = synthesise(jnp.concatenate([inner, outer], axis=1), by_ref, bz_ref)
    for p in range(2, nx - 2):
        i, j = (p - 2) // 2, p % 2
        out_ref[0, p] = a1_ref[p - 1] + change[i][:, j * nz : (j + 1) * nz]
    last = (nx - 4) // 2
    out_ref[0, 0] = a1b_ref[0] + change[last][:, :nz]
    out_ref[0, 1] = a1_ref[0] + change[last][:, nz:]
    out_ref[0, nx - 2] = a1_ref[nx - 3] + change[last + 1][:, :nz]
    out_ref[0, nx - 1] = a1b_ref[1] + change[last + 1][:, nz:]


def join_kernel(inner_ref, outer_ref, out_ref, sems):
    nx = out_ref.shape[1]
    copies = [
        pltpu.make_async_copy(outer_ref.at[pl.ds(0, 2)], out_ref.at[0, pl.ds(0, 2)], sems.at[0]),
        pltpu.make_async_copy(outer_ref.at[pl.ds(2, 2)], out_ref.at[0, pl.ds(nx - 2, 2)], sems.at[1]),
    ]
    for i in range(2, nx - 2, 4):
        copies.append(
            pltpu.make_async_copy(inner_ref.at[pl.ds(i - 2, 4)], out_ref.at[0, pl.ds(i, 4)], sems.at[1 + i // 4 + 1])
        )
    for copy in copies:
        copy.start()
    for copy in copies:
        copy.wait()


def body(start_states, mobility):
    a = start_states[0]
    nx, ny, nz = a.shape
    slices, slabs = lax.axis_size("tm"), lax.axis_size("gx")
    fz, fy, by, bz = [jnp.asarray(t) for t in tables(ny, nz)]
    plane = functools.partial(jax.ShapeDtypeStruct, dtype=F32)
    inner = (nx - 2) // 2

    even_pairs = [(s * slabs + g, s * slabs + (g ^ 1)) for s in range(slices) for g in range(slabs)]
    odd_pairs = []
    for s in range(slices):
        for g in range(slabs):
            other = g + 1 if g % 2 else g - 1
            if 0 <= other < slabs:
                odd_pairs.append((s * slabs + g, s * slabs + other))
            else:
                odd_pairs.append((s * slabs + g, (s ^ 1) * slabs + g))
    ring = [(s, (s + 1) % slices) for s in range(slices)]

    to_even, to_odd = call(
        pack_kernel,
        [plane((3, ny, nz)), plane((3, ny, nz))],
        "pack",
        scratch=[pltpu.SemaphoreType.DMA((4,))],
        specs=[ANY, ANY],
        out_specs=[ANY, ANY],
    )(a, mobility)
    from_even = lax.ppermute(to_even, ("tm", "gx"), even_pairs)
    from_odd = lax.ppermute(to_odd, ("tm", "gx"), odd_pairs)
    g, c1 = call(inner_kernel, [plane((nx - 2, ny, nz)), plane((KY, inner * 2 * KZ))], "inner")(a, mobility, fz, fy)
    c1_in = lax.ppermute(c1, "tm", ring)
    own = call(own_kernel, plane((KY, inner * 2 * KZ)), "own")(a, fz, fy)
    ab, gb, c1b = call(
        outer_kernel, [plane((4, ny, nz)), plane((4, ny, nz)), plane((KY, 4 * KZ))], "outer"
    )(a, mobility, from_even, from_odd, fz, fy)
    c1b_in = lax.ppermute(c1b, "tm", ring)
    acc, own_b = call(later_kernel, [plane((nx, ny, nz)), plane((KY, 4 * KZ))], "later")(
        a, mobility, g, ab, gb, fz, fy
    )
    a1, e2, c2 = call(
        second_inner_kernel,
        [plane((nx - 2, ny, nz)), plane((nx - 4, ny, nz)), plane((KY, (inner - 1) * 2 * KZ))],
        "second_inner",
    )(a, mobility, acc, c1_in, own, fz, fy, by, bz)
    c2_in = lax.ppermute(c2, "tm", ring)
    a1b, e2b, c2b = call(
        second_outer_kernel,
        [plane((2, ny, nz)), plane((4, ny, nz)), plane((KY, 4 * KZ))],
        "second_outer",
    )(ab, mobility, acc, a1, c1b_in, own_b, fz, fy, by, bz)
    c2b_in = lax.ppermute(c2b, "tm", ring)
    end_state = call(
        join_kernel,
        plane((1, nx, ny, nz)),
        "join",
        scratch=[pltpu.SemaphoreType.DMA((2 + (nx - 4) // 4,))],
        specs=[ANY, ANY],
        out_specs=ANY,
    )(e2, e2b)
    next_start = call(last_kernel, plane((1, nx, ny, nz)), "last")(a1, a1b, c1_in, c1b_in, c2_in, c2b_in, by, bz)
    return end_state, next_start


def solution(mesh):
    placed = (P("tm", "gx", None, None), P("gx", None, None))
    return jax.shard_map(
        body,
        mesh=mesh,
        in_specs=placed,
        out_specs=(P("tm", "gx", None, None), P("tm", "gx", None, None)),
        check_vma=False,
    )
```

time: 153 us -> 36.7 us (0.24)
  the two profiles are of different devices: /device:TPU:21 before, /device:TPU:0 now
where the time goes in v1:
time: 36.7 us; the launch traced here: 36.4 us
  waiting for transfers between devices  15.6 us (43%)
  Pallas kernels  9.29 us (25%)
  starting transfers between devices  6.51 us (18%)
  local copies, waits for them, and re-layouts  4.2 us (11%)
  between operations  0.79 us (2%)
    pallas_call x9, Pallas kernels, run(): pl.pallas_call(kernel, out_shape=outs, in_specs=specs or [pl.BlockSpec(me...  9.29 us
    ppermute x1, waiting for transfers between devices, body(): from_odd = lax.ppermute(to_odd, ('tm', 'gx'), odd_pairs)  5.96 us
    ppermute x1, waiting for transfers between devices, body(): c1b_in = lax.ppermute(c1b, 'tm', ring)  5.49 us
    unnamed x18, local copies, waits for them, and re-layouts  4.2 us
    ppermute x1, waiting for transfers between devices, body(): c2b_in = lax.ppermute(c2b, 'tm', ring)  4.14 us
    ppermute x1, starting transfers between devices, body(): c1_in = lax.ppermute(c1, 'tm', ring)  2.99 us
    ppermute x1, starting transfers between devices, body(): from_odd = lax.ppermute(to_odd, ('tm', 'gx'), odd_pairs)  1.56 us
    ppermute x1, starting transfers between devices, body(): c1b_in = lax.ppermute(c1b, 'tm', ring)  1.24 us
  transfers between devices with their start and end apart: 6, of which 3 were waited for; matrix products, arithmetic and copies ran while one was open for 0% of the time, Pallas kernels for 13%

profile of v1, /device:TPU:0, one launch (start us, length us, event | category | flops | bytes accessed | tf_op | source)
XLA Modules:
  0.0 36.4 jit_solution(15614537674164143118)
XLA Ops:
  0.6 1.2 %copy-done = f32[1,16,128,128]{3,2,1,0:T(8,128)S(1)} copy-done((f32[1,16,128,128]{3,2,1,0:T(8,128)S(1)}, f32[1,16,128,128]{3,2,1,0:T(8,128)}, u32[]{:S(2)}) %copy-start) | copy-done | bytes 1048600
  1.9 1.2 %copy-done.1 = f32[16,128,128]{2,1,0:T(8,128)S(1)} copy-done((f32[16,128,128]{2,1,0:T(8,128)S(1)}, f32[16,128,128]{2,1,0:T(8,128)}, u32[]{:S(2)}) %copy-start.1) | copy-done | bytes 1048600
  3.1 0.9 %copy-done.3 = bf16[768,128]{1,0:T(8,128)(2,1)S(1)} copy-done((bf16[768,128]{1,0:T(8,128)(2,1)S(1)}, bf16[768,128]{1,0:T(8,128)(2,1)}, u32[]{:S(2)}) %copy-start.3) | copy-done | bytes 196632
  4.0 0.8 %copy-done.6 = bf16[64,384]{1,0:T(8,128)(2,1)S(1)} copy-done((bf16[64,384]{1,0:T(8,128)(2,1)S(1)}, bf16[64,384]{1,0:T(8,128)(2,1)}, u32[]{:S(2)}) %copy-start.6) | copy-done | bytes 49176
  4.8 1.1 %inner.1 = (f32[14,128,128]{2,1,0:T(8,128)S(1)}, f32[64,896]{1,0:T(8,128)S(1)}) custom-call(f32[16,128,128]{2,1,0:T(8,128)S(1)} %bitcast.1, f32[16,128,128]{2,1,0:T(8,128)S(1)} %copy-done.1, bf16[768,128]{1,0:T(8,128)(2,1)S(1)} %copy-done.3, bf16[64,384]{1,0:T(8,128)(2,1)S(1)} %copy-done.6), custom_call_target="tpu_custom_call" | custom-call | flops 10000000 | bytes 1000000 | tf_op jit(solution)/shard_map/inner/pallas_call | solution.py:130
  5.9 0.0 copy-start.4
  5.9 0.0 copy-start.7
  5.9 3.0 %collective-permute-start.2 = (f32[64,896]{1,0:T(8,128)S(1)}, f32[64,896]{1,0:T(8,128)S(1)}, u32[]{:S(2)}, u32[]{:S(2)}) collective-permute-start(f32[64,896]{1,0:T(8,128)S(1)} %get-tuple-element.23), channel_id=1, source_target_pairs={{0,8},{8,16},{16,24},{24,0},{1,9},{9,17},{17,25},{25,1},{2,10},{10... | collective-permute-start | bytes 688136 | tf_op jit(solution)/shard_map/ppermute | solution.py:351
  8.9 0.5 %pack.1 = (f32[3,128,128]{2,1,0:T(8,128)S(1)}, f32[3,128,128]{2,1,0:T(8,128)S(1)}) custom-call(f32[16,128,128]{2,1,0:T(8,128)S(1)} %bitcast.2, f32[16,128,128]{2,1,0:T(8,128)S(1)} %copy-done.1), custom_call_target="tpu_custom_call" | custom-call | flops 10000000 | bytes 1000000 | tf_op jit(solution)/shard_map/pack/pallas_call | solution.py:130
  9.5 0.1 collective-permute-start
  9.6 1.6 %collective-permute-start.1 = (f32[3,128,128]{2,1,0:T(8,128)S(1)}, f32[3,128,128]{2,1,0:T(8,128)S(1)}, u32[]{:S(2)}, u32[]{:S(2)}) collective-permute-start(f32[3,128,128]{2,1,0:T(8,128)S(1)} %get-tuple-element.19), channel_id=1, source_target_pairs={{0,8},{1,2},{2,1},{3,4},{4,3},{5,6},{6,5},{7,15},{8,0},{9,10},{10,... | collective-permute-start | bytes 589832 | tf_op jit(solution)/shard_map/ppermute | solution.py:349
  11.1 0.8 %own.1.own_ref = f32[64,896]{1,0:T(8,128)S(1)} custom-call(f32[16,128,128]{2,1,0:T(8,128)S(1)} %bitcast.3, bf16[768,128]{1,0:T(8,128)(2,1)S(1)} %copy-done.4, bf16[64,384]{1,0:T(8,128)(2,1)S(1)} %copy-done.7), custom_call_target="tpu_custom_call" | custom-call | flops 10000000 | bytes 1000000 | tf_op jit(solution)/shard_map/own/pallas_call | solution.py:130
  11.9 6.0 %collective-permute-done.1.odd_ref = f32[3,128,128]{2,1,0:T(8,128)S(1)} collective-permute-done((f32[3,128,128]{2,1,0:T(8,128)S(1)}, f32[3,128,128]{2,1,0:T(8,128)S(1)}, u32[]{:S(2)}, u32[]{:S(2)}) %collective-permute-start.1) | collective-permute-done | bytes 196640 | tf_op jit(solution)/shard_map/ppermute | solution.py:349
  17.9 0.6 %outer.1 = (f32[4,128,128]{2,1,0:T(8,128)S(1)}, f32[4,128,128]{2,1,0:T(8,128)S(1)}, f32[64,256]{1,0:T(8,128)S(1)}) custom-call(f32[16,128,128]{2,1,0:T(8,128)S(1)} %bitcast.4, f32[16,128,128]{2,1,0:T(8,128)S(1)} %copy-done.2, f32[3,128,128]{2,1,0:T(8,128)S(1)} %collective-permute-done.even_ref, f32[3,128,128]{2,1,0:T(8,128)S(1)} %collective-permute-done.1.odd_ref, ...), custom_call_target="tpu_custom_call" | custom-call | flops 10000000 | bytes 1000000 | tf_op jit(solution)/shard_map/outer/pallas_call | solution.py:130
  18.5 1.0 %later.1 = (f32[16,128,128]{2,1,0:T(8,128)S(1)}, f32[64,256]{1,0:T(8,128)S(1)}) custom-call(f32[16,128,128]{2,1,0:T(8,128)S(1)} %bitcast.5, f32[16,128,128]{2,1,0:T(8,128)S(1)} %copy-done.2, f32[14,128,128]{2,1,0:T(8,128)S(1)} %get-tuple-element.17.g_ref, f32[4,128,128]{2,1,0:T(8,128)S(1)} %get-tuple-element.20.ab_ref, ...), custom_call_target="tpu_custom_call" | custom-call | flops 10000000 | bytes 1000000 | tf_op jit(solution)/shard_map/later/pallas_call | solution.py:130
  19.5 1.8 %second_inner.1 = (f32[14,128,128]{2,1,0:T(8,128)S(1)}, f32[12,128,128]{2,1,0:T(8,128)S(1)}, f32[64,768]{1,0:T(8,128)S(1)}) custom-call(f32[16,128,128]{2,1,0:T(8,128)S(1)} %bitcast.6, f32[16,128,128]{2,1,0:T(8,128)S(1)} %copy-done.2, f32[16,128,128]{2,1,0:T(8,128)S(1)} %get-tuple-element.22.acc_ref, f32[64,896]{1,0:T(8,128)S(1)} %collective-permute-done.2.c1_ref, ...), custom_call_target="tpu_custom_call" | custom-call | flops 10000000 | bytes 1000000 | tf_op jit(solution)/shard_map/second_inner/pallas_call | solution.py:130
  21.4 0.6 %collective-permute-start.4 = (f32[64,768]{1,0:T(8,128)S(1)}, f32[64,768]{1,0:T(8,128)S(1)}, u32[]{:S(2)}, u32[]{:S(2)}) collective-permute-start(f32[64,768]{1,0:T(8,128)S(1)} %get-tuple-element.30), channel_id=1, source_target_pairs={{0,8},{8,16},{16,24},{24,0},{1,9},{9,17},{17,25},{25,1},{2,10},{10... | collective-permute-start | bytes 589832 | tf_op jit(solution)/shard_map/ppermute | solution.py:365
  21.9 1.2 %collective-permute-start.3 = (f32[64,256]{1,0:T(8,128)S(1)}, f32[64,256]{1,0:T(8,128)S(1)}, u32[]{:S(2)}, u32[]{:S(2)}) collective-permute-start(f32[64,256]{1,0:T(8,128)S(1)} %get-tuple-element.26), channel_id=1, source_target_pairs={{0,8},{8,16},{16,24},{24,0},{1,9},{9,17},{17,25},{25,1},{2,10},{10... | collective-permute-start | bytes 196616 | tf_op jit(solution)/shard_map/ppermute | solution.py:356
  23.2 5.5 %collective-permute-done.3.c1_ref.c1b_ref = f32[64,256]{1,0:T(8,128)S(1)} collective-permute-done((f32[64,256]{1,0:T(8,128)S(1)}, f32[64,256]{1,0:T(8,128)S(1)}, u32[]{:S(2)}, u32[]{:S(2)}) %collective-permute-start.3) | collective-permute-done | bytes 65568 | tf_op jit(solution)/shard_map/ppermute | solution.py:356
  28.7 0.9 %second_outer.1 = (f32[2,128,128]{2,1,0:T(8,128)S(1)}, f32[4,128,128]{2,1,0:T(8,128)S(1)}, f32[64,256]{1,0:T(8,128)S(1)}) custom-call(f32[4,128,128]{2,1,0:T(8,128)S(1)} %get-tuple-element.20.ab_ref, f32[16,128,128]{2,1,0:T(8,128)S(1)} %copy-done.2, f32[16,128,128]{2,1,0:T(8,128)S(1)} %get-tuple-element.22.acc_ref, ...), custom_call_target="tpu_custom_call" | custom-call | flops 10000000 | bytes 1000000 | tf_op jit(solution)/shard_map/second_outer/pallas_call | solution.py:130
  29.6 0.1 collective-permute-start.5
  29.6 1.0 %join.1 = f32[1,16,128,128]{3,2,1,0:T(8,128)} custom-call(f32[12,128,128]{2,1,0:T(8,128)S(1)} %get-tuple-element.24.inner_ref, f32[4,128,128]{2,1,0:T(8,128)S(1)} %get-tuple-element.28.outer_ref), custom_call_target="tpu_custom_call" | custom-call | flops 10000000 | bytes 1000000 | tf_op jit(solution)/shard_map/join/pallas_call | solution.py:130
  30.6 4.1 %collective-permute-done.5.c2b_ref = f32[64,256]{1,0:T(8,128)S(1)} collective-permute-done((f32[64,256]{1,0:T(8,128)S(1)}, f32[64,256]{1,0:T(8,128)S(1)}, u32[]{:S(2)}, u32[]{:S(2)}) %collective-permute-start.5) | collective-permute-done | bytes 65568 | tf_op jit(solution)/shard_map/ppermute | solution.py:371
  34.8 1.6 %last.1 = f32[1,16,128,128]{3,2,1,0:T(8,128)} custom-call(f32[14,128,128]{2,1,0:T(8,128)S(1)} %get-tuple-element.25.a1_ref, f32[2,128,128]{2,1,0:T(8,128)S(1)} %get-tuple-element.29.a1b_ref, f32[64,896]{1,0:T(8,128)S(1)} %collective-permute-done.2.c1_ref, f32[64,256]{1,0:T(8,128)S(1)} %collective-permute-done.3.c1_ref.c1b_ref, ...), custom_call_target="tpu_custom_call" | custom-call | flops 10000000 | bytes 1000000 | tf_op jit(solution)/shard_map/last/pallas_call | solution.py:130
  (15 shorter events, 0.0 us)
Async XLA Ops:
  0.6 1.2 %copy-start = (f32[1,16,128,128]{3,2,1,0:T(8,128)S(1)}, f32[1,16,128,128]{3,2,1,0:T(8,128)}, u32[]{:S(2)}) copy-start(f32[1,16,128,128]{3,2,1,0:T(8,128)} %param.6) | copy-start | bytes 3145732
  1.9 1.2 %copy-start.1 = (f32[16,128,128]{2,1,0:T(8,128)S(1)}, f32[16,128,128]{2,1,0:T(8,128)}, u32[]{:S(2)}) copy-start(f32[16,128,128]{2,1,0:T(8,128)} %mu_ref.11) | copy-start | bytes 3145732
  3.1 0.9 %copy-start.3 = (bf16[768,128]{1,0:T(8,128)(2,1)S(1)}, bf16[768,128]{1,0:T(8,128)(2,1)}, u32[]{:S(2)}) copy-start(bf16[768,128]{1,0:T(8,128)(2,1)} %constant.8.clone.fz_ref) | copy-start | bytes 589828
  4.0 0.8 %copy-start.6 = (bf16[64,384]{1,0:T(8,128)(2,1)S(1)}, bf16[64,384]{1,0:T(8,128)(2,1)}, u32[]{:S(2)}) copy-start(bf16[64,384]{1,0:T(8,128)(2,1)} %constant.9.clone.fy_ref) | copy-start | bytes 147460
  5.9 5.2 %copy-start.4 = (bf16[768,128]{1,0:T(8,128)(2,1)S(1)}, bf16[768,128]{1,0:T(8,128)(2,1)}, u32[]{:S(2)}) copy-start(bf16[768,128]{1,0:T(8,128)(2,1)} %constant.8.clone.fz_ref) | copy-start | bytes 589828
  5.9 5.2 %copy-start.7 = (bf16[64,384]{1,0:T(8,128)(2,1)S(1)}, bf16[64,384]{1,0:T(8,128)(2,1)}, u32[]{:S(2)}) copy-start(bf16[64,384]{1,0:T(8,128)(2,1)} %constant.9.clone.fy_ref) | copy-start | bytes 147460
  5.9 13.6 %collective-permute-start.2 = (f32[64,896]{1,0:T(8,128)S(1)}, f32[64,896]{1,0:T(8,128)S(1)}, u32[]{:S(2)}, u32[]{:S(2)}) collective-permute-start(f32[64,896]{1,0:T(8,128)S(1)} %get-tuple-element.23), channel_id=1, source_target_pairs={{0,8},{8,16},{16,24},{24,0},{1,9},{9,17},{17,25},{25,1},{2,10},{10... | collective-permute-start | bytes 688136 | tf_op jit(solution)/shard_map/ppermute | solution.py:351
  9.5 8.4 %copy-start.2 = (f32[16,128,128]{2,1,0:T(8,128)S(1)}, f32[16,128,128]{2,1,0:T(8,128)}, u32[]{:S(2)}) copy-start(f32[16,128,128]{2,1,0:T(8,128)} %mu_ref.11) | copy-start | bytes 3145732
  9.5 2.4 %collective-permute-start = (f32[3,128,128]{2,1,0:T(8,128)S(1)}, f32[3,128,128]{2,1,0:T(8,128)S(1)}, u32[]{:S(2)}, u32[]{:S(2)}) collective-permute-start(f32[3,128,128]{2,1,0:T(8,128)S(1)} %get-tuple-element.18), channel_id=1, source_target_pairs={{0,1},{1,0},{2,3},{3,2},{4,5},{5,4},{6,7},{7,6},{8,9},{9,8},{10,11... | collective-permute-start | bytes 589832 | tf_op jit(solution)/shard_map/ppermute | solution.py:348
  9.6 8.3 %collective-permute-start.1 = (f32[3,128,128]{2,1,0:T(8,128)S(1)}, f32[3,128,128]{2,1,0:T(8,128)S(1)}, u32[]{:S(2)}, u32[]{:S(2)}) collective-permute-start(f32[3,128,128]{2,1,0:T(8,128)S(1)} %get-tuple-element.19), channel_id=1, source_target_pairs={{0,8},{1,2},{2,1},{3,4},{4,3},{5,6},{6,5},{7,15},{8,0},{9,10},{10,... | collective-permute-start | bytes 589832 | tf_op jit(solution)/shard_map/ppermute | solution.py:349
  18.5 1.1 %copy-start.5 = (bf16[384,256]{1,0:T(8,128)(2,1)S(1)}, bf16[384,256]{1,0:T(8,128)(2,1)}, u32[]{:S(2)}) copy-start(bf16[384,256]{1,0:T(8,128)(2,1)} %constant.11.clone.bz_ref) | copy-start | bytes 589828
  18.5 1.1 %copy-start.8 = (bf16[128,192]{1,0:T(8,128)(2,1)S(1)}, bf16[128,192]{1,0:T(8,128)(2,1)}, u32[]{:S(2)}) copy-start(bf16[128,192]{1,0:T(8,128)(2,1)} %constant.10.clone.by_ref) | copy-start | bytes 147460
  21.4 13.4 %collective-permute-start.4 = (f32[64,768]{1,0:T(8,128)S(1)}, f32[64,768]{1,0:T(8,128)S(1)}, u32[]{:S(2)}, u32[]{:S(2)}) collective-permute-start(f32[64,768]{1,0:T(8,128)S(1)} %get-tuple-element.30), channel_id=1, source_target_pairs={{0,8},{8,16},{16,24},{24,0},{1,9},{9,17},{17,25},{25,1},{2,10},{10... | collective-permute-start | bytes 589832 | tf_op jit(solution)/shard_map/ppermute | solution.py:365
  21.9 6.7 %collective-permute-start.3 = (f32[64,256]{1,0:T(8,128)S(1)}, f32[64,256]{1,0:T(8,128)S(1)}, u32[]{:S(2)}, u32[]{:S(2)}) collective-permute-start(f32[64,256]{1,0:T(8,128)S(1)} %get-tuple-element.26), channel_id=1, source_target_pairs={{0,8},{8,16},{16,24},{24,0},{1,9},{9,17},{17,25},{25,1},{2,10},{10... | collective-permute-start | bytes 196616 | tf_op jit(solution)/shard_map/ppermute | solution.py:356
  29.6 5.2 %collective-permute-start.5 = (f32[64,256]{1,0:T(8,128)S(1)}, f32[64,256]{1,0:T(8,128)S(1)}, u32[]{:S(2)}, u32[]{:S(2)}) collective-permute-start(f32[64,256]{1,0:T(8,128)S(1)} %get-tuple-element.31), channel_id=1, source_target_pairs={{0,8},{8,16},{16,24},{24,0},{1,9},{9,17},{17,25},{25,1},{2,10},{10... | collective-permute-start | bytes 196616 | tf_op jit(solution)/shard_map/ppermute | solution.py:371

commit v2 on v1

--- a/solution.py
+++ b/solution.py
@@ -165,25 +165,60 @@
         copy.wait()
 
 
+def chunks(nx):
+    last = nx // 2
+    middle = (last + 1) // 2
+    first = [list(range(1, middle + 1)), list(range(middle + 1, last)), [0, last]]
+    second = [list(range(1, middle)), list(range(middle, last - 1)), [0, last - 1]]
+    return first, second
+
+
+def planes_of(pairs, shift):
+    return [2 * t + shift + k for t in pairs for k in (0, 1)]
+
+
+def fetch_kernel(a_in, mu_in, fz_in, fy_in, by_in, bz_in, after, a_ref, mu_ref, fz_ref, fy_ref, by_ref, bz_ref, g_ref, c_ref, sems):
+    nx = a_ref.shape[0]
+    pairs = chunks(nx)[0][0]
+    planes = planes_of(pairs, -1)
+    cut = (planes[-1] + 2 + 3) // 4 * 4
+    early, late = [], []
+    for start in range(0, nx, 4):
+        for source, target in ((a_in, a_ref), (mu_in, mu_ref)):
+            (early if start < cut else late).append((source.at[pl.ds(start, 4)], target.at[pl.ds(start, 4)]))
+    early += [(fz_in, fz_ref), (fy_in, fy_ref)]
+    late += [(by_in, by_ref), (bz_in, bz_ref)]
+    copies = [pltpu.make_async_copy(s, t, sems.at[i]) for i, (s, t) in enumerate(early + late)]
+    for copy in copies:
+        copy.start()
+    for copy in copies[: len(early)]:
+        copy.wait()
+    inner_chunk(a_ref, mu_ref, fz_ref, fy_ref, g_ref, c_ref, pairs)
+    for copy in copies[len(early) :]:
+        copy.wait()
+
+
+def inner_chunk(a_ref, mu_ref, fz_ref, fy_ref, g_ref, c_ref, pairs):
+    ends = []
+    for i, p in enumerate(planes_of(pairs, -1)):
+        g = rate(a_ref[p - 1], a_ref[p], a_ref[p + 1], mu_ref[p])
+        g_ref[i] = g
+        ends.append(a_ref[p] + time_step * g)
+    c_ref[...] = analyse(list(zip(ends[::2], ends[1::2])), fz_ref, fy_ref)
+
+
 def inner_kernel(a_ref, mu_ref, fz_ref, fy_ref, g_ref, c_ref):
-    nx = a_ref.shape[0]
-    pairs = []
-    for p in range(1, nx - 1, 2):
-        pair = []
-        for q in (p, p + 1):
-            g = rate(a_ref[q - 1], a_ref[q], a_ref[q + 1], mu_ref[q])
-            g_ref[q - 1] = g
-            pair.append(a_ref[q] + time_step * g)
-        pairs.append(pair)
-    c_ref[...] = analyse(pairs, fz_ref, fy_ref)
-
-
-def own_kernel(a_ref, fz_ref, fy_ref, c_ref):
-    nx = a_ref.shape[0]
-    c_ref[...] = analyse([(a_ref[p], a_ref[p + 1]) for p in range(1, nx - 1, 2)], fz_ref, fy_ref)
-
-
-def outer_kernel(a_ref, mu_ref, even_ref, odd_ref, fz_ref, fy_ref, a_out, g_out, c_ref):
+    inner_chunk(a_ref, mu_ref, fz_ref, fy_ref, g_ref, c_ref, chunks(a_ref.shape[0])[0][1])
+
+
+def own_kernel(a_ref, fz_ref, fy_ref, after, first_ref, second_ref):
+    first, second, _ = chunks(a_ref.shape[0])[0]
+    coeffs = analyse([(a_ref[p - 1], a_ref[p]) for p in planes_of(first + second, -1)[1::2]], fz_ref, fy_ref)
+    first_ref[...] = coeffs[:, : first_ref.shape[1]]
+    second_ref[...] = coeffs[:, first_ref.shape[1] :]
+
+
+def outer_kernel(a_ref, mu_ref, even_ref, odd_ref, fz_ref, fy_ref, after, a_out, g_out, c_ref):
     nx = a_ref.shape[0]
     even = is_even()
     place = lax.axis_index("gx")
@@ -212,22 +247,28 @@
     c_ref[...] = analyse(pairs, fz_ref, fy_ref)
 
 
-def later_kernel(a_ref, mu_ref, g_ref, ab_ref, gb_ref, fz_ref, fy_ref, acc_ref, c_ref):
+def plane_reader(refs, nx):
+    where = {}
+    for ref, pairs in zip(refs, chunks(nx)[0]):
+        for i, p in enumerate(planes_of(pairs, -1)):
+            where[p] = (ref, i)
+
+    def read(p):
+        ref, i = where[p]
+        return ref[i]
+
+    return read
+
+
+def later_kernel(a_ref, mu_ref, g0_ref, g1_ref, g2_ref, ab_ref, fz_ref, fy_ref, acc_ref, c_ref):
     nx = a_ref.shape[0]
     h = time_step
-
-    def plane(p):
-        if p in (-1, 0):
-            return gb_ref[p + 1]
-        if p in (nx - 1, nx):
-            return gb_ref[p - nx + 3]
-        return g_ref[p - 1]
-
+    rates = plane_reader((g0_ref, g1_ref, g2_ref), nx)
     c_ref[...] = analyse([(ab_ref[0], ab_ref[1]), (ab_ref[2], ab_ref[3])], fz_ref, fy_ref)
     for p in range(nx):
-        g = plane(p)
+        g = rates(p)
         a = a_ref[p]
-        laplace = neighbours(g) + (plane(p - 1) + plane(p + 1)) - 5.0 * g
+        laplace = neighbours(g) + (rates(p - 1) + rates(p + 1)) - 5.0 * g
         hg = h * g
         cube = hg * (3.0 * W[1] * a * a + hg * (3.0 * W[2] * a + W[3] * hg))
         acc_ref[p] = h * (W[0] * g + mu_ref[p] * (h * W[1] * laplace - cube))
@@ -237,81 +278,65 @@
     return jnp.where(lax.axis_index("tm") > 0, c - own, 0.0)
 
 
-def second_inner_kernel(a_ref, mu_ref, acc_ref, c1_ref, own_ref, fz_ref, fy_ref, by_ref, bz_ref, a1_ref, e_ref, c2_ref):
-    nx = a_ref.shape[0]
-    nz = a_ref.shape[2]
+def second_kernel(stage, *refs):
+    a_ref, mu_ref, acc_ref, c1_ref, own_ref, fz_ref, fy_ref, by_ref, bz_ref = refs[:9]
+    earlier, (a1_ref, e_ref, c2_ref) = refs[9:-3], refs[-3:]
+    nx, ny, nz = mu_ref.shape
+    first, second = chunks(nx)
     change = synthesise(received(c1_ref[...], own_ref[...]), by_ref, bz_ref)
-    for p in range(1, nx - 1):
-        i, k = (p - 1) // 2, (p - 1) % 2
-        a1_ref[p - 1] = a_ref[p] + change[i][:, k * nz : (k + 1) * nz]
-    pairs = []
-    for p in range(2, nx - 2, 2):
-        pair = []
-        for q in (p, p + 1):
-            v = a1_ref[q - 1]
-            f = rate(a1_ref[q - 2], v, a1_ref[q], mu_ref[q])
-            e = v + time_step * LAST_ROW[0] * f + acc_ref[q]
-            e_ref[q - 2] = e
-            pair.append(e)
-        pairs.append(pair)
-    c2_ref[...] = analyse(pairs, fz_ref, fy_ref)
-
-
-def second_outer_kernel(
-    ab_ref, mu_ref, acc_ref, a1_ref, c1_ref, own_ref, fz_ref, fy_ref, by_ref, bz_ref, a1b_ref, e_ref, c2_ref
-):
-    nx = mu_ref.shape[0]
-    nz = mu_ref.shape[2]
-    change = synthesise(received(c1_ref[...], own_ref[...]), by_ref, bz_ref)
-    outer = [ab_ref[i] + change[i // 2][:, (i % 2) * nz : (i % 2 + 1) * nz] for i in range(4)]
-    a1b_ref[0] = outer[1]
-    a1b_ref[1] = outer[2]
-    pairs = []
-    for start, planes in (
-        (0, [outer[0], outer[1], a1_ref[0], a1_ref[1]]),
-        (nx - 2, [a1_ref[nx - 4], a1_ref[nx - 3], outer[2], outer[3]]),
-    ):
-        pair = []
-        for k in range(2):
-            q = start + k
-            f = rate(planes[k], planes[k + 1], planes[k + 2], mu_ref[q])
-            e = planes[k + 1] + time_step * LAST_ROW[0] * f + acc_ref[q]
-            e_ref[2 * (start > 0) + k] = e
-            pair.append(e)
-        pairs.append(pair)
-    c2_ref[...] = analyse(pairs, fz_ref, fy_ref)
-
-
-def last_kernel(a1_ref, a1b_ref, c1_ref, c1b_ref, c2_ref, c2b_ref, by_ref, bz_ref, out_ref):
-    nx = a1_ref.shape[0] + 2
-    nz = a1_ref.shape[2]
-    k = KZ
-    c1 = c1_ref[...]
-    c1b = c1b_ref[...]
-    inner = received(c2_ref[...], c1[:, k : c1.shape[1] - k])
-    ends = jnp.concatenate([c1b[:, k : 2 * k], c1[:, :k], c1[:, c1.shape[1] - k :], c1b[:, 2 * k : 3 * k]], axis=1)
-    outer = received(c2b_ref[...], ends)
-    change = synthesise(jnp.concatenate([inner, outer], axis=1), by_ref, bz_ref)
-    for p in range(2, nx - 2):
-        i, j = (p - 2) // 2, p % 2
-        out_ref[0, p] = a1_ref[p - 1] + change[i][:, j * nz : (j + 1) * nz]
-    last = (nx - 4) // 2
-    out_ref[0, 0] = a1b_ref[0] + change[last][:, :nz]
-    out_ref[0, 1] = a1_ref[0] + change[last][:, nz:]
-    out_ref[0, nx - 2] = a1_ref[nx - 3] + change[last + 1][:, :nz]
-    out_ref[0, nx - 1] = a1b_ref[1] + change[last + 1][:, nz:]
-
-
-def join_kernel(inner_ref, outer_ref, out_ref, sems):
+    for i, p in enumerate(planes_of(first[stage], -1)):
+        a = a_ref[i] if stage == 2 else a_ref[p]
+        a1_ref[i] = a + change[i // 2][:, (i % 2) * nz : (i % 2 + 1) * nz]
+    values = plane_reader((*earlier, a1_ref), nx)
+    ends = []
+    for i, p in enumerate(planes_of(second[stage], 0)):
+        v = values(p)
+        e = v + time_step * LAST_ROW[0] * rate(values(p - 1), v, values(p + 1), mu_ref[p]) + acc_ref[p]
+        e_ref[i] = e
+        ends.append(e)
+    c2_ref[...] = analyse(list(zip(ends[::2], ends[1::2])), fz_ref, fy_ref)
+
+
+def last_kernel(stages, *refs):
+    count = len(stages)
+    c2_refs, c1_refs, a1_refs = refs[:count], refs[count : count + 3], refs[count + 3 : count + 6]
+    by_ref, bz_ref = refs[count + 6 : count + 8]
+    out_ref, buffer, sems = refs[-3:]
+    nx, ny, nz = out_ref.shape[1:]
+    first, second = chunks(nx)
+    where = {}
+    for ref, pairs in zip(c1_refs, first):
+        for i, p in enumerate(planes_of(pairs, -1)):
+            where[p] = (ref, i)
+
+    def column(p):
+        ref, i = where[p]
+        return ref[:, i * KZ : (i + 1) * KZ]
+
+    values = plane_reader(a1_refs, nx)
+    planes = [p for stage in stages for p in planes_of(second[stage], 0)]
+    before = jnp.concatenate([column(p) for p in planes], axis=1)
+    arrived = jnp.concatenate([ref[...] for ref in c2_refs], axis=1)
+    change = synthesise(received(arrived, before), by_ref, bz_ref)
+    copies = []
+    for i in range(0, len(planes), 2):
+        for k in (0, 1):
+            buffer[i + k] = values(planes[i + k]) + change[i // 2][:, k * nz : (k + 1) * nz]
+        copy = pltpu.make_async_copy(buffer.at[pl.ds(i, 2)], out_ref.at[0, pl.ds(planes[i], 2)], sems.at[i // 2])
+        copy.start()
+        copies.append(copy)
+    for copy in copies:
+        copy.wait()
+
+
+def join_kernel(first_ref, second_ref, third_ref, out_ref, sems):
     nx = out_ref.shape[1]
-    copies = [
-        pltpu.make_async_copy(outer_ref.at[pl.ds(0, 2)], out_ref.at[0, pl.ds(0, 2)], sems.at[0]),
-        pltpu.make_async_copy(outer_ref.at[pl.ds(2, 2)], out_ref.at[0, pl.ds(nx - 2, 2)], sems.at[1]),
-    ]
-    for i in range(2, nx - 2, 4):
-        copies.append(
-            pltpu.make_async_copy(inner_ref.at[pl.ds(i - 2, 4)], out_ref.at[0, pl.ds(i, 4)], sems.at[1 + i // 4 + 1])
-        )
+    copies = []
+    for ref, pairs in zip((first_ref, second_ref, third_ref), chunks(nx)[1]):
+        for i, p in enumerate(planes_of(pairs, 0)[::2]):
+            copies.append(
+                pltpu.make_async_copy(ref.at[pl.ds(2 * i, 2)], out_ref.at[0, pl.ds(p, 2)], sems.at[len(copies)])
+            )
     for copy in copies:
         copy.start()
     for copy in copies:
@@ -319,12 +344,18 @@
 
 
 def body(start_states, mobility):
-    a = start_states[0]
-    nx, ny, nz = a.shape
+    a_in = start_states[0]
+    nx, ny, nz = a_in.shape
     slices, slabs = lax.axis_size("tm"), lax.axis_size("gx")
     fz, fy, by, bz = [jnp.asarray(t) for t in tables(ny, nz)]
-    plane = functools.partial(jax.ShapeDtypeStruct, dtype=F32)
-    inner = (nx - 2) // 2
+    like = functools.partial(jax.ShapeDtypeStruct, dtype=F32)
+    first, second = chunks(nx)
+
+    def grid(count):
+        return like((count, ny, nz))
+
+    def modes(pairs):
+        return like((KY, len(pairs) * 2 * KZ))
 
     even_pairs = [(s * slabs + g, s * slabs + (g ^ 1)) for s in range(slices) for g in range(slabs)]
     odd_pairs = []
@@ -337,47 +368,73 @@
                 odd_pairs.append((s * slabs + g, (s ^ 1) * slabs + g))
     ring = [(s, (s + 1) % slices) for s in range(slices)]
 
+    def onward(c):
+        return lax.ppermute(c, "tm", ring)
+
     to_even, to_odd = call(
         pack_kernel,
-        [plane((3, ny, nz)), plane((3, ny, nz))],
+        [grid(3), grid(3)],
         "pack",
         scratch=[pltpu.SemaphoreType.DMA((4,))],
         specs=[ANY, ANY],
         out_specs=[ANY, ANY],
-    )(a, mobility)
+    )(a_in, mobility)
+    from_odd = lax.ppermute(to_odd, ("tm", "gx"), odd_pairs)
     from_even = lax.ppermute(to_even, ("tm", "gx"), even_pairs)
-    from_odd = lax.ppermute(to_odd, ("tm", "gx"), odd_pairs)
-    g, c1 = call(inner_kernel, [plane((nx - 2, ny, nz)), plane((KY, inner * 2 * KZ))], "inner")(a, mobility, fz, fy)
-    c1_in = lax.ppermute(c1, "tm", ring)
-    own = call(own_kernel, plane((KY, inner * 2 * KZ)), "own")(a, fz, fy)
-    ab, gb, c1b = call(
-        outer_kernel, [plane((4, ny, nz)), plane((4, ny, nz)), plane((KY, 4 * KZ))], "outer"
-    )(a, mobility, from_even, from_odd, fz, fy)
-    c1b_in = lax.ppermute(c1b, "tm", ring)
-    acc, own_b = call(later_kernel, [plane((nx, ny, nz)), plane((KY, 4 * KZ))], "later")(
-        a, mobility, g, ab, gb, fz, fy
+    tables_like = [jax.ShapeDtypeStruct(t.shape, t.dtype) for t in (fz, fy, by, bz)]
+    a, mu, fz, fy, by, bz, g0, c10 = call(
+        fetch_kernel,
+        [grid(nx), grid(nx), *tables_like, grid(2 * len(first[0])), modes(first[0])],
+        "fetch",
+        scratch=[pltpu.SemaphoreType.DMA((nx // 2 + 4,))],
+        specs=[ANY] * 7,
+    )(a_in, mobility, fz, fy, by, bz, to_odd)
+    c10_in = onward(c10)
+    g1, c11 = call(inner_kernel, [grid(2 * len(first[1])), modes(first[1])], "inner")(a, mu, fz, fy)
+    c11_in = onward(c11)
+    vmem = pl.BlockSpec(memory_space=pltpu.VMEM)
+    own0, own1 = call(own_kernel, [modes(first[0]), modes(first[1])], "own", specs=[vmem] * 3 + [ANY])(a, fz, fy, g1)
+    ab, g2, c12 = call(outer_kernel, [grid(4), grid(4), modes(first[2])], "outer", specs=[vmem] * 6 + [ANY])(
+        a, mu, from_even, from_odd, fz, fy, own1
     )
-    a1, e2, c2 = call(
-        second_inner_kernel,
-        [plane((nx - 2, ny, nz)), plane((nx - 4, ny, nz)), plane((KY, (inner - 1) * 2 * KZ))],
-        "second_inner",
-    )(a, mobility, acc, c1_in, own, fz, fy, by, bz)
-    c2_in = lax.ppermute(c2, "tm", ring)
-    a1b, e2b, c2b = call(
-        second_outer_kernel,
-        [plane((2, ny, nz)), plane((4, ny, nz)), plane((KY, 4 * KZ))],
-        "second_outer",
-    )(ab, mobility, acc, a1, c1b_in, own_b, fz, fy, by, bz)
-    c2b_in = lax.ppermute(c2b, "tm", ring)
+    c12_in = onward(c12)
+    acc, own2 = call(later_kernel, [grid(nx), modes(first[2])], "later")(a, mu, g0, g1, g2, ab, fz, fy)
+    a1, e, c2_in = [], [], []
+    for stage, (own, c1_in) in enumerate(zip((own0, own1, own2), (c10_in, c11_in, c12_in))):
+        values, end, c2 = call(
+            functools.partial(second_kernel, stage),
+            [grid(2 * len(first[stage])), grid(2 * len(second[stage])), modes(second[stage])],
+            "second",
+        )(ab if stage == 2 else a, mu, acc, c1_in, own, fz, fy, by, bz, *a1)
+        a1.append(values)
+        e.append(end)
+        c2_in.append(onward(c2))
     end_state = call(
         join_kernel,
-        plane((1, nx, ny, nz)),
+        like((1, nx, ny, nz)),
         "join",
-        scratch=[pltpu.SemaphoreType.DMA((2 + (nx - 4) // 4,))],
-        specs=[ANY, ANY],
+        scratch=[pltpu.SemaphoreType.DMA((nx // 2,))],
+        specs=[ANY] * 3,
         out_specs=ANY,
-    )(e2, e2b)
-    next_start = call(last_kernel, plane((1, nx, ny, nz)), "last")(a1, a1b, c1_in, c1b_in, c2_in, c2b_in, by, bz)
+    )(*e)
+    c1_all = (c10_in, c11_in, c12_in)
+    inner_planes = 2 * (len(second[0]) + len(second[1]))
+    result = call(
+        functools.partial(last_kernel, (0, 1)),
+        like((1, nx, ny, nz)),
+        "last_inner",
+        scratch=[pltpu.VMEM((inner_planes, ny, nz), F32), pltpu.SemaphoreType.DMA((inner_planes // 2,))],
+        out_specs=ANY,
+    )(c2_in[0], c2_in[1], *c1_all, *a1, by, bz)
+    next_start = call(
+        functools.partial(last_kernel, (2,)),
+        like((1, nx, ny, nz)),
+        "last_outer",
+        scratch=[pltpu.VMEM((4, ny, nz), F32), pltpu.SemaphoreType.DMA((2,))],
+        specs=[vmem] * 9 + [ANY],
+        out_specs=ANY,
+        aliases={9: 0},
+    )(c2_in[2], *c1_all, *a1, by, bz, result)
     return end_state, next_start
 
 

time: 36.7 us -> 28.7 us (0.78)
  waiting for transfers between devices: 15.6 us -> 2.31 us
  starting transfers between devices: 6.51 us -> 10.8 us
  Pallas kernels: 9.29 us -> 12.1 us
  local copies, waits for them, and re-layouts: 4.2 us -> 2.46 us
    ppermute x4 -> x6, waiting for transfers between devices: 9.64 us -> 2.31 us  [onward(): return lax.ppermute(c, 'tm', ring)]
    ppermute x1, waiting for transfers between devices: 5.96 us -> 0.01 us  [body(): from_odd = lax.ppermute(to_odd, ('tm', 'gx'), odd_pairs)]
    ppermute x4 -> x6, starting transfers between devices: 4.89 us -> 7.75 us  [onward(): return lax.ppermute(c, 'tm', ring)]
    pallas_call x9 -> x12, Pallas kernels: 9.29 us -> 12.1 us  [run(): pl.pallas_call(kernel, out_shape=outs, in_specs=specs or [pl.BlockSpec(me...]
    unnamed x18 -> x12, local copies, waits for them, and re-layouts: 4.2 us -> 2.46 us
    ppermute x1, starting transfers between devices: 1.56 us -> 2.56 us  [body(): from_odd = lax.ppermute(to_odd, ('tm', 'gx'), odd_pairs)]
    ppermute x1, starting transfers between devices: 0.07 us -> 0.52 us  [body(): from_even = lax.ppermute(to_even, ('tm', 'gx'), even_pairs)]
  transfers between devices with their start and end apart: 6 -> 8, of which waited for: 3 -> 3; matrix products, arithmetic and copies ran while one was open for 0% -> 0% of each run, Pallas kernels for 13% -> 37%
where the time goes in v2:
time: 28.7 us; the launch traced here: 28.5 us
  Pallas kernels  12.1 us (42%)
  starting transfers between devices  10.8 us (38%)
  local copies, waits for them, and re-layouts  2.46 us (9%)
  waiting for transfers between devices  2.31 us (8%)
  between operations  0.76 us (3%)
    pallas_call x12, Pallas kernels, run(): pl.pallas_call(kernel, out_shape=outs, in_specs=specs or [pl.BlockSpec(me...  12.1 us
    ppermute x6, starting transfers between devices, onward(): return lax.ppermute(c, 'tm', ring)  7.75 us
    ppermute x1, starting transfers between devices, body(): from_odd = lax.ppermute(to_odd, ('tm', 'gx'), odd_pairs)  2.56 us
    unnamed x12, local copies, waits for them, and re-layouts  2.46 us
    ppermute x6, waiting for transfers between devices, onward(): return lax.ppermute(c, 'tm', ring)  2.31 us
  transfers between devices with their start and end apart: 8, of which 3 were waited for; matrix products, arithmetic and copies ran while one was open for 0% of the time, Pallas kernels for 37%

profile of v2, /device:TPU:0, one launch (start us, length us, event | category | flops | bytes accessed | tf_op | source)
XLA Modules:
  0.0 28.5 jit_solution(8639792786954160787)
XLA Ops:
  0.6 1.2 %copy-done = f32[1,16,128,128]{3,2,1,0:T(8,128)S(1)} copy-done((f32[1,16,128,128]{3,2,1,0:T(8,128)S(1)}, f32[1,16,128,128]{3,2,1,0:T(8,128)}, u32[]{:S(2)}) %copy-start) | copy-done | bytes 1048600
  1.9 1.2 %copy-done.1 = f32[16,128,128]{2,1,0:T(8,128)S(1)} copy-done((f32[16,128,128]{2,1,0:T(8,128)S(1)}, f32[16,128,128]{2,1,0:T(8,128)}, u32[]{:S(2)}) %copy-start.1) | copy-done | bytes 1048600
  3.1 0.6 %pack.1 = (f32[3,128,128]{2,1,0:T(8,128)S(1)}, f32[3,128,128]{2,1,0:T(8,128)S(1)}) custom-call(f32[16,128,128]{2,1,0:T(8,128)S(1)} %bitcast.1, f32[16,128,128]{2,1,0:T(8,128)S(1)} %copy-done.1), custom_call_target="tpu_custom_call" | custom-call | flops 10000000 | bytes 1000000 | tf_op jit(solution)/shard_map/pack/pallas_call | solution.py:130
  3.7 0.5 %collective-permute-start = (f32[3,128,128]{2,1,0:T(8,128)S(1)}, f32[3,128,128]{2,1,0:T(8,128)S(1)}, u32[]{:S(2)}, u32[]{:S(2)}) collective-permute-start(f32[3,128,128]{2,1,0:T(8,128)S(1)} %get-tuple-element.37), channel_id=1, source_target_pairs={{0,1},{1,0},{2,3},{3,2},{4,5},{5,4},{6,7},{7,6},{8,9},{9,8},{10,11... | collective-permute-start | bytes 589832 | tf_op jit(solution)/shard_map/ppermute | solution.py:383
  4.2 2.6 %collective-permute-start.1 = (f32[3,128,128]{2,1,0:T(8,128)S(1)}, f32[3,128,128]{2,1,0:T(8,128)S(1)}, u32[]{:S(2)}, u32[]{:S(2)}) collective-permute-start(f32[3,128,128]{2,1,0:T(8,128)S(1)} %get-tuple-element.30.after), channel_id=1, source_target_pairs={{0,8},{1,2},{2,1},{3,4},{4,3},{5,6},{6,5},{7,15},{8,0},{9,10},{10,... | collective-permute-start | bytes 589832 | tf_op jit(solution)/shard_map/ppermute | solution.py:382
  6.8 1.8 %fetch.1 = (f32[16,128,128]{2,1,0:T(8,128)S(1)}, f32[16,128,128]{2,1,0:T(8,128)S(1)}, bf16[768,128]{1,0:T(8,128)(2,1)S(1)}, bf16[64,384]{1,0:T(8,128)(2,1)S(1)},...) custom-call(f32[16,128,128]{2,1,0:T(8,128)S(1)} %bitcast.2, ...), custom_call_target="tpu_custom_call" | custom-call | flops 10000000 | bytes 1000000 | tf_op jit(solution)/shard_map/fetch/pallas_call | solution.py:130
  8.9 0.7 %inner.1 = (f32[6,128,128]{2,1,0:T(8,128)S(1)}, f32[64,384]{1,0:T(8,128)S(1)}) custom-call(f32[16,128,128]{2,1,0:T(8,128)S(1)} %get-tuple-element.31.a_ref.refs_0_, f32[16,128,128]{2,1,0:T(8,128)S(1)} %get-tuple-element.32.mu_ref.refs_1_, bf16[768,128]{1,0:T(8,128)(2,1)S(1)} %get-tuple-element.34.fz_ref.refs_5_, ...), custom_call_target="tpu_custom_call" | custom-call | flops 10000000 | bytes 1000000 | tf_op jit(solution)/shard_map/inner/pallas_call | solution.py:130
  9.6 2.8 %collective-permute-start.3 = (f32[64,384]{1,0:T(8,128)S(1)}, f32[64,384]{1,0:T(8,128)S(1)}, u32[]{:S(2)}, u32[]{:S(2)}) collective-permute-start(f32[64,384]{1,0:T(8,128)S(1)} %get-tuple-element.47), channel_id=1, source_target_pairs={{0,8},{8,16},{16,24},{24,0},{1,9},{9,17},{17,25},{25,1},{2,10},{10... | collective-permute-start | bytes 294920 | tf_op jit(solution)/shard_map/ppermute | solution.py:372
  12.3 0.8 %own.1 = (f32[64,512]{1,0:T(8,128)S(1)}, f32[64,384]{1,0:T(8,128)S(1)}) custom-call(f32[16,128,128]{2,1,0:T(8,128)S(1)} %get-tuple-element.31.a_ref.refs_0_, bf16[768,128]{1,0:T(8,128)(2,1)S(1)} %get-tuple-element.34.fz_ref.refs_5_, bf16[64,384]{1,0:T(8,128)(2,1)S(1)} %get-tuple-element.35.fy_ref.refs_6_, f32[6,128,128]{2,1,0:T(8,128)S(1)} %get-tuple-element.36.after.g1_ref), custom_call_target="tpu_custom_call" | custom-call | flops 10000000 | bytes 1000000 | tf_op jit(solution)/shard_map/own/pallas_call | solution.py:130
  13.1 0.6 %outer.1 = (f32[4,128,128]{2,1,0:T(8,128)S(1)}, f32[4,128,128]{2,1,0:T(8,128)S(1)}, f32[64,256]{1,0:T(8,128)S(1)}) custom-call(f32[16,128,128]{2,1,0:T(8,128)S(1)} %get-tuple-element.31.a_ref.refs_0_, f32[16,128,128]{2,1,0:T(8,128)S(1)} %get-tuple-element.32.mu_ref.refs_1_, f32[3,128,128]{2,1,0:T(8,128)S(1)} %collective-permute-done.even_ref, ...), custom_call_target="tpu_custom_call" | custom-call | flops 10000000 | bytes 1000000 | tf_op jit(solution)/shard_map/outer/pallas_call | solution.py:130
  13.7 0.6 %collective-permute-start.4 = (f32[64,256]{1,0:T(8,128)S(1)}, f32[64,256]{1,0:T(8,128)S(1)}, u32[]{:S(2)}, u32[]{:S(2)}) collective-permute-start(f32[64,256]{1,0:T(8,128)S(1)} %get-tuple-element.50), channel_id=1, source_target_pairs={{0,8},{8,16},{16,24},{24,0},{1,9},{9,17},{17,25},{25,1},{2,10},{10... | collective-permute-start | bytes 196616 | tf_op jit(solution)/shard_map/ppermute | solution.py:372
  14.3 1.0 %later.1 = (f32[16,128,128]{2,1,0:T(8,128)S(1)}, f32[64,256]{1,0:T(8,128)S(1)}) custom-call(f32[16,128,128]{2,1,0:T(8,128)S(1)} %get-tuple-element.31.a_ref.refs_0_, f32[16,128,128]{2,1,0:T(8,128)S(1)} %get-tuple-element.32.mu_ref.refs_1_, f32[8,128,128]{2,1,0:T(8,128)S(1)} %get-tuple-element.33.g0_ref, f32[6,128,128]{2,1,0:T(8,128)S(1)} %get-tuple-element.36.after.g1_ref, ...), custom_call_target="tpu_custom_call" | custom-call | flops 10000000 | bytes 1000000 | tf_op jit(solution)/shard_map/later/pallas_call | solution.py:130
  15.3 0.5 %collective-permute-done.2.refs_3_.refs_2_.refs_1_ = f32[64,512]{1,0:T(8,128)S(1)} collective-permute-done((f32[64,512]{1,0:T(8,128)S(1)}, f32[64,512]{1,0:T(8,128)S(1)}, u32[]{:S(2)}, u32[]{:S(2)}) %collective-permute-start.2) | collective-permute-done | bytes 131104 | tf_op jit(solution)/shard_map/ppermute | solution.py:372
  15.8 1.2 %second.3 = (f32[8,128,128]{2,1,0:T(8,128)S(1)}, f32[6,128,128]{2,1,0:T(8,128)S(1)}, f32[64,384]{1,0:T(8,128)S(1)}) custom-call(f32[16,128,128]{2,1,0:T(8,128)S(1)} %get-tuple-element.31.a_ref.refs_0_, f32[16,128,128]{2,1,0:T(8,128)S(1)} %get-tuple-element.32.mu_ref.refs_1_, f32[16,128,128]{2,1,0:T(8,128)S(1)} %get-tuple-element.41.refs_2_, ...), custom_call_target="tpu_custom_call" | custom-call | flops 10000000 | bytes 1000000 | tf_op jit(solution)/shard_map/second/pallas_call | solution.py:130
  17.0 1.0 %collective-permute-start.6 = (f32[64,384]{1,0:T(8,128)S(1)}, f32[64,384]{1,0:T(8,128)S(1)}, u32[]{:S(2)}, u32[]{:S(2)}) collective-permute-start(f32[64,384]{1,0:T(8,128)S(1)} %get-tuple-element.56), channel_id=1, source_target_pairs={{0,8},{8,16},{16,24},{24,0},{1,9},{9,17},{17,25},{25,1},{2,10},{10... | collective-permute-start | bytes 294920 | tf_op jit(solution)/shard_map/ppermute | solution.py:372
  18.0 1.1 %second.4 = (f32[6,128,128]{2,1,0:T(8,128)S(1)}, f32[6,128,128]{2,1,0:T(8,128)S(1)}, f32[64,384]{1,0:T(8,128)S(1)}) custom-call(f32[16,128,128]{2,1,0:T(8,128)S(1)} %get-tuple-element.31.a_ref.refs_0_, f32[16,128,128]{2,1,0:T(8,128)S(1)} %get-tuple-element.32.mu_ref.refs_1_, f32[16,128,128]{2,1,0:T(8,128)S(1)} %get-tuple-element.41.refs_2_, ...), custom_call_target="tpu_custom_call" | custom-call | flops 10000000 | bytes 1000000 | tf_op jit(solution)/shard_map/second/pallas_call | solution.py:130
  19.1 2.1 %collective-permute-start.7 = (f32[64,384]{1,0:T(8,128)S(1)}, f32[64,384]{1,0:T(8,128)S(1)}, u32[]{:S(2)}, u32[]{:S(2)}) collective-permute-start(f32[64,384]{1,0:T(8,128)S(1)} %get-tuple-element.57), channel_id=1, source_target_pairs={{0,8},{8,16},{16,24},{24,0},{1,9},{9,17},{17,25},{25,1},{2,10},{10... | collective-permute-start | bytes 294920 | tf_op jit(solution)/shard_map/ppermute | solution.py:372
  21.2 0.9 %second.5 = (f32[4,128,128]{2,1,0:T(8,128)S(1)}, f32[4,128,128]{2,1,0:T(8,128)S(1)}, f32[64,256]{1,0:T(8,128)S(1)}) custom-call(f32[4,128,128]{2,1,0:T(8,128)S(1)} %get-tuple-element.40.ab_ref.refs_0_, f32[16,128,128]{2,1,0:T(8,128)S(1)} %get-tuple-element.32.mu_ref.refs_1_, f32[16,128,128]{2,1,0:T(8,128)S(1)} %get-tuple-element.41.refs_2_, ...), custom_call_target="tpu_custom_call" | custom-call | flops 10000000 | bytes 1000000 | tf_op jit(solution)/shard_map/second/pallas_call | solution.py:130
  22.1 1.0 %collective-permute-start.5 = (f32[64,256]{1,0:T(8,128)S(1)}, f32[64,256]{1,0:T(8,128)S(1)}, u32[]{:S(2)}, u32[]{:S(2)}) collective-permute-start(f32[64,256]{1,0:T(8,128)S(1)} %get-tuple-element.54), channel_id=1, source_target_pairs={{0,8},{8,16},{16,24},{24,0},{1,9},{9,17},{17,25},{25,1},{2,10},{10... | collective-permute-start | bytes 196616 | tf_op jit(solution)/shard_map/ppermute | solution.py:372
  23.1 1.0 %join.1 = f32[1,16,128,128]{3,2,1,0:T(8,128)} custom-call(f32[6,128,128]{2,1,0:T(8,128)S(1)} %get-tuple-element.46.first_ref, f32[6,128,128]{2,1,0:T(8,128)S(1)} %get-tuple-element.49.second_ref, f32[4,128,128]{2,1,0:T(8,128)S(1)} %get-tuple-element.53.third_ref), custom_call_target="tpu_custom_call" | custom-call | flops 10000000 | bytes 1000000 | tf_op jit(solution)/shard_map/join/pallas_call | solution.py:130
  24.2 1.3 %collective-permute-done.7.refs_1_ = f32[64,384]{1,0:T(8,128)S(1)} collective-permute-done((f32[64,384]{1,0:T(8,128)S(1)}, f32[64,384]{1,0:T(8,128)S(1)}, u32[]{:S(2)}, u32[]{:S(2)}) %collective-permute-start.7) | collective-permute-done | bytes 98336 | tf_op jit(solution)/shard_map/ppermute | solution.py:372
  25.4 1.4 %last_inner.1.refs_9_ = f32[1,16,128,128]{3,2,1,0:T(8,128)} custom-call(f32[64,384]{1,0:T(8,128)S(1)} %collective-permute-done.6.refs_0_, f32[64,384]{1,0:T(8,128)S(1)} %collective-permute-done.7.refs_1_, f32[64,512]{1,0:T(8,128)S(1)} %collective-permute-done.2.refs_3_.refs_2_.refs_1_, f32[64,384]{1,0:T(8,128)S(1)} %collective-permute-done.3.refs_3_.refs_2_, ...), custom_call_target="tpu_custom_call" | custom-call | flops 10000000 | bytes 1000000 | tf_op jit(solution)/shard_map/last_inner/pallas_call | solution.py:130
  26.8 0.5 %collective-permute-done.5.refs_0_ = f32[64,256]{1,0:T(8,128)S(1)} collective-permute-done((f32[64,256]{1,0:T(8,128)S(1)}, f32[64,256]{1,0:T(8,128)S(1)}, u32[]{:S(2)}, u32[]{:S(2)}) %collective-permute-start.5) | collective-permute-done | bytes 65568 | tf_op jit(solution)/shard_map/ppermute | solution.py:372
  27.3 1.1 %last_outer.1 = f32[1,16,128,128]{3,2,1,0:T(8,128)} custom-call(f32[64,256]{1,0:T(8,128)S(1)} %collective-permute-done.5.refs_0_, f32[64,512]{1,0:T(8,128)S(1)} %collective-permute-done.2.refs_3_.refs_2_.refs_1_, f32[64,384]{1,0:T(8,128)S(1)} %collective-permute-done.3.refs_3_.refs_2_, ...), custom_call_target="tpu_custom_call", output_to_operand_aliasing={{}: (9, {})} | custom-call | flops 10000000 | bytes 1000000 | tf_op jit(solution)/shard_map/last_outer/pallas_call | solution.py:130
  (16 shorter events, 0.4 us)
Async XLA Ops:
  0.6 1.2 %copy-start = (f32[1,16,128,128]{3,2,1,0:T(8,128)S(1)}, f32[1,16,128,128]{3,2,1,0:T(8,128)}, u32[]{:S(2)}) copy-start(f32[1,16,128,128]{3,2,1,0:T(8,128)} %param.6) | copy-start | bytes 3145732
  1.9 1.2 %copy-start.1 = (f32[16,128,128]{2,1,0:T(8,128)S(1)}, f32[16,128,128]{2,1,0:T(8,128)}, u32[]{:S(2)}) copy-start(f32[16,128,128]{2,1,0:T(8,128)} %mu_in.1) | copy-start | bytes 3145732
  3.1 3.7 %copy-start.2 = (bf16[384,256]{1,0:T(8,128)(2,1)S(1)}, bf16[384,256]{1,0:T(8,128)(2,1)}, u32[]{:S(2)}) copy-start(bf16[384,256]{1,0:T(8,128)(2,1)} %constant.11.clone.bz_in) | copy-start | bytes 589828
  3.1 3.7 %copy-start.3 = (bf16[768,128]{1,0:T(8,128)(2,1)S(1)}, bf16[768,128]{1,0:T(8,128)(2,1)}, u32[]{:S(2)}) copy-start(bf16[768,128]{1,0:T(8,128)(2,1)} %constant.8.clone.fz_in) | copy-start | bytes 589828
  3.1 3.7 %copy-start.4 = (bf16[128,192]{1,0:T(8,128)(2,1)S(1)}, bf16[128,192]{1,0:T(8,128)(2,1)}, u32[]{:S(2)}) copy-start(bf16[128,192]{1,0:T(8,128)(2,1)} %constant.10.clone.by_in) | copy-start | bytes 147460
  3.1 3.7 %copy-start.5 = (bf16[64,384]{1,0:T(8,128)(2,1)S(1)}, bf16[64,384]{1,0:T(8,128)(2,1)}, u32[]{:S(2)}) copy-start(bf16[64,384]{1,0:T(8,128)(2,1)} %constant.9.clone.fy_in) | copy-start | bytes 147460
  3.7 9.4 %collective-permute-start = (f32[3,128,128]{2,1,0:T(8,128)S(1)}, f32[3,128,128]{2,1,0:T(8,128)S(1)}, u32[]{:S(2)}, u32[]{:S(2)}) collective-permute-start(f32[3,128,128]{2,1,0:T(8,128)S(1)} %get-tuple-element.37), channel_id=1, source_target_pairs={{0,1},{1,0},{2,3},{3,2},{4,5},{5,4},{6,7},{7,6},{8,9},{9,8},{10,11... | collective-permute-start | bytes 589832 | tf_op jit(solution)/shard_map/ppermute | solution.py:383
  4.2 8.9 %collective-permute-start.1 = (f32[3,128,128]{2,1,0:T(8,128)S(1)}, f32[3,128,128]{2,1,0:T(8,128)S(1)}, u32[]{:S(2)}, u32[]{:S(2)}) collective-permute-start(f32[3,128,128]{2,1,0:T(8,128)S(1)} %get-tuple-element.30.after), channel_id=1, source_target_pairs={{0,8},{1,2},{2,1},{3,4},{4,3},{5,6},{6,5},{7,15},{8,0},{9,10},{10,... | collective-permute-start | bytes 589832 | tf_op jit(solution)/shard_map/ppermute | solution.py:382
  8.5 7.3 %collective-permute-start.2 = (f32[64,512]{1,0:T(8,128)S(1)}, f32[64,512]{1,0:T(8,128)S(1)}, u32[]{:S(2)}, u32[]{:S(2)}) collective-permute-start(f32[64,512]{1,0:T(8,128)S(1)} %get-tuple-element.42), channel_id=1, source_target_pairs={{0,8},{8,16},{16,24},{24,0},{1,9},{9,17},{17,25},{25,1},{2,10},{10... | collective-permute-start | bytes 393224 | tf_op jit(solution)/shard_map/ppermute | solution.py:372
  9.6 8.5 %collective-permute-start.3 = (f32[64,384]{1,0:T(8,128)S(1)}, f32[64,384]{1,0:T(8,128)S(1)}, u32[]{:S(2)}, u32[]{:S(2)}) collective-permute-start(f32[64,384]{1,0:T(8,128)S(1)} %get-tuple-element.47), channel_id=1, source_target_pairs={{0,8},{8,16},{16,24},{24,0},{1,9},{9,17},{17,25},{25,1},{2,10},{10... | collective-permute-start | bytes 294920 | tf_op jit(solution)/shard_map/ppermute | solution.py:372
  13.7 7.6 %collective-permute-start.4 = (f32[64,256]{1,0:T(8,128)S(1)}, f32[64,256]{1,0:T(8,128)S(1)}, u32[]{:S(2)}, u32[]{:S(2)}) collective-permute-start(f32[64,256]{1,0:T(8,128)S(1)} %get-tuple-element.50), channel_id=1, source_target_pairs={{0,8},{8,16},{16,24},{24,0},{1,9},{9,17},{17,25},{25,1},{2,10},{10... | collective-permute-start | bytes 196616 | tf_op jit(solution)/shard_map/ppermute | solution.py:372
  17.0 7.1 %collective-permute-start.6 = (f32[64,384]{1,0:T(8,128)S(1)}, f32[64,384]{1,0:T(8,128)S(1)}, u32[]{:S(2)}, u32[]{:S(2)}) collective-permute-start(f32[64,384]{1,0:T(8,128)S(1)} %get-tuple-element.56), channel_id=1, source_target_pairs={{0,8},{8,16},{16,24},{24,0},{1,9},{9,17},{17,25},{25,1},{2,10},{10... | collective-permute-start | bytes 294920 | tf_op jit(solution)/shard_map/ppermute | solution.py:372
  19.1 6.3 %collective-permute-start.7 = (f32[64,384]{1,0:T(8,128)S(1)}, f32[64,384]{1,0:T(8,128)S(1)}, u32[]{:S(2)}, u32[]{:S(2)}) collective-permute-start(f32[64,384]{1,0:T(8,128)S(1)} %get-tuple-element.57), channel_id=1, source_target_pairs={{0,8},{8,16},{16,24},{24,0},{1,9},{9,17},{17,25},{25,1},{2,10},{10... | collective-permute-start | bytes 294920 | tf_op jit(solution)/shard_map/ppermute | solution.py:372
  22.1 5.2 %collective-permute-start.5 = (f32[64,256]{1,0:T(8,128)S(1)}, f32[64,256]{1,0:T(8,128)S(1)}, u32[]{:S(2)}, u32[]{:S(2)}) collective-permute-start(f32[64,256]{1,0:T(8,128)S(1)} %get-tuple-element.54), channel_id=1, source_target_pairs={{0,8},{8,16},{16,24},{24,0},{1,9},{9,17},{17,25},{25,1},{2,10},{10... | collective-permute-start | bytes 196616 | tf_op jit(solution)/shard_map/ppermute | solution.py:372

commit v3 on v2

--- a/solution.py
+++ b/solution.py
@@ -344,10 +344,11 @@
 
 
 def body(start_states, mobility):
-    a_in = start_states[0]
-    nx, ny, nz = a_in.shape
+    nx, ny, nz = mobility.shape
+    a_in = pltpu.with_memory_space_constraint(start_states[0], pltpu.HBM)
+    mobility = pltpu.with_memory_space_constraint(mobility, pltpu.HBM)
     slices, slabs = lax.axis_size("tm"), lax.axis_size("gx")
-    fz, fy, by, bz = [jnp.asarray(t) for t in tables(ny, nz)]
+    fz, fy, by, bz = [pltpu.with_memory_space_constraint(jnp.asarray(t), pltpu.HBM) for t in tables(ny, nz)]
     like = functools.partial(jax.ShapeDtypeStruct, dtype=F32)
     first, second = chunks(nx)
 

time: 28.7 us -> 27.2 us (0.948)
  local copies, waits for them, and re-layouts: 2.46 us -> 0 us
  Pallas kernels: 12.1 us -> 13.2 us
    unnamed x12 -> x0, local copies, waits for them, and re-layouts: 2.46 us -> none
    pallas_call x12, Pallas kernels: 12.1 us -> 13.2 us  [run(): pl.pallas_call(kernel, out_shape=outs, in_specs=specs or [pl.BlockSpec(me...]
  transfers between devices with their start and end apart: 8 -> 8, of which waited for: 3 -> 3; matrix products, arithmetic and copies ran while one was open for 0% -> 0% of each run, Pallas kernels for 37% -> 41%
where the time goes in v3:
time: 27.2 us; the launch traced here: 27 us
  Pallas kernels  13.2 us (49%)
  starting transfers between devices  10.8 us (40%)
  waiting for transfers between devices  2.31 us (8%)
  between operations  0.75 us (3%)
    pallas_call x12, Pallas kernels, run(): pl.pallas_call(kernel, out_shape=outs, in_specs=specs or [pl.BlockSpec(me...  13.2 us
    ppermute x6, starting transfers between devices, onward(): return lax.ppermute(c, 'tm', ring)  7.75 us
    ppermute x1, starting transfers between devices, body(): from_odd = lax.ppermute(to_odd, ('tm', 'gx'), odd_pairs)  2.56 us
    ppermute x6, waiting for transfers between devices, onward(): return lax.ppermute(c, 'tm', ring)  2.31 us
  transfers between devices with their start and end apart: 8, of which 3 were waited for; matrix products, arithmetic and copies ran while one was open for 0% of the time, Pallas kernels for 41%

profile of v3, /device:TPU:0, one launch (start us, length us, event | category | flops | bytes accessed | tf_op | source)
XLA Modules:
  0.0 27.0 jit_solution(4332419503362166134)
XLA Ops:
  0.6 1.0 %pack.1 = (f32[3,128,128]{2,1,0:T(8,128)S(1)}, f32[3,128,128]{2,1,0:T(8,128)S(1)}) custom-call(f32[16,128,128]{2,1,0:T(8,128)} %bitcast.1, f32[16,128,128]{2,1,0:T(8,128)} %mu_in.1), custom_call_target="tpu_custom_call" | custom-call | flops 10000000 | bytes 1000000 | tf_op jit(solution)/shard_map/pack/pallas_call | solution.py:130
  1.7 0.5 %collective-permute-start = (f32[3,128,128]{2,1,0:T(8,128)S(1)}, f32[3,128,128]{2,1,0:T(8,128)S(1)}, u32[]{:S(2)}, u32[]{:S(2)}) collective-permute-start(f32[3,128,128]{2,1,0:T(8,128)S(1)} %get-tuple-element.37), channel_id=1, source_target_pairs={{0,1},{1,0},{2,3},{3,2},{4,5},{5,4},{6,7},{7,6},{8,9},{9,8},{10,11... | collective-permute-start | bytes 589832 | tf_op jit(solution)/shard_map/ppermute | solution.py:384
  2.2 2.6 %collective-permute-start.1 = (f32[3,128,128]{2,1,0:T(8,128)S(1)}, f32[3,128,128]{2,1,0:T(8,128)S(1)}, u32[]{:S(2)}, u32[]{:S(2)}) collective-permute-start(f32[3,128,128]{2,1,0:T(8,128)S(1)} %get-tuple-element.30.after), channel_id=1, source_target_pairs={{0,8},{1,2},{2,1},{3,4},{4,3},{5,6},{6,5},{7,15},{8,0},{9,10},{10,... | collective-permute-start | bytes 589832 | tf_op jit(solution)/shard_map/ppermute | solution.py:383
  4.8 2.3 %fetch.1 = (f32[16,128,128]{2,1,0:T(8,128)S(1)}, f32[16,128,128]{2,1,0:T(8,128)S(1)}, bf16[768,128]{1,0:T(8,128)(2,1)S(1)}, bf16[64,384]{1,0:T(8,128)(2,1)S(1)},...) custom-call(f32[16,128,128]{2,1,0:T(8,128)} %bitcast.2, ...), custom_call_target="tpu_custom_call" | custom-call | flops 10000000 | bytes 1000000 | tf_op jit(solution)/shard_map/fetch/pallas_call | solution.py:130
  7.1 0.1 collective-permute-start.2
  7.2 0.7 %inner.1 = (f32[6,128,128]{2,1,0:T(8,128)S(1)}, f32[64,384]{1,0:T(8,128)S(1)}) custom-call(f32[16,128,128]{2,1,0:T(8,128)S(1)} %get-tuple-element.31.a_ref.refs_0_, f32[16,128,128]{2,1,0:T(8,128)S(1)} %get-tuple-element.32.mu_ref.refs_1_, bf16[768,128]{1,0:T(8,128)(2,1)S(1)} %get-tuple-element.34.fz_ref.refs_5_, ...), custom_call_target="tpu_custom_call" | custom-call | flops 10000000 | bytes 1000000 | tf_op jit(solution)/shard_map/inner/pallas_call | solution.py:130
  7.9 3.0 %collective-permute-start.3 = (f32[64,384]{1,0:T(8,128)S(1)}, f32[64,384]{1,0:T(8,128)S(1)}, u32[]{:S(2)}, u32[]{:S(2)}) collective-permute-start(f32[64,384]{1,0:T(8,128)S(1)} %get-tuple-element.47), channel_id=1, source_target_pairs={{0,8},{8,16},{16,24},{24,0},{1,9},{9,17},{17,25},{25,1},{2,10},{10... | collective-permute-start | bytes 294920 | tf_op jit(solution)/shard_map/ppermute | solution.py:373
  10.9 0.8 %own.1 = (f32[64,512]{1,0:T(8,128)S(1)}, f32[64,384]{1,0:T(8,128)S(1)}) custom-call(f32[16,128,128]{2,1,0:T(8,128)S(1)} %get-tuple-element.31.a_ref.refs_0_, bf16[768,128]{1,0:T(8,128)(2,1)S(1)} %get-tuple-element.34.fz_ref.refs_5_, bf16[64,384]{1,0:T(8,128)(2,1)S(1)} %get-tuple-element.35.fy_ref.refs_6_, f32[6,128,128]{2,1,0:T(8,128)S(1)} %get-tuple-element.36.after.g1_ref), custom_call_target="tpu_custom_call" | custom-call | flops 10000000 | bytes 1000000 | tf_op jit(solution)/shard_map/own/pallas_call | solution.py:130
  11.7 0.0 collective-permute-done.even_ref
  11.7 0.6 %outer.1 = (f32[4,128,128]{2,1,0:T(8,128)S(1)}, f32[4,128,128]{2,1,0:T(8,128)S(1)}, f32[64,256]{1,0:T(8,128)S(1)}) custom-call(f32[16,128,128]{2,1,0:T(8,128)S(1)} %get-tuple-element.31.a_ref.refs_0_, f32[16,128,128]{2,1,0:T(8,128)S(1)} %get-tuple-element.32.mu_ref.refs_1_, f32[3,128,128]{2,1,0:T(8,128)S(1)} %collective-permute-done.even_ref, ...), custom_call_target="tpu_custom_call" | custom-call | flops 10000000 | bytes 1000000 | tf_op jit(solution)/shard_map/outer/pallas_call | solution.py:130
  12.3 0.6 %collective-permute-start.4 = (f32[64,256]{1,0:T(8,128)S(1)}, f32[64,256]{1,0:T(8,128)S(1)}, u32[]{:S(2)}, u32[]{:S(2)}) collective-permute-start(f32[64,256]{1,0:T(8,128)S(1)} %get-tuple-element.50), channel_id=1, source_target_pairs={{0,8},{8,16},{16,24},{24,0},{1,9},{9,17},{17,25},{25,1},{2,10},{10... | collective-permute-start | bytes 196616 | tf_op jit(solution)/shard_map/ppermute | solution.py:373
  12.9 1.0 %later.1 = (f32[16,128,128]{2,1,0:T(8,128)S(1)}, f32[64,256]{1,0:T(8,128)S(1)}) custom-call(f32[16,128,128]{2,1,0:T(8,128)S(1)} %get-tuple-element.31.a_ref.refs_0_, f32[16,128,128]{2,1,0:T(8,128)S(1)} %get-tuple-element.32.mu_ref.refs_1_, f32[8,128,128]{2,1,0:T(8,128)S(1)} %get-tuple-element.33.g0_ref, f32[6,128,128]{2,1,0:T(8,128)S(1)} %get-tuple-element.36.after.g1_ref, ...), custom_call_target="tpu_custom_call" | custom-call | flops 10000000 | bytes 1000000 | tf_op jit(solution)/shard_map/later/pallas_call | solution.py:130
  13.9 0.5 %collective-permute-done.2.refs_3_.refs_2_.refs_1_ = f32[64,512]{1,0:T(8,128)S(1)} collective-permute-done((f32[64,512]{1,0:T(8,128)S(1)}, f32[64,512]{1,0:T(8,128)S(1)}, u32[]{:S(2)}, u32[]{:S(2)}) %collective-permute-start.2) | collective-permute-done | bytes 131104 | tf_op jit(solution)/shard_map/ppermute | solution.py:373
  14.4 1.2 %second.3 = (f32[8,128,128]{2,1,0:T(8,128)S(1)}, f32[6,128,128]{2,1,0:T(8,128)S(1)}, f32[64,384]{1,0:T(8,128)S(1)}) custom-call(f32[16,128,128]{2,1,0:T(8,128)S(1)} %get-tuple-element.31.a_ref.refs_0_, f32[16,128,128]{2,1,0:T(8,128)S(1)} %get-tuple-element.32.mu_ref.refs_1_, f32[16,128,128]{2,1,0:T(8,128)S(1)} %get-tuple-element.41.refs_2_, ...), custom_call_target="tpu_custom_call" | custom-call | flops 10000000 | bytes 1000000 | tf_op jit(solution)/shard_map/second/pallas_call | solution.py:130
  15.6 1.0 %collective-permute-start.6 = (f32[64,384]{1,0:T(8,128)S(1)}, f32[64,384]{1,0:T(8,128)S(1)}, u32[]{:S(2)}, u32[]{:S(2)}) collective-permute-start(f32[64,384]{1,0:T(8,128)S(1)} %get-tuple-element.56), channel_id=1, source_target_pairs={{0,8},{8,16},{16,24},{24,0},{1,9},{9,17},{17,25},{25,1},{2,10},{10... | collective-permute-start | bytes 294920 | tf_op jit(solution)/shard_map/ppermute | solution.py:373
  16.6 1.1 %second.4 = (f32[6,128,128]{2,1,0:T(8,128)S(1)}, f32[6,128,128]{2,1,0:T(8,128)S(1)}, f32[64,384]{1,0:T(8,128)S(1)}) custom-call(f32[16,128,128]{2,1,0:T(8,128)S(1)} %get-tuple-element.31.a_ref.refs_0_, f32[16,128,128]{2,1,0:T(8,128)S(1)} %get-tuple-element.32.mu_ref.refs_1_, f32[16,128,128]{2,1,0:T(8,128)S(1)} %get-tuple-element.41.refs_2_, ...), custom_call_target="tpu_custom_call" | custom-call | flops 10000000 | bytes 1000000 | tf_op jit(solution)/shard_map/second/pallas_call | solution.py:130
  17.7 2.1 %collective-permute-start.7 = (f32[64,384]{1,0:T(8,128)S(1)}, f32[64,384]{1,0:T(8,128)S(1)}, u32[]{:S(2)}, u32[]{:S(2)}) collective-permute-start(f32[64,384]{1,0:T(8,128)S(1)} %get-tuple-element.57), channel_id=1, source_target_pairs={{0,8},{8,16},{16,24},{24,0},{1,9},{9,17},{17,25},{25,1},{2,10},{10... | collective-permute-start | bytes 294920 | tf_op jit(solution)/shard_map/ppermute | solution.py:373
  19.8 0.9 %second.5 = (f32[4,128,128]{2,1,0:T(8,128)S(1)}, f32[4,128,128]{2,1,0:T(8,128)S(1)}, f32[64,256]{1,0:T(8,128)S(1)}) custom-call(f32[4,128,128]{2,1,0:T(8,128)S(1)} %get-tuple-element.40.ab_ref.refs_0_, f32[16,128,128]{2,1,0:T(8,128)S(1)} %get-tuple-element.32.mu_ref.refs_1_, f32[16,128,128]{2,1,0:T(8,128)S(1)} %get-tuple-element.41.refs_2_, ...), custom_call_target="tpu_custom_call" | custom-call | flops 10000000 | bytes 1000000 | tf_op jit(solution)/shard_map/second/pallas_call | solution.py:130
  20.7 1.0 %collective-permute-start.5 = (f32[64,256]{1,0:T(8,128)S(1)}, f32[64,256]{1,0:T(8,128)S(1)}, u32[]{:S(2)}, u32[]{:S(2)}) collective-permute-start(f32[64,256]{1,0:T(8,128)S(1)} %get-tuple-element.54), channel_id=1, source_target_pairs={{0,8},{8,16},{16,24},{24,0},{1,9},{9,17},{17,25},{25,1},{2,10},{10... | collective-permute-start | bytes 196616 | tf_op jit(solution)/shard_map/ppermute | solution.py:373
  21.7 1.0 %join.1 = f32[1,16,128,128]{3,2,1,0:T(8,128)} custom-call(f32[6,128,128]{2,1,0:T(8,128)S(1)} %get-tuple-element.46.first_ref, f32[6,128,128]{2,1,0:T(8,128)S(1)} %get-tuple-element.49.second_ref, f32[4,128,128]{2,1,0:T(8,128)S(1)} %get-tuple-element.53.third_ref), custom_call_target="tpu_custom_call" | custom-call | flops 10000000 | bytes 1000000 | tf_op jit(solution)/shard_map/join/pallas_call | solution.py:130
  22.7 1.3 %collective-permute-done.7.refs_1_ = f32[64,384]{1,0:T(8,128)S(1)} collective-permute-done((f32[64,384]{1,0:T(8,128)S(1)}, f32[64,384]{1,0:T(8,128)S(1)}, u32[]{:S(2)}, u32[]{:S(2)}) %collective-permute-start.7) | collective-permute-done | bytes 98336 | tf_op jit(solution)/shard_map/ppermute | solution.py:373
  24.0 1.4 %last_inner.1.refs_9_ = f32[1,16,128,128]{3,2,1,0:T(8,128)} custom-call(f32[64,384]{1,0:T(8,128)S(1)} %collective-permute-done.6.refs_0_, f32[64,384]{1,0:T(8,128)S(1)} %collective-permute-done.7.refs_1_, f32[64,512]{1,0:T(8,128)S(1)} %collective-permute-done.2.refs_3_.refs_2_.refs_1_, f32[64,384]{1,0:T(8,128)S(1)} %collective-permute-done.3.refs_3_.refs_2_, ...), custom_call_target="tpu_custom_call" | custom-call | flops 10000000 | bytes 1000000 | tf_op jit(solution)/shard_map/last_inner/pallas_call | solution.py:130
  25.4 0.5 %collective-permute-done.5.refs_0_ = f32[64,256]{1,0:T(8,128)S(1)} collective-permute-done((f32[64,256]{1,0:T(8,128)S(1)}, f32[64,256]{1,0:T(8,128)S(1)}, u32[]{:S(2)}, u32[]{:S(2)}) %collective-permute-start.5) | collective-permute-done | bytes 65568 | tf_op jit(solution)/shard_map/ppermute | solution.py:373
  25.9 1.1 %last_outer.1 = f32[1,16,128,128]{3,2,1,0:T(8,128)} custom-call(f32[64,256]{1,0:T(8,128)S(1)} %collective-permute-done.5.refs_0_, f32[64,512]{1,0:T(8,128)S(1)} %collective-permute-done.2.refs_3_.refs_2_.refs_1_, f32[64,384]{1,0:T(8,128)S(1)} %collective-permute-done.3.refs_3_.refs_2_, ...), custom_call_target="tpu_custom_call", output_to_operand_aliasing={{}: (9, {})} | custom-call | flops 10000000 | bytes 1000000 | tf_op jit(solution)/shard_map/last_outer/pallas_call | solution.py:130
  (4 shorter events, 0.0 us)
Async XLA Ops:
  1.7 10.0 %collective-permute-start = (f32[3,128,128]{2,1,0:T(8,128)S(1)}, f32[3,128,128]{2,1,0:T(8,128)S(1)}, u32[]{:S(2)}, u32[]{:S(2)}) collective-permute-start(f32[3,128,128]{2,1,0:T(8,128)S(1)} %get-tuple-element.37), channel_id=1, source_target_pairs={{0,1},{1,0},{2,3},{3,2},{4,5},{5,4},{6,7},{7,6},{8,9},{9,8},{10,11... | collective-permute-start | bytes 589832 | tf_op jit(solution)/shard_map/ppermute | solution.py:384
  2.2 9.5 %collective-permute-start.1 = (f32[3,128,128]{2,1,0:T(8,128)S(1)}, f32[3,128,128]{2,1,0:T(8,128)S(1)}, u32[]{:S(2)}, u32[]{:S(2)}) collective-permute-start(f32[3,128,128]{2,1,0:T(8,128)S(1)} %get-tuple-element.30.after), channel_id=1, source_target_pairs={{0,8},{1,2},{2,1},{3,4},{4,3},{5,6},{6,5},{7,15},{8,0},{9,10},{10,... | collective-permute-start | bytes 589832 | tf_op jit(solution)/shard_map/ppermute | solution.py:383
  7.1 7.3 %collective-permute-start.2 = (f32[64,512]{1,0:T(8,128)S(1)}, f32[64,512]{1,0:T(8,128)S(1)}, u32[]{:S(2)}, u32[]{:S(2)}) collective-permute-start(f32[64,512]{1,0:T(8,128)S(1)} %get-tuple-element.42), channel_id=1, source_target_pairs={{0,8},{8,16},{16,24},{24,0},{1,9},{9,17},{17,25},{25,1},{2,10},{10... | collective-permute-start | bytes 393224 | tf_op jit(solution)/shard_map/ppermute | solution.py:373
  7.9 8.7 %collective-permute-start.3 = (f32[64,384]{1,0:T(8,128)S(1)}, f32[64,384]{1,0:T(8,128)S(1)}, u32[]{:S(2)}, u32[]{:S(2)}) collective-permute-start(f32[64,384]{1,0:T(8,128)S(1)} %get-tuple-element.47), channel_id=1, source_target_pairs={{0,8},{8,16},{16,24},{24,0},{1,9},{9,17},{17,25},{25,1},{2,10},{10... | collective-permute-start | bytes 294920 | tf_op jit(solution)/shard_map/ppermute | solution.py:373
  12.3 7.6 %collective-permute-start.4 = (f32[64,256]{1,0:T(8,128)S(1)}, f32[64,256]{1,0:T(8,128)S(1)}, u32[]{:S(2)}, u32[]{:S(2)}) collective-permute-start(f32[64,256]{1,0:T(8,128)S(1)} %get-tuple-element.50), channel_id=1, source_target_pairs={{0,8},{8,16},{16,24},{24,0},{1,9},{9,17},{17,25},{25,1},{2,10},{10... | collective-permute-start | bytes 196616 | tf_op jit(solution)/shard_map/ppermute | solution.py:373
  15.6 7.1 %collective-permute-start.6 = (f32[64,384]{1,0:T(8,128)S(1)}, f32[64,384]{1,0:T(8,128)S(1)}, u32[]{:S(2)}, u32[]{:S(2)}) collective-permute-start(f32[64,384]{1,0:T(8,128)S(1)} %get-tuple-element.56), channel_id=1, source_target_pairs={{0,8},{8,16},{16,24},{24,0},{1,9},{9,17},{17,25},{25,1},{2,10},{10... | collective-permute-start | bytes 294920 | tf_op jit(solution)/shard_map/ppermute | solution.py:373
  17.7 6.3 %collective-permute-start.7 = (f32[64,384]{1,0:T(8,128)S(1)}, f32[64,384]{1,0:T(8,128)S(1)}, u32[]{:S(2)}, u32[]{:S(2)}) collective-permute-start(f32[64,384]{1,0:T(8,128)S(1)} %get-tuple-element.57), channel_id=1, source_target_pairs={{0,8},{8,16},{16,24},{24,0},{1,9},{9,17},{17,25},{25,1},{2,10},{10... | collective-permute-start | bytes 294920 | tf_op jit(solution)/shard_map/ppermute | solution.py:373
  20.7 5.2 %collective-permute-start.5 = (f32[64,256]{1,0:T(8,128)S(1)}, f32[64,256]{1,0:T(8,128)S(1)}, u32[]{:S(2)}, u32[]{:S(2)}) collective-permute-start(f32[64,256]{1,0:T(8,128)S(1)} %get-tuple-element.54), channel_id=1, source_target_pairs={{0,8},{8,16},{16,24},{24,0},{1,9},{9,17},{17,25},{25,1},{2,10},{10... | collective-permute-start | bytes 196616 | tf_op jit(solution)/shard_map/ppermute | solution.py:373

commit v4 on v3

v4 whole, which is shorter than its diff:
```python
import functools
import math

import jax
import jax.numpy as jnp
import numpy as np
from jax import lax
from jax.experimental import pallas as pl
from jax.experimental.pallas import tpu as pltpu
from jax.sharding import PartitionSpec as P

KY = 64
KZ = 64
time_step = 0.05
F32 = jnp.float32
BF16 = jnp.bfloat16
VMEM_LIMIT = 24 * 2**20
COST = 10**8
ANY = pl.BlockSpec(memory_space=pl.ANY)
VMEM = pl.BlockSpec(memory_space=pltpu.VMEM)


def CUTS(last):
    return [last - 2]


def basis_value(node_times, source, point):
    total = 1.0
    for other in range(5):
        if other != source:
            total = total * (point - node_times[other]) / (node_times[source] - node_times[other])
    return total


def lobatto():
    root = math.sqrt(3.0 / 7.0)
    node_times = [0.0, (1.0 - root) / 2.0, 0.5, (1.0 + root) / 2.0, 1.0]
    gauss_points = [-math.sqrt(0.6), 0.0, math.sqrt(0.6)]
    gauss_weights = [5.0 / 9.0, 8.0 / 9.0, 5.0 / 9.0]
    last_row = []
    for source in range(5):
        integral = 0.0
        for point, weight in zip(gauss_points, gauss_weights):
            integral += 0.5 * weight * basis_value(node_times, source, 0.5 * (1.0 + point))
        last_row.append(integral)
    return node_times, last_row


NODE_TIMES, LAST_ROW = lobatto()
W = [sum(LAST_ROW[j] * NODE_TIMES[j] ** k for j in range(1, 5)) for k in range(4)]


def dct_rows(count, kept):
    freq = np.arange(kept, dtype=np.float64)[:, None]
    place = np.arange(count, dtype=np.float64)[None, :]
    matrix = np.cos(np.pi * (place + 0.5) * freq / count) * np.sqrt(2.0 / count)
    return np.where(freq == 0, matrix * np.sqrt(0.5), matrix)


def halves(matrix):
    high = matrix.astype(jnp.bfloat16)
    low = (matrix - high.astype(np.float64)).astype(jnp.bfloat16)
    return high, low


def tables(ny, nz):
    cy = dct_rows(ny, KY)
    cz = dct_rows(nz, KZ)
    twice = np.zeros((2 * nz, 2 * KZ))
    twice[:nz, :KZ] = cz.T
    twice[nz:, KZ:] = cz.T
    zh, zl = halves(twice)
    fz = np.concatenate([zh, zh, zl], axis=0)
    yh, yl = halves(cy)
    fy = np.concatenate([yh, yh, yl], axis=1)
    by = np.concatenate([yh.T, yh.T, yl.T], axis=1)
    bz = np.concatenate([zh.T, zh.T, zl.T], axis=0)
    return fz, fy, by, bz


def split(x):
    high = x.astype(BF16)
    return high, (x - high.astype(F32)).astype(BF16)


def dot(a, b):
    return jnp.dot(a, b, preferred_element_type=F32)


def neighbours(v):
    ny, nz = v.shape
    rows = lax.broadcasted_iota(jnp.int32, v.shape, 0)
    lanes = lax.broadcasted_iota(jnp.int32, v.shape, 1)
    total = jnp.where(rows == 0, 0.0, pltpu.roll(v, 1, 0))
    total = total + jnp.where(rows == ny - 1, 0.0, pltpu.roll(v, ny - 1, 0))
    total = total + jnp.where(lanes == 0, 0.0, pltpu.roll(v, 1, 1))
    return total + jnp.where(lanes == nz - 1, 0.0, pltpu.roll(v, nz - 1, 1))


def rate(below, v, above, mobility):
    return mobility * (neighbours(v) + (below + above) - v * (5.0 + v * v))


def analyse(pairs, fz_ref, fy_ref):
    rows = []
    for first, second in pairs:
        first_high, first_low = split(first)
        second_high, second_low = split(second)
        rows.append(
            jnp.concatenate([first_high, second_high, first_low, second_low, first_high, second_high], axis=1)
        )
    half = dot(jnp.concatenate(rows, axis=0), fz_ref[...])
    ny = pairs[0][0].shape[0]
    columns = []
    for i in range(len(pairs)):
        high, low = split(half[i * ny : (i + 1) * ny])
        columns.append(jnp.concatenate([high, low, high], axis=0))
    return dot(fy_ref[...], jnp.concatenate(columns, axis=1))


def synthesise(coeffs, by_ref, bz_ref):
    high, low = split(coeffs)
    half = dot(by_ref[...], jnp.concatenate([high, low, high], axis=0))
    width = 2 * KZ
    count = coeffs.shape[1] // width
    rows = []
    for i in range(count):
        high, low = split(half[:, i * width : (i + 1) * width])
        rows.append(jnp.concatenate([high, low, high], axis=1))
    planes = dot(jnp.concatenate(rows, axis=0), bz_ref[...])
    ny = half.shape[0]
    return [planes[i * ny : (i + 1) * ny] for i in range(count)]


def call(kernel, outs, name, scratch=(), specs=None, out_specs=None, aliases={}, cost=COST):
    def run(*args):
        return pl.pallas_call(
            kernel,
            out_shape=outs,
            in_specs=specs or [VMEM] * len(args),
            out_specs=out_specs or jax.tree.map(lambda _: VMEM, outs),
            scratch_shapes=scratch,
            input_output_aliases=aliases,
            compiler_params=pltpu.CompilerParams(vmem_limit_bytes=VMEM_LIMIT),
            cost_estimate=pl.CostEstimate(flops=100 * cost, bytes_accessed=10 * cost, transcendentals=0),
            name=name,
        )(*args)

    return run


def chunks(nx):
    last = nx // 2
    cuts = [1, *CUTS(last)]
    first = [list(range(cuts[i], cuts[i + 1])) for i in range(len(cuts) - 1)]
    second = [list(range(cuts[i] - (i > 0), cuts[i + 1] - 1)) for i in range(len(cuts) - 1)]
    first.append([0, *range(cuts[-1], last), last])
    second.append([0, *range(cuts[-1] - 1, last - 1), last - 1])
    return first, second


def planes_of(pairs, shift):
    return [2 * t + shift + k for t in pairs for k in (0, 1)]


def outer_planes(nx):
    return [-1, 0, nx - 1, nx]


def reader(*parts):
    where = {}
    for ref, planes in parts:
        for i, p in enumerate(planes):
            where[p] = (ref, i)

    def read(p):
        ref, i = where[p]
        return ref[i]

    return read


def by_pairs(planes):
    return list(zip(planes[::2], planes[1::2]))


def is_even():
    return lax.rem(lax.axis_index("gx"), 2) == 0


def fetch_kernel(a_in, mu_in, *refs):
    table_ins, (even_ref, odd_ref, a_ref, mu_ref), table_refs, sems = refs[:4], refs[4:8], refs[8:12], refs[12]
    nx = a_ref.shape[0]
    even = is_even()
    moves = []
    for out, is_tail in ((odd_ref, jnp.logical_not(even)), (even_ref, even)):
        moves.append((a_in.at[pl.ds(jnp.where(is_tail, nx - 2, 0), 2)], out.at[pl.ds(0, 2)]))
        moves.append((mu_in.at[pl.ds(jnp.where(is_tail, nx - 1, 0), 1)], out.at[pl.ds(2, 1)]))
    for start in range(0, nx, 4):
        moves.append((a_in.at[pl.ds(start, 4)], a_ref.at[pl.ds(start, 4)]))
        moves.append((mu_in.at[pl.ds(start, 4)], mu_ref.at[pl.ds(start, 4)]))
    moves += zip(table_ins, table_refs)
    copies = [pltpu.make_async_copy(s, t, sems.at[i]) for i, (s, t) in enumerate(moves)]
    for copy in copies:
        copy.start()
    for copy in copies:
        copy.wait()


def inner_kernel(stage, a_ref, mu_ref, fz_ref, fy_ref, g_ref, c_ref):
    ends = []
    for i, p in enumerate(planes_of(chunks(a_ref.shape[0])[0][stage], -1)):
        g = rate(a_ref[p - 1], a_ref[p], a_ref[p + 1], mu_ref[p])
        g_ref[i] = g
        ends.append(a_ref[p] + time_step * g)
    c_ref[...] = analyse(by_pairs(ends), fz_ref, fy_ref)


def later_part(below, g, above, a, mobility):
    h = time_step
    laplace = neighbours(g) + (below + above) - 5.0 * g
    hg = h * g
    cube = hg * (3.0 * W[1] * a * a + hg * (3.0 * W[2] * a + W[3] * hg))
    return h * (W[0] * g + mobility * (h * W[1] * laplace - cube))


def middle_kernel(a_ref, mu_ref, fz_ref, fy_ref, *refs):
    nx = a_ref.shape[0]
    first = chunks(nx)[0]
    early = [planes_of(part, -1) for part in first[:-1]]
    g_refs, (g_ref, acc_ref), own_refs = refs[: len(early)], refs[len(early) : len(early) + 2], refs[len(early) + 2 :]
    rest = planes_of(first[-1][1:-1], -1)
    for i, p in enumerate(rest):
        g_ref[i] = rate(a_ref[p - 1], a_ref[p], a_ref[p + 1], mu_ref[p])
    rates = reader(*zip(g_refs, early), (g_ref, rest))
    inner = sum(first[:-1], []) + first[-1][1:-1]
    coeffs = analyse([(a_ref[p - 1], a_ref[p]) for p in planes_of(inner, -1)[1::2]], fz_ref, fy_ref)
    start = 0
    for ref in own_refs:
        ref[...] = coeffs[:, start : start + ref.shape[1]]
        start += ref.shape[1]
    for p in range(2, nx - 2):
        acc_ref[p - 2] = later_part(rates(p - 1), rates(p), rates(p + 1), a_ref[p], mu_ref[p])


def outer_kernel(a_ref, mu_ref, even_ref, odd_ref, g_ref, fz_ref, fy_ref, after, a_out, g_out, c_ref):
    nx = a_ref.shape[0]
    even = is_even()
    place = lax.axis_index("gx")
    count = lax.axis_size("gx")
    keep_low = (place > 0).astype(F32)
    keep_high = (place < count - 1).astype(F32)
    low = [jnp.where(even, odd_ref[i], even_ref[i]) * keep_low for i in range(3)]
    high = [jnp.where(even, even_ref[i], odd_ref[i]) * keep_high for i in range(3)]
    starts = [low[0], low[1], a_ref[0], a_ref[1]]
    ends = [a_ref[nx - 2], a_ref[nx - 1], high[0], high[1]]
    values = starts[1:3] + ends[1:3]
    rates = [
        rate(starts[0], starts[1], starts[2], low[2]),
        rate(starts[1], starts[2], starts[3], mu_ref[0]),
        rate(ends[0], ends[1], ends[2], mu_ref[nx - 1]),
        rate(ends[1], ends[2], ends[3], high[2]),
    ]
    for i in range(4):
        a_out[i] = values[i]
        g_out[i] = rates[i]
    outer = [v + time_step * g for v, g in zip(values, rates)]
    rest = planes_of(chunks(nx)[0][-1][1:-1], -1)
    inner = [a_ref[p] + time_step * g_ref[i] for i, p in enumerate(rest)]
    c_ref[...] = analyse(by_pairs(outer[:2] + inner + outer[2:]), fz_ref, fy_ref)


def later_kernel(a_ref, mu_ref, ab_ref, gb_ref, low_ref, high_ref, rest_ref, fz_ref, fy_ref, acc_ref, c_ref):
    nx = a_ref.shape[0]
    first = chunks(nx)[0]
    rates = reader(
        (gb_ref, outer_planes(nx)), (low_ref, planes_of(first[0], -1)), (high_ref, planes_of(first[-1][1:-1], -1))
    )
    own = analyse([(ab_ref[0], ab_ref[1]), (ab_ref[2], ab_ref[3])], fz_ref, fy_ref)
    width = 2 * KZ
    c_ref[:, :width] = own[:, :width]
    c_ref[:, width : c_ref.shape[1] - width] = rest_ref[...]
    c_ref[:, c_ref.shape[1] - width :] = own[:, width:]
    for i, p in enumerate((0, 1, nx - 2, nx - 1)):
        acc_ref[i] = later_part(rates(p - 1), rates(p), rates(p + 1), a_ref[p], mu_ref[p])


def received(c, own):
    return jnp.where(lax.axis_index("tm") > 0, c - own, 0.0)


def second_kernel(stage, *refs):
    a_ref, ab_ref, mu_ref, acc_ref, accb_ref, c1_ref, own_ref, fz_ref, fy_ref, by_ref, bz_ref = refs[:11]
    earlier, (a1_ref, e_ref, c2_ref) = refs[11:-3], refs[-3:]
    nx, ny, nz = mu_ref.shape
    first, second = chunks(nx)
    change = synthesise(received(c1_ref[...], own_ref[...]), by_ref, bz_ref)
    before = reader((a_ref, range(nx)), (ab_ref, outer_planes(nx)))
    for i, p in enumerate(planes_of(first[stage], -1)):
        a1_ref[i] = before(p) + change[i // 2][:, (i % 2) * nz : (i % 2 + 1) * nz]
    values = reader(*[(ref, planes_of(part, -1)) for ref, part in zip((*earlier, a1_ref), first)])
    parts = reader((acc_ref, range(2, nx - 2)), (accb_ref, (0, 1, nx - 2, nx - 1)))
    ends = []
    for i, p in enumerate(planes_of(second[stage], 0)):
        v = values(p)
        e = v + time_step * LAST_ROW[0] * rate(values(p - 1), v, values(p + 1), mu_ref[p]) + parts(p)
        e_ref[i] = e
        ends.append(e)
    c2_ref[...] = analyse(by_pairs(ends), fz_ref, fy_ref)


def last_kernel(stage, count, *refs):
    c2_ref, by_ref, bz_ref = refs[:3]
    c1_refs, a1_refs = refs[3 : 3 + count], refs[3 + count : 3 + 2 * count]
    out_ref, buffer, sems = refs[-3:]
    nx, ny, nz = out_ref.shape[1:]
    first, second = chunks(nx)
    where = {}
    for ref, part in zip(c1_refs, first):
        for i, p in enumerate(planes_of(part, -1)):
            where[p] = (ref, i)

    def column(p):
        ref, i = where[p]
        return ref[:, i * KZ : (i + 1) * KZ]

    values = reader(*[(ref, planes_of(part, -1)) for ref, part in zip(a1_refs, first)])
    planes = planes_of(second[stage], 0)
    before = jnp.concatenate([column(p) for p in planes], axis=1)
    change = synthesise(received(c2_ref[...], before), by_ref, bz_ref)
    copies = []
    for i in range(0, len(planes), 2):
        for k in (0, 1):
            buffer[i + k] = values(planes[i + k]) + change[i // 2][:, k * nz : (k + 1) * nz]
        copy = pltpu.make_async_copy(buffer.at[pl.ds(i, 2)], out_ref.at[0, pl.ds(planes[i], 2)], sems.at[i // 2])
        copy.start()
        copies.append(copy)
    for copy in copies:
        copy.wait()


def join_kernel(*refs):
    parts, out_ref, sems = refs[:-2], refs[-2], refs[-1]
    copies = []
    for ref, part in zip(parts, chunks(out_ref.shape[1])[1]):
        for i, p in enumerate(planes_of(part, 0)[::2]):
            copies.append(
                pltpu.make_async_copy(ref.at[pl.ds(2 * i, 2)], out_ref.at[0, pl.ds(p, 2)], sems.at[len(copies)])
            )
    for copy in copies:
        copy.start()
    for copy in copies:
        copy.wait()


def body(start_states, mobility):
    nx, ny, nz = mobility.shape
    slices, slabs = lax.axis_size("tm"), lax.axis_size("gx")
    inputs = [start_states[0], mobility, *map(jnp.asarray, tables(ny, nz))]
    inputs = [pltpu.with_memory_space_constraint(x, pltpu.HBM) for x in inputs]
    first, second = chunks(nx)
    count = len(first)

    def grid(planes):
        return jax.ShapeDtypeStruct((planes, ny, nz), F32)

    def modes(pairs):
        return jax.ShapeDtypeStruct((KY, len(pairs) * 2 * KZ), F32)

    even_pairs = [(s * slabs + g, s * slabs + (g ^ 1)) for s in range(slices) for g in range(slabs)]
    odd_pairs = []
    for s in range(slices):
        for g in range(slabs):
            other = g + 1 if g % 2 else g - 1
            if 0 <= other < slabs:
                odd_pairs.append((s * slabs + g, s * slabs + other))
            else:
                odd_pairs.append((s * slabs + g, (s ^ 1) * slabs + g))
    ring = [(s, (s + 1) % slices) for s in range(slices)]

    def onward(c):
        return lax.ppermute(c, "tm", ring)

    to_even, to_odd, a, mu, fz, fy, by, bz = call(
        fetch_kernel,
        [grid(3), grid(3), grid(nx), grid(nx), *[jax.ShapeDtypeStruct(t.shape, t.dtype) for t in inputs[2:]]],
        "fetch",
        scratch=[pltpu.SemaphoreType.DMA((8 + nx // 2,))],
        specs=[ANY] * 6,
    )(*inputs)
    from_odd = lax.ppermute(to_odd, ("tm", "gx"), odd_pairs)
    from_even = lax.ppermute(to_even, ("tm", "gx"), even_pairs)
    g, c1 = [], []
    for stage, part in enumerate(first[:-1]):
        rates, c = call(functools.partial(inner_kernel, stage), [grid(2 * len(part)), modes(part)], "inner")(
            a, mu, fz, fy
        )
        g.append(rates)
        c1.append(onward(c))
    rest = first[-1][1:-1]
    g_rest, acc, *own, own_rest = call(
        middle_kernel,
        [grid(2 * len(rest)), grid(nx - 4), *[modes(part) for part in first[:-1]], modes(rest)],
        "middle",
        cost=0,
    )(a, mu, fz, fy, *g)
    ab, gb, c = call(outer_kernel, [grid(4), grid(4), modes(first[-1])], "outer", specs=[VMEM] * 7 + [ANY])(
        a, mu, from_even, from_odd, g_rest, fz, fy, acc
    )
    c1.append(onward(c))
    accb, own_last = call(later_kernel, [grid(4), modes(first[-1])], "later")(
        a, mu, ab, gb, g[0], g_rest, own_rest, fz, fy
    )
    own.append(own_last)
    a1, e, c2 = [], [], []
    for stage in range(count):
        values, end, c = call(
            functools.partial(second_kernel, stage),
            [grid(2 * len(first[stage])), grid(2 * len(second[stage])), modes(second[stage])],
            "second",
        )(a, ab, mu, acc, accb, c1[stage], own[stage], fz, fy, by, bz, *a1)
        a1.append(values)
        e.append(end)
        c2.append(onward(c))
    whole = jax.ShapeDtypeStruct((1, nx, ny, nz), F32)
    end_state = call(
        join_kernel,
        whole,
        "join",
        scratch=[pltpu.SemaphoreType.DMA((nx // 2,))],
        specs=[ANY] * count,
        out_specs=ANY,
    )(*e)
    result = []
    for stage, part in enumerate(second):
        result = [
            call(
                functools.partial(last_kernel, stage, count),
                whole,
                "last",
                scratch=[pltpu.VMEM((2 * len(part), ny, nz), F32), pltpu.SemaphoreType.DMA((len(part),))],
                specs=[VMEM] * (3 + 2 * count) + [ANY] * len(result),
                out_specs=ANY,
                aliases={3 + 2 * count: 0} if result else {},
            )(c2[stage], by, bz, *c1, *a1, *result)
        ]
    return end_state, result[0]


def solution(mesh):
    placed = (P("tm", "gx", None, None), P("gx", None, None))
    return jax.shard_map(
        body,
        mesh=mesh,
        in_specs=placed,
        out_specs=(P("tm", "gx", None, None), P("tm", "gx", None, None)),
        check_vma=False,
    )
```

time: 27.2 us -> 26.1 us (0.960)
  waiting for transfers between devices: 2.31 us -> 6.54 us
  starting transfers between devices: 10.8 us -> 7.21 us
  Pallas kernels: 13.2 us -> 11.5 us
    ppermute x6 -> x4, starting transfers between devices: 7.75 us -> 4.13 us  [onward(): return lax.ppermute(c, 'tm', ring)]
    ppermute x6 -> x4, waiting for transfers between devices: 2.31 us -> 5.09 us  [onward(): return lax.ppermute(c, 'tm', ring)]
    pallas_call x12 -> x10, Pallas kernels: 13.2 us -> 11.5 us  [run(): pl.pallas_call(kernel, out_shape=outs, in_specs=specs or [VMEM] * len(arg...]
    ppermute x1, waiting for transfers between devices: 0.01 us -> 1.45 us  [body(): from_odd = lax.ppermute(to_odd, ('tm', 'gx'), odd_pairs)]
  transfers between devices with their start and end apart: 8 -> 6, of which waited for: 3 -> 5; matrix products, arithmetic and copies ran while one was open for 0% -> 0% of each run, Pallas kernels for 41% -> 32%
where the time goes in v4:
time: 26.1 us; the launch traced here: 25.9 us
  Pallas kernels  11.5 us (44%)
  starting transfers between devices  7.21 us (28%)
  waiting for transfers between devices  6.54 us (25%)
  between operations  0.71 us (3%)
    pallas_call x10, Pallas kernels, run(): pl.pallas_call(kernel, out_shape=outs, in_specs=specs or [VMEM] * len(arg...  11.5 us
    ppermute x4, waiting for transfers between devices, onward(): return lax.ppermute(c, 'tm', ring)  5.09 us
    ppermute x4, starting transfers between devices, onward(): return lax.ppermute(c, 'tm', ring)  4.13 us
    ppermute x1, starting transfers between devices, body(): from_odd = lax.ppermute(to_odd, ('tm', 'gx'), odd_pairs)  2.56 us
    ppermute x1, waiting for transfers between devices, body(): from_odd = lax.ppermute(to_odd, ('tm', 'gx'), odd_pairs)  1.45 us
  transfers between devices with their start and end apart: 6, of which 5 were waited for; matrix products, arithmetic and copies ran while one was open for 0% of the time, Pallas kernels for 32%

profile of v4, /device:TPU:0, one launch (start us, length us, event | category | flops | bytes accessed | tf_op | source)
XLA Modules:
  0.0 25.9 jit_solution(17635718450593594076)
XLA Ops:
  0.6 2.0 %fetch.1 = (f32[3,128,128]{2,1,0:T(8,128)S(1)}, f32[3,128,128]{2,1,0:T(8,128)S(1)}, f32[16,128,128]{2,1,0:T(8,128)S(1)}, f32[16,128,128]{2,1,0:T(8,128)S(1)}, bf...) custom-call(f32[16,128,128]{2,1,0:T(8,128)} %bitcast.1, ...), custom_call_target="tpu_custom_call" | custom-call | flops 10000000000 | bytes 1000000000 | tf_op jit(solution)/shard_map/fetch/pallas_call | solution.py:137
  2.6 0.5 %collective-permute-start = (f32[3,128,128]{2,1,0:T(8,128)S(1)}, f32[3,128,128]{2,1,0:T(8,128)S(1)}, u32[]{:S(2)}, u32[]{:S(2)}) collective-permute-start(f32[3,128,128]{2,1,0:T(8,128)S(1)} %get-tuple-element.29), channel_id=1, source_target_pairs={{0,1},{1,0},{2,3},{3,2},{4,5},{5,4},{6,7},{7,6},{8,9},{9,8},{10,11... | collective-permute-start | bytes 589832 | tf_op jit(solution)/shard_map/ppermute | solution.py:392
  3.2 2.6 %collective-permute-start.1 = (f32[3,128,128]{2,1,0:T(8,128)S(1)}, f32[3,128,128]{2,1,0:T(8,128)S(1)}, u32[]{:S(2)}, u32[]{:S(2)}) collective-permute-start(f32[3,128,128]{2,1,0:T(8,128)S(1)} %get-tuple-element.30), channel_id=1, source_target_pairs={{0,8},{1,2},{2,1},{3,4},{4,3},{5,6},{6,5},{7,15},{8,0},{9,10},{10,... | collective-permute-start | bytes 589832 | tf_op jit(solution)/shard_map/ppermute | solution.py:391
  5.7 0.9 %inner.1 = (f32[10,128,128]{2,1,0:T(8,128)S(1)}, f32[64,640]{1,0:T(8,128)S(1)}) custom-call(f32[16,128,128]{2,1,0:T(8,128)S(1)} %get-tuple-element.27.a_ref.refs_0_, f32[16,128,128]{2,1,0:T(8,128)S(1)} %get-tuple-element.28.mu_ref.refs_2_, bf16[768,128]{1,0:T(8,128)(2,1)S(1)} %get-tuple-element.31.fz_ref.refs_7_, ...), custom_call_target="tpu_custom_call" | custom-call | flops 10000000000 | bytes 1000000000 | tf_op jit(solution)/shard_map/inner/pallas_call | solution.py:137
  6.7 0.1 collective-permute-start.2
  6.8 1.2 %middle.1 = (f32[4,128,128]{2,1,0:T(8,128)S(1)}, f32[12,128,128]{2,1,0:T(8,128)S(1)}, f32[64,640]{1,0:T(8,128)S(1)}, f32[64,256]{1,0:T(8,128)S(1)}) custom-call(f32[16,128,128]{2,1,0:T(8,128)S(1)} %get-tuple-element.27.a_ref.refs_0_, f32[16,128,128]{2,1,0:T(8,128)S(1)} %get-tuple-element.28.mu_ref.refs_2_, ...), custom_call_target="tpu_custom_call" | custom-call | tf_op jit(solution)/shard_map/middle/pallas_call | solution.py:137
  7.9 0.0 collective-permute-done.even_ref
  7.9 1.5 %collective-permute-done.1.odd_ref = f32[3,128,128]{2,1,0:T(8,128)S(1)} collective-permute-done((f32[3,128,128]{2,1,0:T(8,128)S(1)}, f32[3,128,128]{2,1,0:T(8,128)S(1)}, u32[]{:S(2)}, u32[]{:S(2)}) %collective-permute-start.1) | collective-permute-done | bytes 196640 | tf_op jit(solution)/shard_map/ppermute | solution.py:391
  9.4 0.7 %outer.1 = (f32[4,128,128]{2,1,0:T(8,128)S(1)}, f32[4,128,128]{2,1,0:T(8,128)S(1)}, f32[64,512]{1,0:T(8,128)S(1)}) custom-call(f32[16,128,128]{2,1,0:T(8,128)S(1)} %get-tuple-element.27.a_ref.refs_0_, f32[16,128,128]{2,1,0:T(8,128)S(1)} %get-tuple-element.28.mu_ref.refs_2_, f32[3,128,128]{2,1,0:T(8,128)S(1)} %collective-permute-done.even_ref, ...), custom_call_target="tpu_custom_call" | custom-call | flops 10000000000 | bytes 1000000000 | tf_op jit(solution)/shard_map/outer/pallas_call | solution.py:137
  10.1 2.4 %collective-permute-start.3 = (f32[64,512]{1,0:T(8,128)S(1)}, f32[64,512]{1,0:T(8,128)S(1)}, u32[]{:S(2)}, u32[]{:S(2)}) collective-permute-start(f32[64,512]{1,0:T(8,128)S(1)} %get-tuple-element.45), channel_id=1, source_target_pairs={{0,8},{8,16},{16,24},{24,0},{1,9},{9,17},{17,25},{25,1},{2,10},{10... | collective-permute-start | bytes 393224 | tf_op jit(solution)/shard_map/ppermute | solution.py:382
  12.5 0.5 %later.1 = (f32[4,128,128]{2,1,0:T(8,128)S(1)}, f32[64,512]{1,0:T(8,128)S(1)}) custom-call(f32[16,128,128]{2,1,0:T(8,128)S(1)} %get-tuple-element.27.a_ref.refs_0_, f32[16,128,128]{2,1,0:T(8,128)S(1)} %get-tuple-element.28.mu_ref.refs_2_, f32[4,128,128]{2,1,0:T(8,128)S(1)} %get-tuple-element.36.ab_ref.refs_1_, f32[4,128,128]{2,1,0:T(8,128)S(1)} %get-tuple-element.37.gb_ref, ...), custom_call_target="tpu_custom_call" | custom-call | flops 10000000000 | bytes 1000000000 | tf_op jit(solution)/shard_map/later/pallas_call | solution.py:137
  13.0 1.6 %collective-permute-done.2.refs_5_.refs_3_ = f32[64,640]{1,0:T(8,128)S(1)} collective-permute-done((f32[64,640]{1,0:T(8,128)S(1)}, f32[64,640]{1,0:T(8,128)S(1)}, u32[]{:S(2)}, u32[]{:S(2)}) %collective-permute-start.2) | collective-permute-done | bytes 163872 | tf_op jit(solution)/shard_map/ppermute | solution.py:382
  14.6 1.4 %second.2 = (f32[10,128,128]{2,1,0:T(8,128)S(1)}, f32[8,128,128]{2,1,0:T(8,128)S(1)}, f32[64,512]{1,0:T(8,128)S(1)}) custom-call(f32[16,128,128]{2,1,0:T(8,128)S(1)} %get-tuple-element.27.a_ref.refs_0_, f32[4,128,128]{2,1,0:T(8,128)S(1)} %get-tuple-element.36.ab_ref.refs_1_, f32[16,128,128]{2,1,0:T(8,128)S(1)} %get-tuple-element.28.mu_ref.refs_2_, ...), custom_call_target="tpu_custom_call" | custom-call | flops 10000000000 | bytes 1000000000 | tf_op jit(solution)/shard_map/second/pallas_call | solution.py:137
  16.0 0.4 %collective-permute-start.5 = (f32[64,512]{1,0:T(8,128)S(1)}, f32[64,512]{1,0:T(8,128)S(1)}, u32[]{:S(2)}, u32[]{:S(2)}) collective-permute-start(f32[64,512]{1,0:T(8,128)S(1)} %get-tuple-element.51), channel_id=1, source_target_pairs={{0,8},{8,16},{16,24},{24,0},{1,9},{9,17},{17,25},{25,1},{2,10},{10... | collective-permute-start | bytes 393224 | tf_op jit(solution)/shard_map/ppermute | solution.py:382
  16.4 0.8 %collective-permute-done.3.refs_5_.refs_4_ = f32[64,512]{1,0:T(8,128)S(1)} collective-permute-done((f32[64,512]{1,0:T(8,128)S(1)}, f32[64,512]{1,0:T(8,128)S(1)}, u32[]{:S(2)}, u32[]{:S(2)}) %collective-permute-start.3) | collective-permute-done | bytes 131104 | tf_op jit(solution)/shard_map/ppermute | solution.py:382
  17.2 1.3 %second.3 = (f32[8,128,128]{2,1,0:T(8,128)S(1)}, f32[8,128,128]{2,1,0:T(8,128)S(1)}, f32[64,512]{1,0:T(8,128)S(1)}) custom-call(f32[16,128,128]{2,1,0:T(8,128)S(1)} %get-tuple-element.27.a_ref.refs_0_, f32[4,128,128]{2,1,0:T(8,128)S(1)} %get-tuple-element.36.ab_ref.refs_1_, f32[16,128,128]{2,1,0:T(8,128)S(1)} %get-tuple-element.28.mu_ref.refs_2_, ...), custom_call_target="tpu_custom_call" | custom-call | flops 10000000000 | bytes 1000000000 | tf_op jit(solution)/shard_map/second/pallas_call | solution.py:137
  18.5 1.3 %collective-permute-start.4 = (f32[64,512]{1,0:T(8,128)S(1)}, f32[64,512]{1,0:T(8,128)S(1)}, u32[]{:S(2)}, u32[]{:S(2)}) collective-permute-start(f32[64,512]{1,0:T(8,128)S(1)} %get-tuple-element.49), channel_id=1, source_target_pairs={{0,8},{8,16},{16,24},{24,0},{1,9},{9,17},{17,25},{25,1},{2,10},{10... | collective-permute-start | bytes 393224 | tf_op jit(solution)/shard_map/ppermute | solution.py:382
  19.8 1.0 %join.1 = f32[1,16,128,128]{3,2,1,0:T(8,128)} custom-call(f32[8,128,128]{2,1,0:T(8,128)S(1)} %get-tuple-element.44.refs_0_, f32[8,128,128]{2,1,0:T(8,128)S(1)} %get-tuple-element.48.refs_1_), custom_call_target="tpu_custom_call" | custom-call | flops 10000000000 | bytes 1000000000 | tf_op jit(solution)/shard_map/join/pallas_call | solution.py:137
  20.8 1.4 %collective-permute-done.5.refs_0_ = f32[64,512]{1,0:T(8,128)S(1)} collective-permute-done((f32[64,512]{1,0:T(8,128)S(1)}, f32[64,512]{1,0:T(8,128)S(1)}, u32[]{:S(2)}, u32[]{:S(2)}) %collective-permute-start.5) | collective-permute-done | bytes 131104 | tf_op jit(solution)/shard_map/ppermute | solution.py:382
  22.2 1.2 %last.2.refs_7_ = f32[1,16,128,128]{3,2,1,0:T(8,128)} custom-call(f32[64,512]{1,0:T(8,128)S(1)} %collective-permute-done.5.refs_0_, bf16[128,192]{1,0:T(8,128)(2,1)S(1)} %get-tuple-element.42.refs_9_.refs_1_, bf16[384,256]{1,0:T(8,128)(2,1)S(1)} %get-tuple-element.43.refs_10_.refs_2_, f32[64,640]{1,0:T(8,128)S(1)} %collective-permute-done.2.refs_5_.refs_3_, ...), custom_call_target="tpu_custom_call" | custom-call | flops 10000000000 | bytes 1000000000 | tf_op jit(solution)/shard_map/last/pallas_call | solution.py:137
  23.4 1.3 %collective-permute-done.4.refs_0_ = f32[64,512]{1,0:T(8,128)S(1)} collective-permute-done((f32[64,512]{1,0:T(8,128)S(1)}, f32[64,512]{1,0:T(8,128)S(1)}, u32[]{:S(2)}, u32[]{:S(2)}) %collective-permute-start.4) | collective-permute-done | bytes 131104 | tf_op jit(solution)/shard_map/ppermute | solution.py:382
  24.7 1.2 %last.3 = f32[1,16,128,128]{3,2,1,0:T(8,128)} custom-call(f32[64,512]{1,0:T(8,128)S(1)} %collective-permute-done.4.refs_0_, bf16[128,192]{1,0:T(8,128)(2,1)S(1)} %get-tuple-element.42.refs_9_.refs_1_, bf16[384,256]{1,0:T(8,128)(2,1)S(1)} %get-tuple-element.43.refs_10_.refs_2_, ...), custom_call_target="tpu_custom_call", output_to_operand_aliasing={{}: (7, {})} | custom-call | flops 10000000000 | bytes 1000000000 | tf_op jit(solution)/shard_map/last/pallas_call | solution.py:137
Async XLA Ops:
  2.6 5.3 %collective-permute-start = (f32[3,128,128]{2,1,0:T(8,128)S(1)}, f32[3,128,128]{2,1,0:T(8,128)S(1)}, u32[]{:S(2)}, u32[]{:S(2)}) collective-permute-start(f32[3,128,128]{2,1,0:T(8,128)S(1)} %get-tuple-element.29), channel_id=1, source_target_pairs={{0,1},{1,0},{2,3},{3,2},{4,5},{5,4},{6,7},{7,6},{8,9},{9,8},{10,11... | collective-permute-start | bytes 589832 | tf_op jit(solution)/shard_map/ppermute | solution.py:392
  3.2 6.2 %collective-permute-start.1 = (f32[3,128,128]{2,1,0:T(8,128)S(1)}, f32[3,128,128]{2,1,0:T(8,128)S(1)}, u32[]{:S(2)}, u32[]{:S(2)}) collective-permute-start(f32[3,128,128]{2,1,0:T(8,128)S(1)} %get-tuple-element.30), channel_id=1, source_target_pairs={{0,8},{1,2},{2,1},{3,4},{4,3},{5,6},{6,5},{7,15},{8,0},{9,10},{10,... | collective-permute-start | bytes 589832 | tf_op jit(solution)/shard_map/ppermute | solution.py:391
  6.7 7.9 %collective-permute-start.2 = (f32[64,640]{1,0:T(8,128)S(1)}, f32[64,640]{1,0:T(8,128)S(1)}, u32[]{:S(2)}, u32[]{:S(2)}) collective-permute-start(f32[64,640]{1,0:T(8,128)S(1)} %get-tuple-element.40), channel_id=1, source_target_pairs={{0,8},{8,16},{16,24},{24,0},{1,9},{9,17},{17,25},{25,1},{2,10},{10... | collective-permute-start | bytes 491528 | tf_op jit(solution)/shard_map/ppermute | solution.py:382
  10.1 7.1 %collective-permute-start.3 = (f32[64,512]{1,0:T(8,128)S(1)}, f32[64,512]{1,0:T(8,128)S(1)}, u32[]{:S(2)}, u32[]{:S(2)}) collective-permute-start(f32[64,512]{1,0:T(8,128)S(1)} %get-tuple-element.45), channel_id=1, source_target_pairs={{0,8},{8,16},{16,24},{24,0},{1,9},{9,17},{17,25},{25,1},{2,10},{10... | collective-permute-start | bytes 393224 | tf_op jit(solution)/shard_map/ppermute | solution.py:382
  16.0 6.2 %collective-permute-start.5 = (f32[64,512]{1,0:T(8,128)S(1)}, f32[64,512]{1,0:T(8,128)S(1)}, u32[]{:S(2)}, u32[]{:S(2)}) collective-permute-start(f32[64,512]{1,0:T(8,128)S(1)} %get-tuple-element.51), channel_id=1, source_target_pairs={{0,8},{8,16},{16,24},{24,0},{1,9},{9,17},{17,25},{25,1},{2,10},{10... | collective-permute-start | bytes 393224 | tf_op jit(solution)/shard_map/ppermute | solution.py:382
  18.5 6.2 %collective-permute-start.4 = (f32[64,512]{1,0:T(8,128)S(1)}, f32[64,512]{1,0:T(8,128)S(1)}, u32[]{:S(2)}, u32[]{:S(2)}) collective-permute-start(f32[64,512]{1,0:T(8,128)S(1)} %get-tuple-element.49), channel_id=1, source_target_pairs={{0,8},{8,16},{16,24},{24,0},{1,9},{9,17},{17,25},{25,1},{2,10},{10... | collective-permute-start | bytes 393224 | tf_op jit(solution)/shard_map/ppermute | solution.py:382

commit v5 on v4

--- a/solution.py
+++ b/solution.py
@@ -188,32 +188,32 @@
     return lax.rem(lax.axis_index("gx"), 2) == 0
 
 
-def fetch_kernel(a_in, mu_in, *refs):
-    table_ins, (even_ref, odd_ref, a_ref, mu_ref), table_refs, sems = refs[:4], refs[4:8], refs[8:12], refs[12]
+def pack_kernel(a_ref, mu_ref, odd_ref, sems):
     nx = a_ref.shape[0]
     even = is_even()
-    moves = []
-    for out, is_tail in ((odd_ref, jnp.logical_not(even)), (even_ref, even)):
-        moves.append((a_in.at[pl.ds(jnp.where(is_tail, nx - 2, 0), 2)], out.at[pl.ds(0, 2)]))
-        moves.append((mu_in.at[pl.ds(jnp.where(is_tail, nx - 1, 0), 1)], out.at[pl.ds(2, 1)]))
-    for start in range(0, nx, 4):
-        moves.append((a_in.at[pl.ds(start, 4)], a_ref.at[pl.ds(start, 4)]))
-        moves.append((mu_in.at[pl.ds(start, 4)], mu_ref.at[pl.ds(start, 4)]))
-    moves += zip(table_ins, table_refs)
-    copies = [pltpu.make_async_copy(s, t, sems.at[i]) for i, (s, t) in enumerate(moves)]
+    copies = [
+        pltpu.make_async_copy(a_ref.at[pl.ds(jnp.where(even, 0, nx - 2), 2)], odd_ref.at[pl.ds(0, 2)], sems.at[0]),
+        pltpu.make_async_copy(mu_ref.at[pl.ds(jnp.where(even, 0, nx - 1), 1)], odd_ref.at[pl.ds(2, 1)], sems.at[1]),
+    ]
     for copy in copies:
         copy.start()
     for copy in copies:
         copy.wait()
 
 
-def inner_kernel(stage, a_ref, mu_ref, fz_ref, fy_ref, g_ref, c_ref):
+def inner_kernel(stage, a_ref, mu_ref, fz_ref, fy_ref, after, g_ref, c_ref, *even_ref):
     ends = []
     for i, p in enumerate(planes_of(chunks(a_ref.shape[0])[0][stage], -1)):
         g = rate(a_ref[p - 1], a_ref[p], a_ref[p + 1], mu_ref[p])
         g_ref[i] = g
         ends.append(a_ref[p] + time_step * g)
     c_ref[...] = analyse(by_pairs(ends), fz_ref, fy_ref)
+    if stage == 0:
+        nx = a_ref.shape[0]
+        even = is_even()
+        even_ref[0][0] = jnp.where(even, a_ref[nx - 2], a_ref[0])
+        even_ref[0][1] = jnp.where(even, a_ref[nx - 1], a_ref[1])
+        even_ref[0][2] = jnp.where(even, mu_ref[nx - 1], mu_ref[0])
 
 
 def later_part(below, g, above, a, mobility):
@@ -310,8 +310,8 @@
 
 
 def last_kernel(stage, count, *refs):
-    c2_ref, by_ref, bz_ref = refs[:3]
-    c1_refs, a1_refs = refs[3 : 3 + count], refs[3 + count : 3 + 2 * count]
+    c2_ref, by_ref, bz_ref, a_ref = refs[:4]
+    c1_refs, a1_refs = refs[4 : 4 + count], refs[4 + count : 4 + 2 * count]
     out_ref, buffer, sems = refs[-3:]
     nx, ny, nz = out_ref.shape[1:]
     first, second = chunks(nx)
@@ -324,19 +324,39 @@
         ref, i = where[p]
         return ref[:, i * KZ : (i + 1) * KZ]
 
-    values = reader(*[(ref, planes_of(part, -1)) for ref, part in zip(a1_refs, first)])
-    planes = planes_of(second[stage], 0)
-    before = jnp.concatenate([column(p) for p in planes], axis=1)
-    change = synthesise(received(c2_ref[...], before), by_ref, bz_ref)
-    copies = []
-    for i in range(0, len(planes), 2):
-        for k in (0, 1):
-            buffer[i + k] = values(planes[i + k]) + change[i // 2][:, k * nz : (k + 1) * nz]
-        copy = pltpu.make_async_copy(buffer.at[pl.ds(i, 2)], out_ref.at[0, pl.ds(planes[i], 2)], sems.at[i // 2])
-        copy.start()
-        copies.append(copy)
-    for copy in copies:
-        copy.wait()
+    receives = lax.axis_index("tm") > 0
+
+    @pl.when(receives)
+    def _():
+        values = reader(*[(ref, planes_of(part, -1)) for ref, part in zip(a1_refs, first)])
+        planes = planes_of(second[stage], 0)
+        before = jnp.concatenate([column(p) for p in planes], axis=1)
+        change = synthesise(c2_ref[...] - before, by_ref, bz_ref)
+        copies = []
+        for i in range(0, len(planes), 2):
+            for k in (0, 1):
+                buffer[i + k] = values(planes[i + k]) + change[i // 2][:, k * nz : (k + 1) * nz]
+            copy = pltpu.make_async_copy(
+                buffer.at[pl.ds(i, 2)], out_ref.at[0, pl.ds(planes[i], 2)], sems.at[i // 2]
+            )
+            copy.start()
+            copies.append(copy)
+        for copy in copies:
+            copy.wait()
+
+    if stage == 0:
+
+        @pl.when(jnp.logical_not(receives))
+        def _():
+            half = nx // 2
+            copies = [
+                pltpu.make_async_copy(a_ref.at[pl.ds(i * half, half)], out_ref.at[0, pl.ds(i * half, half)], sems.at[i])
+                for i in range(2)
+            ]
+            for copy in copies:
+                copy.start()
+            for copy in copies:
+                copy.wait()
 
 
 def join_kernel(*refs):
@@ -356,8 +376,8 @@
 def body(start_states, mobility):
     nx, ny, nz = mobility.shape
     slices, slabs = lax.axis_size("tm"), lax.axis_size("gx")
-    inputs = [start_states[0], mobility, *map(jnp.asarray, tables(ny, nz))]
-    inputs = [pltpu.with_memory_space_constraint(x, pltpu.HBM) for x in inputs]
+    a, mu = start_states[0], mobility
+    fz, fy, by, bz = map(jnp.asarray, tables(ny, nz))
     first, second = chunks(nx)
     count = len(first)
 
@@ -375,28 +395,28 @@
             if 0 <= other < slabs:
                 odd_pairs.append((s * slabs + g, s * slabs + other))
             else:
-                odd_pairs.append((s * slabs + g, (s ^ 1) * slabs + g))
+                odd_pairs.append((s * slabs + g, (s ^ 2) * slabs + g))
     ring = [(s, (s + 1) % slices) for s in range(slices)]
 
     def onward(c):
         return lax.ppermute(c, "tm", ring)
 
-    to_even, to_odd, a, mu, fz, fy, by, bz = call(
-        fetch_kernel,
-        [grid(3), grid(3), grid(nx), grid(nx), *[jax.ShapeDtypeStruct(t.shape, t.dtype) for t in inputs[2:]]],
-        "fetch",
-        scratch=[pltpu.SemaphoreType.DMA((8 + nx // 2,))],
-        specs=[ANY] * 6,
-    )(*inputs)
+    to_odd = call(pack_kernel, grid(3), "pack", scratch=[pltpu.SemaphoreType.DMA((2,))], specs=[ANY] * 2)(
+        *[pltpu.with_memory_space_constraint(x, pltpu.HBM) for x in (a, mu)]
+    )
     from_odd = lax.ppermute(to_odd, ("tm", "gx"), odd_pairs)
-    from_even = lax.ppermute(to_even, ("tm", "gx"), even_pairs)
     g, c1 = [], []
     for stage, part in enumerate(first[:-1]):
-        rates, c = call(functools.partial(inner_kernel, stage), [grid(2 * len(part)), modes(part)], "inner")(
-            a, mu, fz, fy
-        )
+        rates, c, *to_even = call(
+            functools.partial(inner_kernel, stage),
+            [grid(2 * len(part)), modes(part)] + [grid(3)] * (stage == 0),
+            "inner",
+            specs=[VMEM] * 4 + [ANY],
+        )(a, mu, fz, fy, to_odd)
         g.append(rates)
         c1.append(onward(c))
+        if stage == 0:
+            from_even = lax.ppermute(to_even[0], ("tm", "gx"), even_pairs)
     rest = first[-1][1:-1]
     g_rest, acc, *own, own_rest = call(
         middle_kernel,
@@ -439,10 +459,10 @@
                 whole,
                 "last",
                 scratch=[pltpu.VMEM((2 * len(part), ny, nz), F32), pltpu.SemaphoreType.DMA((len(part),))],
-                specs=[VMEM] * (3 + 2 * count) + [ANY] * len(result),
+                specs=[VMEM] * (4 + 2 * count) + [ANY] * len(result),
                 out_specs=ANY,
-                aliases={3 + 2 * count: 0} if result else {},
-            )(c2[stage], by, bz, *c1, *a1, *result)
+                aliases={4 + 2 * count: 0} if result else {},
+            )(c2[stage], by, bz, a, *c1, *a1, *result)
         ]
     return end_state, result[0]
 

time: 26.1 us -> 24 us (0.920)
  Pallas kernels: 11.5 us -> 9.14 us
  starting transfers between devices: 7.21 us -> 8.9 us
  waiting for transfers between devices: 6.54 us -> 4.99 us
    pallas_call x10, Pallas kernels: 11.5 us -> 9.14 us  [run(): pl.pallas_call(kernel, out_shape=outs, in_specs=specs or [VMEM] * len(arg...]
    ppermute x4, starting transfers between devices: 4.13 us -> 5.63 us  [onward(): return lax.ppermute(c, 'tm', ring)]
    ppermute x1, waiting for transfers between devices: 1.45 us -> 0.01 us  [body(): from_odd = lax.ppermute(to_odd, ('tm', 'gx'), odd_pairs)]
    ppermute x1, starting transfers between devices: 2.56 us -> 3.03 us  [body(): from_odd = lax.ppermute(to_odd, ('tm', 'gx'), odd_pairs)]
    ppermute x1, starting transfers between devices: 0.52 us -> 0.24 us  [body(): from_even = lax.ppermute(to_even[0], ('tm', 'gx'), even_pairs)]
  transfers between devices with their start and end apart: 6 -> 6, of which waited for: 5 -> 4; matrix products, arithmetic and copies ran while one was open for 0% -> 0% of each run, Pallas kernels for 32% -> 34%
where the time goes in v5:
time: 24 us; the launch traced here: 23.8 us
  Pallas kernels  9.14 us (38%)
  starting transfers between devices  8.9 us (37%)
  waiting for transfers between devices  4.99 us (21%)
  between operations  0.75 us (3%)
    pallas_call x10, Pallas kernels, run(): pl.pallas_call(kernel, out_shape=outs, in_specs=specs or [VMEM] * len(arg...  9.14 us
    ppermute x4, starting transfers between devices, onward(): return lax.ppermute(c, 'tm', ring)  5.63 us
    ppermute x4, waiting for transfers between devices, onward(): return lax.ppermute(c, 'tm', ring)  4.99 us
    ppermute x1, starting transfers between devices, body(): from_odd = lax.ppermute(to_odd, ('tm', 'gx'), odd_pairs)  3.03 us
  transfers between devices with their start and end apart: 6, of which 4 were waited for; matrix products, arithmetic and copies ran while one was open for 0% of the time, Pallas kernels for 34%

profile of v5, /device:TPU:0, one launch (start us, length us, event | category | flops | bytes accessed | tf_op | source)
XLA Modules:
  0.0 23.8 jit_solution(8706065961841306396)
XLA Ops:
  0.6 0.0 copy-start
  0.6 0.0 copy-start.2
  0.7 0.0 copy-start.3
  0.7 1.1 %pack.1.after = f32[3,128,128]{2,1,0:T(8,128)S(1)} custom-call(f32[16,128,128]{2,1,0:T(8,128)} %bitcast.1, f32[16,128,128]{2,1,0:T(8,128)} %refs_2_.5), custom_call_target="tpu_custom_call" | custom-call | flops 10000000000 | bytes 1000000000 | tf_op jit(solution)/shard_map/pack/pallas_call | solution.py:137
  1.8 3.0 %collective-permute-start.1 = (f32[3,128,128]{2,1,0:T(8,128)S(1)}, f32[3,128,128]{2,1,0:T(8,128)S(1)}, u32[]{:S(2)}, u32[]{:S(2)}) collective-permute-start(f32[3,128,128]{2,1,0:T(8,128)S(1)} %pack.1.after), channel_id=1, source_target_pairs={{0,16},{1,2},{2,1},{3,4},{4,3},{5,6},{6,5},{7,23},{8,24},{9,10},{1... | collective-permute-start | bytes 589832 | tf_op jit(solution)/shard_map/ppermute | solution.py:407
  4.8 1.0 %inner.1 = (f32[10,128,128]{2,1,0:T(8,128)S(1)}, f32[64,640]{1,0:T(8,128)S(1)}, f32[3,128,128]{2,1,0:T(8,128)S(1)}) custom-call(f32[16,128,128]{2,1,0:T(8,128)S(1)} %bitcast.2, f32[16,128,128]{2,1,0:T(8,128)S(1)} %copy-done, bf16[768,128]{1,0:T(8,128)(2,1)S(1)} %copy-done.2, bf16[64,384]{1,0:T(8,128)(2,1)S(1)} %copy-done.3, f32[3,128,128]{2,1,0:T(8,128)S(1)} %pack.1.after), custom_call_target="tpu_custom_call" | custom-call | flops 10000000000 | bytes 1000000000 | tf_op jit(solution)/shard_map/inner/pallas_call | solution.py:137
  5.8 0.2 collective-permute-start
  6.0 1.5 %collective-permute-start.2 = (f32[64,640]{1,0:T(8,128)S(1)}, f32[64,640]{1,0:T(8,128)S(1)}, u32[]{:S(2)}, u32[]{:S(2)}) collective-permute-start(f32[64,640]{1,0:T(8,128)S(1)} %get-tuple-element.28), channel_id=1, source_target_pairs={{0,8},{8,16},{16,24},{24,0},{1,9},{9,17},{17,25},{25,1},{2,10},{10... | collective-permute-start | bytes 491528 | tf_op jit(solution)/shard_map/ppermute | solution.py:402
  7.5 1.2 %middle.1 = (f32[4,128,128]{2,1,0:T(8,128)S(1)}, f32[12,128,128]{2,1,0:T(8,128)S(1)}, f32[64,640]{1,0:T(8,128)S(1)}, f32[64,256]{1,0:T(8,128)S(1)}) custom-call(f32[16,128,128]{2,1,0:T(8,128)S(1)} %bitcast.3, f32[16,128,128]{2,1,0:T(8,128)S(1)} %copy-done, bf16[768,128]{1,0:T(8,128)(2,1)S(1)} %copy-done.2, bf16[64,384]{1,0:T(8,128)(2,1)S(1)} %copy-done.3, ...), custom_call_target="tpu_custom_call" | custom-call | tf_op jit(solution)/shard_map/middle/pallas_call | solution.py:137
  8.7 0.0 collective-permute-done.1.odd_ref
  8.7 0.0 collective-permute-done.even_ref
  8.7 0.7 %outer.1 = (f32[4,128,128]{2,1,0:T(8,128)S(1)}, f32[4,128,128]{2,1,0:T(8,128)S(1)}, f32[64,512]{1,0:T(8,128)S(1)}) custom-call(f32[16,128,128]{2,1,0:T(8,128)S(1)} %bitcast.4, f32[16,128,128]{2,1,0:T(8,128)S(1)} %copy-done, f32[3,128,128]{2,1,0:T(8,128)S(1)} %collective-permute-done.even_ref, f32[3,128,128]{2,1,0:T(8,128)S(1)} %collective-permute-done.1.odd_ref, ...), custom_call_target="tpu_custom_call" | custom-call | flops 10000000000 | bytes 1000000000 | tf_op jit(solution)/shard_map/outer/pallas_call | solution.py:137
  9.4 1.8 %collective-permute-start.3 = (f32[64,512]{1,0:T(8,128)S(1)}, f32[64,512]{1,0:T(8,128)S(1)}, u32[]{:S(2)}, u32[]{:S(2)}) collective-permute-start(f32[64,512]{1,0:T(8,128)S(1)} %get-tuple-element.31), channel_id=1, source_target_pairs={{0,8},{8,16},{16,24},{24,0},{1,9},{9,17},{17,25},{25,1},{2,10},{10... | collective-permute-start | bytes 393224 | tf_op jit(solution)/shard_map/ppermute | solution.py:402
  11.2 0.5 %later.1 = (f32[4,128,128]{2,1,0:T(8,128)S(1)}, f32[64,512]{1,0:T(8,128)S(1)}) custom-call(f32[16,128,128]{2,1,0:T(8,128)S(1)} %bitcast.5, f32[16,128,128]{2,1,0:T(8,128)S(1)} %copy-done, f32[4,128,128]{2,1,0:T(8,128)S(1)} %get-tuple-element.24.ab_ref.refs_1_, f32[4,128,128]{2,1,0:T(8,128)S(1)} %get-tuple-element.25.gb_ref, ...), custom_call_target="tpu_custom_call" | custom-call | flops 10000000000 | bytes 1000000000 | tf_op jit(solution)/shard_map/later/pallas_call | solution.py:137
  11.7 1.9 %collective-permute-done.2.refs_5_.refs_4_ = f32[64,640]{1,0:T(8,128)S(1)} collective-permute-done((f32[64,640]{1,0:T(8,128)S(1)}, f32[64,640]{1,0:T(8,128)S(1)}, u32[]{:S(2)}, u32[]{:S(2)}) %collective-permute-start.2) | collective-permute-done | bytes 163872 | tf_op jit(solution)/shard_map/ppermute | solution.py:402
  13.6 1.4 %second.2 = (f32[10,128,128]{2,1,0:T(8,128)S(1)}, f32[8,128,128]{2,1,0:T(8,128)S(1)}, f32[64,512]{1,0:T(8,128)S(1)}) custom-call(f32[16,128,128]{2,1,0:T(8,128)S(1)} %bitcast.6, f32[4,128,128]{2,1,0:T(8,128)S(1)} %get-tuple-element.24.ab_ref.refs_1_, f32[16,128,128]{2,1,0:T(8,128)S(1)} %copy-done, f32[12,128,128]{2,1,0:T(8,128)S(1)} %get-tuple-element.23.after.refs_3_, ...), custom_call_target="tpu_custom_call" | custom-call | flops 10000000000 | bytes 1000000000 | tf_op jit(solution)/shard_map/second/pallas_call | solution.py:137
  15.1 0.8 %collective-permute-start.5 = (f32[64,512]{1,0:T(8,128)S(1)}, f32[64,512]{1,0:T(8,128)S(1)}, u32[]{:S(2)}, u32[]{:S(2)}) collective-permute-start(f32[64,512]{1,0:T(8,128)S(1)} %get-tuple-element.37), channel_id=1, source_target_pairs={{0,8},{8,16},{16,24},{24,0},{1,9},{9,17},{17,25},{25,1},{2,10},{10... | collective-permute-start | bytes 393224 | tf_op jit(solution)/shard_map/ppermute | solution.py:402
  15.8 0.3 %collective-permute-done.3.refs_5_ = f32[64,512]{1,0:T(8,128)S(1)} collective-permute-done((f32[64,512]{1,0:T(8,128)S(1)}, f32[64,512]{1,0:T(8,128)S(1)}, u32[]{:S(2)}, u32[]{:S(2)}) %collective-permute-start.3) | collective-permute-done | bytes 131104 | tf_op jit(solution)/shard_map/ppermute | solution.py:402
  16.2 1.3 %second.3 = (f32[8,128,128]{2,1,0:T(8,128)S(1)}, f32[8,128,128]{2,1,0:T(8,128)S(1)}, f32[64,512]{1,0:T(8,128)S(1)}) custom-call(f32[16,128,128]{2,1,0:T(8,128)S(1)} %bitcast.7, f32[4,128,128]{2,1,0:T(8,128)S(1)} %get-tuple-element.24.ab_ref.refs_1_, f32[16,128,128]{2,1,0:T(8,128)S(1)} %copy-done, f32[12,128,128]{2,1,0:T(8,128)S(1)} %get-tuple-element.23.after.refs_3_, ...), custom_call_target="tpu_custom_call" | custom-call | flops 10000000000 | bytes 1000000000 | tf_op jit(solution)/shard_map/second/pallas_call | solution.py:137
  17.5 1.6 %collective-permute-start.4 = (f32[64,512]{1,0:T(8,128)S(1)}, f32[64,512]{1,0:T(8,128)S(1)}, u32[]{:S(2)}, u32[]{:S(2)}) collective-permute-start(f32[64,512]{1,0:T(8,128)S(1)} %get-tuple-element.35), channel_id=1, source_target_pairs={{0,8},{8,16},{16,24},{24,0},{1,9},{9,17},{17,25},{25,1},{2,10},{10... | collective-permute-start | bytes 393224 | tf_op jit(solution)/shard_map/ppermute | solution.py:402
  19.0 1.0 %join.1 = f32[1,16,128,128]{3,2,1,0:T(8,128)} custom-call(f32[8,128,128]{2,1,0:T(8,128)S(1)} %get-tuple-element.30.refs_0_, f32[8,128,128]{2,1,0:T(8,128)S(1)} %get-tuple-element.34.refs_1_), custom_call_target="tpu_custom_call" | custom-call | flops 10000000000 | bytes 1000000000 | tf_op jit(solution)/shard_map/join/pallas_call | solution.py:137
  20.0 1.3 %collective-permute-done.5.refs_0_ = f32[64,512]{1,0:T(8,128)S(1)} collective-permute-done((f32[64,512]{1,0:T(8,128)S(1)}, f32[64,512]{1,0:T(8,128)S(1)}, u32[]{:S(2)}, u32[]{:S(2)}) %collective-permute-start.5) | collective-permute-done | bytes 131104 | tf_op jit(solution)/shard_map/ppermute | solution.py:402
  21.4 1.0 %last.2.refs_8_ = f32[1,16,128,128]{3,2,1,0:T(8,128)} custom-call(f32[64,512]{1,0:T(8,128)S(1)} %collective-permute-done.5.refs_0_, bf16[128,192]{1,0:T(8,128)(2,1)S(1)} %copy-done.5, bf16[384,256]{1,0:T(8,128)(2,1)S(1)} %copy-done.4, f32[16,128,128]{2,1,0:T(8,128)S(1)} %bitcast.8, f32[64,640]{1,0:T(8,128)S(1)} %collective-permute-done.2.refs_5_.refs_4_, ...), custom_call_target="tpu_custom_call" | custom-call | flops 10000000000 | bytes 1000000000 | tf_op jit(solution)/shard_map/last/pallas_call | solution.py:137
  22.4 1.4 %collective-permute-done.4.refs_0_ = f32[64,512]{1,0:T(8,128)S(1)} collective-permute-done((f32[64,512]{1,0:T(8,128)S(1)}, f32[64,512]{1,0:T(8,128)S(1)}, u32[]{:S(2)}, u32[]{:S(2)}) %collective-permute-start.4) | collective-permute-done | bytes 131104 | tf_op jit(solution)/shard_map/ppermute | solution.py:402
  (10 shorter events, 0.1 us)
Async XLA Ops:
  0.6 4.2 %copy-start = (f32[16,128,128]{2,1,0:T(8,128)S(1)}, f32[16,128,128]{2,1,0:T(8,128)}, u32[]{:S(2)}) copy-start(f32[16,128,128]{2,1,0:T(8,128)} %refs_2_.5) | copy-start | bytes 3145732
  0.6 4.2 %copy-start.1 = (f32[1,16,128,128]{3,2,1,0:T(8,128)S(1)}, f32[1,16,128,128]{3,2,1,0:T(8,128)}, u32[]{:S(2)}) copy-start(f32[1,16,128,128]{3,2,1,0:T(8,128)} %param.6) | copy-start | bytes 3145732
  0.6 4.2 %copy-start.2 = (bf16[768,128]{1,0:T(8,128)(2,1)S(1)}, bf16[768,128]{1,0:T(8,128)(2,1)}, u32[]{:S(2)}) copy-start(bf16[768,128]{1,0:T(8,128)(2,1)} %constant.8.clone.fz_ref.refs_7_) | copy-start | bytes 589828
  0.7 4.1 %copy-start.3 = (bf16[64,384]{1,0:T(8,128)(2,1)S(1)}, bf16[64,384]{1,0:T(8,128)(2,1)}, u32[]{:S(2)}) copy-start(bf16[64,384]{1,0:T(8,128)(2,1)} %constant.9.clone.fy_ref.refs_8_) | copy-start | bytes 147460
  1.8 6.9 %collective-permute-start.1 = (f32[3,128,128]{2,1,0:T(8,128)S(1)}, f32[3,128,128]{2,1,0:T(8,128)S(1)}, u32[]{:S(2)}, u32[]{:S(2)}) collective-permute-start(f32[3,128,128]{2,1,0:T(8,128)S(1)} %pack.1.after), channel_id=1, source_target_pairs={{0,16},{1,2},{2,1},{3,4},{4,3},{5,6},{6,5},{7,23},{8,24},{9,10},{1... | collective-permute-start | bytes 589832 | tf_op jit(solution)/shard_map/ppermute | solution.py:407
  5.8 2.9 %collective-permute-start = (f32[3,128,128]{2,1,0:T(8,128)S(1)}, f32[3,128,128]{2,1,0:T(8,128)S(1)}, u32[]{:S(2)}, u32[]{:S(2)}) collective-permute-start(f32[3,128,128]{2,1,0:T(8,128)S(1)} %get-tuple-element.20), channel_id=1, source_target_pairs={{0,1},{1,0},{2,3},{3,2},{4,5},{5,4},{6,7},{7,6},{8,9},{9,8},{10,11... | collective-permute-start | bytes 589832 | tf_op jit(solution)/shard_map/ppermute | solution.py:419
  6.0 7.6 %collective-permute-start.2 = (f32[64,640]{1,0:T(8,128)S(1)}, f32[64,640]{1,0:T(8,128)S(1)}, u32[]{:S(2)}, u32[]{:S(2)}) collective-permute-start(f32[64,640]{1,0:T(8,128)S(1)} %get-tuple-element.28), channel_id=1, source_target_pairs={{0,8},{8,16},{16,24},{24,0},{1,9},{9,17},{17,25},{25,1},{2,10},{10... | collective-permute-start | bytes 491528 | tf_op jit(solution)/shard_map/ppermute | solution.py:402
  9.4 6.8 %collective-permute-start.3 = (f32[64,512]{1,0:T(8,128)S(1)}, f32[64,512]{1,0:T(8,128)S(1)}, u32[]{:S(2)}, u32[]{:S(2)}) collective-permute-start(f32[64,512]{1,0:T(8,128)S(1)} %get-tuple-element.31), channel_id=1, source_target_pairs={{0,8},{8,16},{16,24},{24,0},{1,9},{9,17},{17,25},{25,1},{2,10},{10... | collective-permute-start | bytes 393224 | tf_op jit(solution)/shard_map/ppermute | solution.py:402
  11.2 2.4 %copy-start.4 = (bf16[384,256]{1,0:T(8,128)(2,1)S(1)}, bf16[384,256]{1,0:T(8,128)(2,1)}, u32[]{:S(2)}) copy-start(bf16[384,256]{1,0:T(8,128)(2,1)} %constant.11.clone.refs_10_.refs_2_) | copy-start | bytes 589828
  11.2 2.4 %copy-start.5 = (bf16[128,192]{1,0:T(8,128)(2,1)S(1)}, bf16[128,192]{1,0:T(8,128)(2,1)}, u32[]{:S(2)}) copy-start(bf16[128,192]{1,0:T(8,128)(2,1)} %constant.10.clone.refs_9_.refs_1_) | copy-start | bytes 147460
  15.1 6.3 %collective-permute-start.5 = (f32[64,512]{1,0:T(8,128)S(1)}, f32[64,512]{1,0:T(8,128)S(1)}, u32[]{:S(2)}, u32[]{:S(2)}) collective-permute-start(f32[64,512]{1,0:T(8,128)S(1)} %get-tuple-element.37), channel_id=1, source_target_pairs={{0,8},{8,16},{16,24},{24,0},{1,9},{9,17},{17,25},{25,1},{2,10},{10... | collective-permute-start | bytes 393224 | tf_op jit(solution)/shard_map/ppermute | solution.py:402
  17.5 6.3 %collective-permute-start.4 = (f32[64,512]{1,0:T(8,128)S(1)}, f32[64,512]{1,0:T(8,128)S(1)}, u32[]{:S(2)}, u32[]{:S(2)}) collective-permute-start(f32[64,512]{1,0:T(8,128)S(1)} %get-tuple-element.35), channel_id=1, source_target_pairs={{0,8},{8,16},{16,24},{24,0},{1,9},{9,17},{17,25},{25,1},{2,10},{10... | collective-permute-start | bytes 393224 | tf_op jit(solution)/shard_map/ppermute | solution.py:402

commit v6 on v5

--- a/solution.py
+++ b/solution.py
@@ -18,10 +18,6 @@
 COST = 10**8
 ANY = pl.BlockSpec(memory_space=pl.ANY)
 VMEM = pl.BlockSpec(memory_space=pltpu.VMEM)
-
-
-def CUTS(last):
-    return [last - 2]
 
 
 def basis_value(node_times, source, point):
@@ -70,9 +66,9 @@
     twice[:nz, :KZ] = cz.T
     twice[nz:, KZ:] = cz.T
     zh, zl = halves(twice)
-    fz = np.concatenate([zh, zh, zl], axis=0)
+    fz = np.concatenate([zh, zl], axis=1)
     yh, yl = halves(cy)
-    fy = np.concatenate([yh, yh, yl], axis=1)
+    fy = np.block([[yh, yh], [yl, np.zeros_like(yl)]])
     by = np.concatenate([yh.T, yh.T, yl.T], axis=1)
     bz = np.concatenate([zh.T, zh.T, zl.T], axis=0)
     return fz, fy, by, bz
@@ -89,12 +85,15 @@
 
 def neighbours(v):
     ny, nz = v.shape
-    rows = lax.broadcasted_iota(jnp.int32, v.shape, 0)
+    rows = lax.broadcasted_iota(jnp.int32, (8, nz), 0)
     lanes = lax.broadcasted_iota(jnp.int32, v.shape, 1)
-    total = jnp.where(rows == 0, 0.0, pltpu.roll(v, 1, 0))
-    total = total + jnp.where(rows == ny - 1, 0.0, pltpu.roll(v, ny - 1, 0))
-    total = total + jnp.where(lanes == 0, 0.0, pltpu.roll(v, 1, 1))
-    return total + jnp.where(lanes == nz - 1, 0.0, pltpu.roll(v, nz - 1, 1))
+    low = pltpu.roll(v, 1, 0)
+    high = pltpu.roll(v, ny - 1, 0)
+    low = jnp.concatenate([jnp.where(rows == 0, 0.0, low[:8]), low[8:]], axis=0)
+    high = jnp.concatenate([high[: ny - 8], jnp.where(rows == 7, 0.0, high[ny - 8 :])], axis=0)
+    left = jnp.where(lanes == 0, 0.0, pltpu.roll(v, 1, 1))
+    right = jnp.where(lanes == nz - 1, 0.0, pltpu.roll(v, nz - 1, 1))
+    return (low + high) + (left + right)
 
 
 def rate(below, v, above, mobility):
@@ -106,16 +105,17 @@
     for first, second in pairs:
         first_high, first_low = split(first)
         second_high, second_low = split(second)
-        rows.append(
-            jnp.concatenate([first_high, second_high, first_low, second_low, first_high, second_high], axis=1)
-        )
-    half = dot(jnp.concatenate(rows, axis=0), fz_ref[...])
+        rows.append(jnp.concatenate([first_high, second_high, first_low, second_low], axis=1))
+    rows = jnp.concatenate(rows, axis=0)
+    width, nz = 2 * KZ, pairs[0][0].shape[1]
+    half = dot(rows[:, : 2 * nz], fz_ref[...])
+    half = half[:, :width] + half[:, width:] + dot(rows[:, 2 * nz :], fz_ref[:, :width])
     ny = pairs[0][0].shape[0]
     columns = []
     for i in range(len(pairs)):
-        high, low = split(half[i * ny : (i + 1) * ny])
-        columns.append(jnp.concatenate([high, low, high], axis=0))
-    return dot(fy_ref[...], jnp.concatenate(columns, axis=1))
+        columns.append(jnp.concatenate(split(half[i * ny : (i + 1) * ny]), axis=0))
+    coeffs = dot(fy_ref[...], jnp.concatenate(columns, axis=1))
+    return coeffs[:KY] + coeffs[KY:]
 
 
 def synthesise(coeffs, by_ref, bz_ref):
@@ -151,11 +151,9 @@
 
 def chunks(nx):
     last = nx // 2
-    cuts = [1, *CUTS(last)]
-    first = [list(range(cuts[i], cuts[i + 1])) for i in range(len(cuts) - 1)]
-    second = [list(range(cuts[i] - (i > 0), cuts[i + 1] - 1)) for i in range(len(cuts) - 1)]
-    first.append([0, *range(cuts[-1], last), last])
-    second.append([0, *range(cuts[-1] - 1, last - 1), last - 1])
+    early, soon = last - 3, last - 4
+    first = [list(range(1, early + 1)), [0, *range(early + 1, last + 1)]]
+    second = [list(range(1, soon + 1)), [0, *range(soon + 1, last)]]
     return first, second
 
 
@@ -294,10 +292,20 @@
     earlier, (a1_ref, e_ref, c2_ref) = refs[11:-3], refs[-3:]
     nx, ny, nz = mu_ref.shape
     first, second = chunks(nx)
-    change = synthesise(received(c1_ref[...], own_ref[...]), by_ref, bz_ref)
     before = reader((a_ref, range(nx)), (ab_ref, outer_planes(nx)))
-    for i, p in enumerate(planes_of(first[stage], -1)):
-        a1_ref[i] = before(p) + change[i // 2][:, (i % 2) * nz : (i % 2 + 1) * nz]
+    receives = lax.axis_index("tm") > 0
+
+    @pl.when(receives)
+    def _():
+        change = synthesise(c1_ref[...] - own_ref[...], by_ref, bz_ref)
+        for i, p in enumerate(planes_of(first[stage], -1)):
+            a1_ref[i] = before(p) + change[i // 2][:, (i % 2) * nz : (i % 2 + 1) * nz]
+
+    @pl.when(jnp.logical_not(receives))
+    def _():
+        for i, p in enumerate(planes_of(first[stage], -1)):
+            a1_ref[i] = before(p)
+
     values = reader(*[(ref, planes_of(part, -1)) for ref, part in zip((*earlier, a1_ref), first)])
     parts = reader((acc_ref, range(2, nx - 2)), (accb_ref, (0, 1, nx - 2, nx - 1)))
     ends = []

time: 24 us -> 23.3 us (0.971)
  Pallas kernels: 9.14 us -> 7.62 us
  starting transfers between devices: 8.9 us -> 9.59 us
    pallas_call x10, Pallas kernels: 9.14 us -> 7.62 us  [run(): pl.pallas_call(kernel, out_shape=outs, in_specs=specs or [VMEM] * len(arg...]
    ppermute x4, starting transfers between devices: 5.63 us -> 6.33 us  [onward(): return lax.ppermute(c, 'tm', ring)]
  transfers between devices with their start and end apart: 6 -> 6, of which waited for: 4 -> 4; matrix products, arithmetic and copies ran while one was open for 0% -> 0% of each run, Pallas kernels for 34% -> 28%
where the time goes in v6:
time: 23.3 us; the launch traced here: 23.2 us
  starting transfers between devices  9.59 us (41%)
  Pallas kernels  7.62 us (33%)
  waiting for transfers between devices  5.17 us (22%)
  between operations  0.74 us (3%)
    pallas_call x10, Pallas kernels, run(): pl.pallas_call(kernel, out_shape=outs, in_specs=specs or [VMEM] * len(arg...  7.62 us
    ppermute x4, starting transfers between devices, onward(): return lax.ppermute(c, 'tm', ring)  6.33 us
    ppermute x4, waiting for transfers between devices, onward(): return lax.ppermute(c, 'tm', ring)  5.16 us
    ppermute x1, starting transfers between devices, body(): from_odd = lax.ppermute(to_odd, ('tm', 'gx'), odd_pairs)  3.03 us
  transfers between devices with their start and end apart: 6, of which 4 were waited for; matrix products, arithmetic and copies ran while one was open for 0% of the time, Pallas kernels for 28%

profile of v6, /device:TPU:0, one launch (start us, length us, event | category | flops | bytes accessed | tf_op | source)
XLA Modules:
  0.0 23.2 jit_solution(11242434264559105972)
XLA Ops:
  0.6 0.0 copy-start.2
  0.7 0.0 copy-start.3
  0.7 1.1 %pack.1.after = f32[3,128,128]{2,1,0:T(8,128)S(1)} custom-call(f32[16,128,128]{2,1,0:T(8,128)} %bitcast.1, f32[16,128,128]{2,1,0:T(8,128)} %refs_2_.5), custom_call_target="tpu_custom_call" | custom-call | flops 10000000000 | bytes 1000000000 | tf_op jit(solution)/shard_map/pack/pallas_call | solution.py:137
  1.8 3.0 %collective-permute-start.1 = (f32[3,128,128]{2,1,0:T(8,128)S(1)}, f32[3,128,128]{2,1,0:T(8,128)S(1)}, u32[]{:S(2)}, u32[]{:S(2)}) collective-permute-start(f32[3,128,128]{2,1,0:T(8,128)S(1)} %pack.1.after), channel_id=1, source_target_pairs={{0,16},{1,2},{2,1},{3,4},{4,3},{5,6},{6,5},{7,23},{8,24},{9,10},{1... | collective-permute-start | bytes 589832 | tf_op jit(solution)/shard_map/ppermute | solution.py:415
  4.8 0.0 copy-done.1
  4.8 0.8 %inner.1 = (f32[10,128,128]{2,1,0:T(8,128)S(1)}, f32[64,640]{1,0:T(8,128)S(1)}, f32[3,128,128]{2,1,0:T(8,128)S(1)}) custom-call(f32[16,128,128]{2,1,0:T(8,128)S(1)} %bitcast.2, f32[16,128,128]{2,1,0:T(8,128)S(1)} %copy-done, bf16[256,256]{1,0:T(8,128)(2,1)S(1)} %copy-done.2, bf16[128,256]{1,0:T(8,128)(2,1)S(1)} %copy-done.3, f32[3,128,128]{2,1,0:T(8,128)S(1)} %pack.1.after), custom_call_target="tpu_custom_call" | custom-call | flops 10000000000 | bytes 1000000000 | tf_op jit(solution)/shard_map/inner/pallas_call | solution.py:137
  5.6 0.2 %collective-permute-start = (f32[3,128,128]{2,1,0:T(8,128)S(1)}, f32[3,128,128]{2,1,0:T(8,128)S(1)}, u32[]{:S(2)}, u32[]{:S(2)}) collective-permute-start(f32[3,128,128]{2,1,0:T(8,128)S(1)} %get-tuple-element.20), channel_id=1, source_target_pairs={{0,1},{1,0},{2,3},{3,2},{4,5},{5,4},{6,7},{7,6},{8,9},{9,8},{10,11... | collective-permute-start | bytes 589832 | tf_op jit(solution)/shard_map/ppermute | solution.py:427
  5.8 1.5 %collective-permute-start.2 = (f32[64,640]{1,0:T(8,128)S(1)}, f32[64,640]{1,0:T(8,128)S(1)}, u32[]{:S(2)}, u32[]{:S(2)}) collective-permute-start(f32[64,640]{1,0:T(8,128)S(1)} %get-tuple-element.28), channel_id=1, source_target_pairs={{0,8},{8,16},{16,24},{24,0},{1,9},{9,17},{17,25},{25,1},{2,10},{10... | collective-permute-start | bytes 491528 | tf_op jit(solution)/shard_map/ppermute | solution.py:410
  7.3 1.1 %middle.1 = (f32[4,128,128]{2,1,0:T(8,128)S(1)}, f32[12,128,128]{2,1,0:T(8,128)S(1)}, f32[64,640]{1,0:T(8,128)S(1)}, f32[64,256]{1,0:T(8,128)S(1)}) custom-call(f32[16,128,128]{2,1,0:T(8,128)S(1)} %bitcast.3, f32[16,128,128]{2,1,0:T(8,128)S(1)} %copy-done, bf16[256,256]{1,0:T(8,128)(2,1)S(1)} %copy-done.2, bf16[128,256]{1,0:T(8,128)(2,1)S(1)} %copy-done.3, ...), custom_call_target="tpu_custom_call" | custom-call | tf_op jit(solution)/shard_map/middle/pallas_call | solution.py:137
  8.5 0.0 collective-permute-done.1.odd_ref
  8.5 0.0 collective-permute-done.even_ref
  8.5 0.6 %outer.1 = (f32[4,128,128]{2,1,0:T(8,128)S(1)}, f32[4,128,128]{2,1,0:T(8,128)S(1)}, f32[64,512]{1,0:T(8,128)S(1)}) custom-call(f32[16,128,128]{2,1,0:T(8,128)S(1)} %bitcast.4, f32[16,128,128]{2,1,0:T(8,128)S(1)} %copy-done, f32[3,128,128]{2,1,0:T(8,128)S(1)} %collective-permute-done.even_ref, f32[3,128,128]{2,1,0:T(8,128)S(1)} %collective-permute-done.1.odd_ref, ...), custom_call_target="tpu_custom_call" | custom-call | flops 10000000000 | bytes 1000000000 | tf_op jit(solution)/shard_map/outer/pallas_call | solution.py:137
  9.1 2.0 %collective-permute-start.3 = (f32[64,512]{1,0:T(8,128)S(1)}, f32[64,512]{1,0:T(8,128)S(1)}, u32[]{:S(2)}, u32[]{:S(2)}) collective-permute-start(f32[64,512]{1,0:T(8,128)S(1)} %get-tuple-element.31), channel_id=1, source_target_pairs={{0,8},{8,16},{16,24},{24,0},{1,9},{9,17},{17,25},{25,1},{2,10},{10... | collective-permute-start | bytes 393224 | tf_op jit(solution)/shard_map/ppermute | solution.py:410
  11.1 0.4 %later.1 = (f32[4,128,128]{2,1,0:T(8,128)S(1)}, f32[64,512]{1,0:T(8,128)S(1)}) custom-call(f32[16,128,128]{2,1,0:T(8,128)S(1)} %bitcast.5, f32[16,128,128]{2,1,0:T(8,128)S(1)} %copy-done, f32[4,128,128]{2,1,0:T(8,128)S(1)} %get-tuple-element.24.ab_ref.refs_1_, f32[4,128,128]{2,1,0:T(8,128)S(1)} %get-tuple-element.25.gb_ref, ...), custom_call_target="tpu_custom_call" | custom-call | flops 10000000000 | bytes 1000000000 | tf_op jit(solution)/shard_map/later/pallas_call | solution.py:137
  11.5 2.1 %collective-permute-done.2.refs_5_.refs_4_ = f32[64,640]{1,0:T(8,128)S(1)} collective-permute-done((f32[64,640]{1,0:T(8,128)S(1)}, f32[64,640]{1,0:T(8,128)S(1)}, u32[]{:S(2)}, u32[]{:S(2)}) %collective-permute-start.2) | collective-permute-done | bytes 163872 | tf_op jit(solution)/shard_map/ppermute | solution.py:410
  13.6 0.8 %second.2 = (f32[10,128,128]{2,1,0:T(8,128)S(1)}, f32[8,128,128]{2,1,0:T(8,128)S(1)}, f32[64,512]{1,0:T(8,128)S(1)}) custom-call(f32[16,128,128]{2,1,0:T(8,128)S(1)} %bitcast.6, f32[4,128,128]{2,1,0:T(8,128)S(1)} %get-tuple-element.24.ab_ref.refs_1_, f32[16,128,128]{2,1,0:T(8,128)S(1)} %copy-done, f32[12,128,128]{2,1,0:T(8,128)S(1)} %get-tuple-element.23.after.refs_3_, ...), custom_call_target="tpu_custom_call" | custom-call | flops 10000000000 | bytes 1000000000 | tf_op jit(solution)/shard_map/second/pallas_call | solution.py:137
  14.4 1.1 %collective-permute-start.5 = (f32[64,512]{1,0:T(8,128)S(1)}, f32[64,512]{1,0:T(8,128)S(1)}, u32[]{:S(2)}, u32[]{:S(2)}) collective-permute-start(f32[64,512]{1,0:T(8,128)S(1)} %get-tuple-element.37), channel_id=1, source_target_pairs={{0,8},{8,16},{16,24},{24,0},{1,9},{9,17},{17,25},{25,1},{2,10},{10... | collective-permute-start | bytes 393224 | tf_op jit(solution)/shard_map/ppermute | solution.py:410
  15.5 0.5 %collective-permute-done.3.refs_5_ = f32[64,512]{1,0:T(8,128)S(1)} collective-permute-done((f32[64,512]{1,0:T(8,128)S(1)}, f32[64,512]{1,0:T(8,128)S(1)}, u32[]{:S(2)}, u32[]{:S(2)}) %collective-permute-start.3) | collective-permute-done | bytes 131104 | tf_op jit(solution)/shard_map/ppermute | solution.py:410
  16.0 0.8 %second.3 = (f32[8,128,128]{2,1,0:T(8,128)S(1)}, f32[8,128,128]{2,1,0:T(8,128)S(1)}, f32[64,512]{1,0:T(8,128)S(1)}) custom-call(f32[16,128,128]{2,1,0:T(8,128)S(1)} %bitcast.7, f32[4,128,128]{2,1,0:T(8,128)S(1)} %get-tuple-element.24.ab_ref.refs_1_, f32[16,128,128]{2,1,0:T(8,128)S(1)} %copy-done, f32[12,128,128]{2,1,0:T(8,128)S(1)} %get-tuple-element.23.after.refs_3_, ...), custom_call_target="tpu_custom_call" | custom-call | flops 10000000000 | bytes 1000000000 | tf_op jit(solution)/shard_map/second/pallas_call | solution.py:137
  16.8 1.8 %collective-permute-start.4 = (f32[64,512]{1,0:T(8,128)S(1)}, f32[64,512]{1,0:T(8,128)S(1)}, u32[]{:S(2)}, u32[]{:S(2)}) collective-permute-start(f32[64,512]{1,0:T(8,128)S(1)} %get-tuple-element.35), channel_id=1, source_target_pairs={{0,8},{8,16},{16,24},{24,0},{1,9},{9,17},{17,25},{25,1},{2,10},{10... | collective-permute-start | bytes 393224 | tf_op jit(solution)/shard_map/ppermute | solution.py:410
  18.5 1.0 %join.1 = f32[1,16,128,128]{3,2,1,0:T(8,128)} custom-call(f32[8,128,128]{2,1,0:T(8,128)S(1)} %get-tuple-element.30.refs_0_, f32[8,128,128]{2,1,0:T(8,128)S(1)} %get-tuple-element.34.refs_1_), custom_call_target="tpu_custom_call" | custom-call | flops 10000000000 | bytes 1000000000 | tf_op jit(solution)/shard_map/join/pallas_call | solution.py:137
  19.5 1.1 %collective-permute-done.5.refs_0_ = f32[64,512]{1,0:T(8,128)S(1)} collective-permute-done((f32[64,512]{1,0:T(8,128)S(1)}, f32[64,512]{1,0:T(8,128)S(1)}, u32[]{:S(2)}, u32[]{:S(2)}) %collective-permute-start.5) | collective-permute-done | bytes 131104 | tf_op jit(solution)/shard_map/ppermute | solution.py:410
  20.6 1.0 %last.2.refs_8_ = f32[1,16,128,128]{3,2,1,0:T(8,128)} custom-call(f32[64,512]{1,0:T(8,128)S(1)} %collective-permute-done.5.refs_0_, bf16[128,192]{1,0:T(8,128)(2,1)S(1)} %copy-done.5, bf16[384,256]{1,0:T(8,128)(2,1)S(1)} %copy-done.4, f32[16,128,128]{2,1,0:T(8,128)S(1)} %bitcast.8, f32[64,640]{1,0:T(8,128)S(1)} %collective-permute-done.2.refs_5_.refs_4_, ...), custom_call_target="tpu_custom_call" | custom-call | flops 10000000000 | bytes 1000000000 | tf_op jit(solution)/shard_map/last/pallas_call | solution.py:137
  21.6 1.5 %collective-permute-done.4.refs_0_ = f32[64,512]{1,0:T(8,128)S(1)} collective-permute-done((f32[64,512]{1,0:T(8,128)S(1)}, f32[64,512]{1,0:T(8,128)S(1)}, u32[]{:S(2)}, u32[]{:S(2)}) %collective-permute-start.4) | collective-permute-done | bytes 131104 | tf_op jit(solution)/shard_map/ppermute | solution.py:410
  (10 shorter events, 0.1 us)
Async XLA Ops:
  0.6 4.2 %copy-start = (f32[16,128,128]{2,1,0:T(8,128)S(1)}, f32[16,128,128]{2,1,0:T(8,128)}, u32[]{:S(2)}) copy-start(f32[16,128,128]{2,1,0:T(8,128)} %refs_2_.5) | copy-start | bytes 3145732
  0.6 4.2 %copy-start.1 = (f32[1,16,128,128]{3,2,1,0:T(8,128)S(1)}, f32[1,16,128,128]{3,2,1,0:T(8,128)}, u32[]{:S(2)}) copy-start(f32[1,16,128,128]{3,2,1,0:T(8,128)} %param.6) | copy-start | bytes 3145732
  0.6 4.2 %copy-start.2 = (bf16[256,256]{1,0:T(8,128)(2,1)S(1)}, bf16[256,256]{1,0:T(8,128)(2,1)}, u32[]{:S(2)}) copy-start(bf16[256,256]{1,0:T(8,128)(2,1)} %constant.8.clone.fz_ref.refs_7_) | copy-start | bytes 393220
  0.7 4.1 %copy-start.3 = (bf16[128,256]{1,0:T(8,128)(2,1)S(1)}, bf16[128,256]{1,0:T(8,128)(2,1)}, u32[]{:S(2)}) copy-start(bf16[128,256]{1,0:T(8,128)(2,1)} %constant.9.clone.fy_ref.refs_8_) | copy-start | bytes 196612
  1.8 6.7 %collective-permute-start.1 = (f32[3,128,128]{2,1,0:T(8,128)S(1)}, f32[3,128,128]{2,1,0:T(8,128)S(1)}, u32[]{:S(2)}, u32[]{:S(2)}) collective-permute-start(f32[3,128,128]{2,1,0:T(8,128)S(1)} %pack.1.after), channel_id=1, source_target_pairs={{0,16},{1,2},{2,1},{3,4},{4,3},{5,6},{6,5},{7,23},{8,24},{9,10},{1... | collective-permute-start | bytes 589832 | tf_op jit(solution)/shard_map/ppermute | solution.py:415
  5.6 2.9 %collective-permute-start = (f32[3,128,128]{2,1,0:T(8,128)S(1)}, f32[3,128,128]{2,1,0:T(8,128)S(1)}, u32[]{:S(2)}, u32[]{:S(2)}) collective-permute-start(f32[3,128,128]{2,1,0:T(8,128)S(1)} %get-tuple-element.20), channel_id=1, source_target_pairs={{0,1},{1,0},{2,3},{3,2},{4,5},{5,4},{6,7},{7,6},{8,9},{9,8},{10,11... | collective-permute-start | bytes 589832 | tf_op jit(solution)/shard_map/ppermute | solution.py:427
  5.8 7.8 %collective-permute-start.2 = (f32[64,640]{1,0:T(8,128)S(1)}, f32[64,640]{1,0:T(8,128)S(1)}, u32[]{:S(2)}, u32[]{:S(2)}) collective-permute-start(f32[64,640]{1,0:T(8,128)S(1)} %get-tuple-element.28), channel_id=1, source_target_pairs={{0,8},{8,16},{16,24},{24,0},{1,9},{9,17},{17,25},{25,1},{2,10},{10... | collective-permute-start | bytes 491528 | tf_op jit(solution)/shard_map/ppermute | solution.py:410
  9.1 6.9 %collective-permute-start.3 = (f32[64,512]{1,0:T(8,128)S(1)}, f32[64,512]{1,0:T(8,128)S(1)}, u32[]{:S(2)}, u32[]{:S(2)}) collective-permute-start(f32[64,512]{1,0:T(8,128)S(1)} %get-tuple-element.31), channel_id=1, source_target_pairs={{0,8},{8,16},{16,24},{24,0},{1,9},{9,17},{17,25},{25,1},{2,10},{10... | collective-permute-start | bytes 393224 | tf_op jit(solution)/shard_map/ppermute | solution.py:410
  11.1 2.5 %copy-start.4 = (bf16[384,256]{1,0:T(8,128)(2,1)S(1)}, bf16[384,256]{1,0:T(8,128)(2,1)}, u32[]{:S(2)}) copy-start(bf16[384,256]{1,0:T(8,128)(2,1)} %constant.11.clone.refs_10_.refs_2_) | copy-start | bytes 589828
  11.1 2.5 %copy-start.5 = (bf16[128,192]{1,0:T(8,128)(2,1)S(1)}, bf16[128,192]{1,0:T(8,128)(2,1)}, u32[]{:S(2)}) copy-start(bf16[128,192]{1,0:T(8,128)(2,1)} %constant.10.clone.refs_9_.refs_1_) | copy-start | bytes 147460
  14.4 6.2 %collective-permute-start.5 = (f32[64,512]{1,0:T(8,128)S(1)}, f32[64,512]{1,0:T(8,128)S(1)}, u32[]{:S(2)}, u32[]{:S(2)}) collective-permute-start(f32[64,512]{1,0:T(8,128)S(1)} %get-tuple-element.37), channel_id=1, source_target_pairs={{0,8},{8,16},{16,24},{24,0},{1,9},{9,17},{17,25},{25,1},{2,10},{10... | collective-permute-start | bytes 393224 | tf_op jit(solution)/shard_map/ppermute | solution.py:410
  16.8 6.4 %collective-permute-start.4 = (f32[64,512]{1,0:T(8,128)S(1)}, f32[64,512]{1,0:T(8,128)S(1)}, u32[]{:S(2)}, u32[]{:S(2)}) collective-permute-start(f32[64,512]{1,0:T(8,128)S(1)} %get-tuple-element.35), channel_id=1, source_target_pairs={{0,8},{8,16},{16,24},{24,0},{1,9},{9,17},{17,25},{25,1},{2,10},{10... | collective-permute-start | bytes 393224 | tf_op jit(solution)/shard_map/ppermute | solution.py:410

commit v7 on v6

--- a/solution.py
+++ b/solution.py
@@ -239,6 +239,10 @@
         start += ref.shape[1]
     for p in range(2, nx - 2):
         acc_ref[p - 2] = later_part(rates(p - 1), rates(p), rates(p + 1), a_ref[p], mu_ref[p])
+
+
+def mark_kernel(from_odd, after, out_ref):
+    out_ref[...] = jnp.zeros_like(out_ref)
 
 
 def outer_kernel(a_ref, mu_ref, even_ref, odd_ref, g_ref, fz_ref, fy_ref, after, a_out, g_out, c_ref):
@@ -432,8 +436,9 @@
         "middle",
         cost=0,
     )(a, mu, fz, fy, *g)
+    mark = call(mark_kernel, jax.ShapeDtypeStruct((8, 128), F32), "mark", specs=[ANY, ANY])(from_odd, acc)
     ab, gb, c = call(outer_kernel, [grid(4), grid(4), modes(first[-1])], "outer", specs=[VMEM] * 7 + [ANY])(
-        a, mu, from_even, from_odd, g_rest, fz, fy, acc
+        a, mu, from_even, from_odd, g_rest, fz, fy, mark
     )
     c1.append(onward(c))
     accb, own_last = call(later_kernel, [grid(4), modes(first[-1])], "later")(

time: 23.3 us -> 22.7 us (0.974)
  starting transfers between devices: 9.59 us -> 8.85 us
    ppermute x4, starting transfers between devices: 6.33 us -> 5.82 us  [onward(): return lax.ppermute(c, 'tm', ring)]
    pallas_call x10 -> x11, Pallas kernels: 7.62 us -> 7.72 us  [run(): pl.pallas_call(kernel, out_shape=outs, in_specs=specs or [VMEM] * len(arg...]
  transfers between devices with their start and end apart: 6 -> 6, of which waited for: 4 -> 6; matrix products, arithmetic and copies ran while one was open for 0% -> 0% of each run, Pallas kernels for 28% -> 29%
where the time goes in v7:
time: 22.7 us; the launch traced here: 22.6 us
  starting transfers between devices  8.85 us (39%)
  Pallas kernels  7.72 us (34%)
  waiting for transfers between devices  5.24 us (23%)
  between operations  0.73 us (3%)
    pallas_call x11, Pallas kernels, run(): pl.pallas_call(kernel, out_shape=outs, in_specs=specs or [VMEM] * len(arg...  7.72 us
    ppermute x4, starting transfers between devices, onward(): return lax.ppermute(c, 'tm', ring)  5.82 us
    ppermute x4, waiting for transfers between devices, onward(): return lax.ppermute(c, 'tm', ring)  4.98 us
    ppermute x1, starting transfers between devices, body(): from_odd = lax.ppermute(to_odd, ('tm', 'gx'), odd_pairs)  3.03 us
  transfers between devices with their start and end apart: 6, of which 6 were waited for; matrix products, arithmetic and copies ran while one was open for 0% of the time, Pallas kernels for 29%

profile of v7, /device:TPU:0, one launch (start us, length us, event | category | flops | bytes accessed | tf_op | source)
XLA Modules:
  0.0 22.6 jit_solution(15145865805589588804)
XLA Ops:
  0.6 0.0 copy-start.2
  0.7 0.0 copy-start.3
  0.7 1.1 %pack.1.after = f32[3,128,128]{2,1,0:T(8,128)S(1)} custom-call(f32[16,128,128]{2,1,0:T(8,128)} %bitcast.1, f32[16,128,128]{2,1,0:T(8,128)} %refs_2_.5), custom_call_target="tpu_custom_call" | custom-call | flops 10000000000 | bytes 1000000000 | tf_op jit(solution)/shard_map/pack/pallas_call | solution.py:137
  1.8 3.0 %collective-permute-start.1 = (f32[3,128,128]{2,1,0:T(8,128)S(1)}, f32[3,128,128]{2,1,0:T(8,128)S(1)}, u32[]{:S(2)}, u32[]{:S(2)}) collective-permute-start(f32[3,128,128]{2,1,0:T(8,128)S(1)} %pack.1.after), channel_id=1, source_target_pairs={{0,16},{1,2},{2,1},{3,4},{4,3},{5,6},{6,5},{7,23},{8,24},{9,10},{1... | collective-permute-start | bytes 589832 | tf_op jit(solution)/shard_map/ppermute | solution.py:419
  4.8 0.0 copy-done.1
  4.8 0.8 %inner.1 = (f32[10,128,128]{2,1,0:T(8,128)S(1)}, f32[64,640]{1,0:T(8,128)S(1)}, f32[3,128,128]{2,1,0:T(8,128)S(1)}) custom-call(f32[16,128,128]{2,1,0:T(8,128)S(1)} %bitcast.2, f32[16,128,128]{2,1,0:T(8,128)S(1)} %copy-done, bf16[256,256]{1,0:T(8,128)(2,1)S(1)} %copy-done.2, bf16[128,256]{1,0:T(8,128)(2,1)S(1)} %copy-done.3, f32[3,128,128]{2,1,0:T(8,128)S(1)} %pack.1.after), custom_call_target="tpu_custom_call" | custom-call | flops 10000000000 | bytes 1000000000 | tf_op jit(solution)/shard_map/inner/pallas_call | solution.py:137
  5.6 1.5 %collective-permute-start.2 = (f32[64,640]{1,0:T(8,128)S(1)}, f32[64,640]{1,0:T(8,128)S(1)}, u32[]{:S(2)}, u32[]{:S(2)}) collective-permute-start(f32[64,640]{1,0:T(8,128)S(1)} %get-tuple-element.28), channel_id=1, source_target_pairs={{0,8},{8,16},{16,24},{24,0},{1,9},{9,17},{17,25},{25,1},{2,10},{10... | collective-permute-start | bytes 491528 | tf_op jit(solution)/shard_map/ppermute | solution.py:414
  7.2 0.0 collective-permute-start
  7.2 1.2 %middle.1 = (f32[4,128,128]{2,1,0:T(8,128)S(1)}, f32[12,128,128]{2,1,0:T(8,128)S(1)}, f32[64,640]{1,0:T(8,128)S(1)}, f32[64,256]{1,0:T(8,128)S(1)}) custom-call(f32[16,128,128]{2,1,0:T(8,128)S(1)} %bitcast.3, f32[16,128,128]{2,1,0:T(8,128)S(1)} %copy-done, bf16[256,256]{1,0:T(8,128)(2,1)S(1)} %copy-done.2, bf16[128,256]{1,0:T(8,128)(2,1)S(1)} %copy-done.3, ...), custom_call_target="tpu_custom_call" | custom-call | tf_op jit(solution)/shard_map/middle/pallas_call | solution.py:137
  8.3 0.1 collective-permute-done.1.from_odd.odd_ref
  8.5 0.1 collective-permute-done.even_ref
  8.6 0.6 %outer.1 = (f32[4,128,128]{2,1,0:T(8,128)S(1)}, f32[4,128,128]{2,1,0:T(8,128)S(1)}, f32[64,512]{1,0:T(8,128)S(1)}) custom-call(f32[16,128,128]{2,1,0:T(8,128)S(1)} %bitcast.4, f32[16,128,128]{2,1,0:T(8,128)S(1)} %copy-done, f32[3,128,128]{2,1,0:T(8,128)S(1)} %collective-permute-done.even_ref, f32[3,128,128]{2,1,0:T(8,128)S(1)} %collective-permute-done.1.from_odd.odd_ref, ...), custom_call_target="tpu_custom_call" | custom-call | flops 10000000000 | bytes 1000000000 | tf_op jit(solution)/shard_map/outer/pallas_call | solution.py:137
  9.2 1.9 %collective-permute-start.3 = (f32[64,512]{1,0:T(8,128)S(1)}, f32[64,512]{1,0:T(8,128)S(1)}, u32[]{:S(2)}, u32[]{:S(2)}) collective-permute-start(f32[64,512]{1,0:T(8,128)S(1)} %get-tuple-element.31), channel_id=1, source_target_pairs={{0,8},{8,16},{16,24},{24,0},{1,9},{9,17},{17,25},{25,1},{2,10},{10... | collective-permute-start | bytes 393224 | tf_op jit(solution)/shard_map/ppermute | solution.py:414
  11.1 0.5 %later.1 = (f32[4,128,128]{2,1,0:T(8,128)S(1)}, f32[64,512]{1,0:T(8,128)S(1)}) custom-call(f32[16,128,128]{2,1,0:T(8,128)S(1)} %bitcast.5, f32[16,128,128]{2,1,0:T(8,128)S(1)} %copy-done, f32[4,128,128]{2,1,0:T(8,128)S(1)} %get-tuple-element.24.ab_ref.refs_1_, f32[4,128,128]{2,1,0:T(8,128)S(1)} %get-tuple-element.25.gb_ref, ...), custom_call_target="tpu_custom_call" | custom-call | flops 10000000000 | bytes 1000000000 | tf_op jit(solution)/shard_map/later/pallas_call | solution.py:137
  11.6 1.3 %collective-permute-done.2.refs_5_.refs_4_ = f32[64,640]{1,0:T(8,128)S(1)} collective-permute-done((f32[64,640]{1,0:T(8,128)S(1)}, f32[64,640]{1,0:T(8,128)S(1)}, u32[]{:S(2)}, u32[]{:S(2)}) %collective-permute-start.2) | collective-permute-done | bytes 163872 | tf_op jit(solution)/shard_map/ppermute | solution.py:414
  12.8 0.8 %second.2 = (f32[10,128,128]{2,1,0:T(8,128)S(1)}, f32[8,128,128]{2,1,0:T(8,128)S(1)}, f32[64,512]{1,0:T(8,128)S(1)}) custom-call(f32[16,128,128]{2,1,0:T(8,128)S(1)} %bitcast.6, f32[4,128,128]{2,1,0:T(8,128)S(1)} %get-tuple-element.24.ab_ref.refs_1_, f32[16,128,128]{2,1,0:T(8,128)S(1)} %copy-done, f32[12,128,128]{2,1,0:T(8,128)S(1)} %get-tuple-element.23.after.refs_3_, ...), custom_call_target="tpu_custom_call" | custom-call | flops 10000000000 | bytes 1000000000 | tf_op jit(solution)/shard_map/second/pallas_call | solution.py:137
  13.6 1.2 %collective-permute-start.5 = (f32[64,512]{1,0:T(8,128)S(1)}, f32[64,512]{1,0:T(8,128)S(1)}, u32[]{:S(2)}, u32[]{:S(2)}) collective-permute-start(f32[64,512]{1,0:T(8,128)S(1)} %get-tuple-element.37), channel_id=1, source_target_pairs={{0,8},{8,16},{16,24},{24,0},{1,9},{9,17},{17,25},{25,1},{2,10},{10... | collective-permute-start | bytes 393224 | tf_op jit(solution)/shard_map/ppermute | solution.py:414
  14.8 1.0 %collective-permute-done.3.refs_5_ = f32[64,512]{1,0:T(8,128)S(1)} collective-permute-done((f32[64,512]{1,0:T(8,128)S(1)}, f32[64,512]{1,0:T(8,128)S(1)}, u32[]{:S(2)}, u32[]{:S(2)}) %collective-permute-start.3) | collective-permute-done | bytes 131104 | tf_op jit(solution)/shard_map/ppermute | solution.py:414
  15.8 0.8 %second.3 = (f32[8,128,128]{2,1,0:T(8,128)S(1)}, f32[8,128,128]{2,1,0:T(8,128)S(1)}, f32[64,512]{1,0:T(8,128)S(1)}) custom-call(f32[16,128,128]{2,1,0:T(8,128)S(1)} %bitcast.7, f32[4,128,128]{2,1,0:T(8,128)S(1)} %get-tuple-element.24.ab_ref.refs_1_, f32[16,128,128]{2,1,0:T(8,128)S(1)} %copy-done, f32[12,128,128]{2,1,0:T(8,128)S(1)} %get-tuple-element.23.after.refs_3_, ...), custom_call_target="tpu_custom_call" | custom-call | flops 10000000000 | bytes 1000000000 | tf_op jit(solution)/shard_map/second/pallas_call | solution.py:137
  16.6 1.2 %collective-permute-start.4 = (f32[64,512]{1,0:T(8,128)S(1)}, f32[64,512]{1,0:T(8,128)S(1)}, u32[]{:S(2)}, u32[]{:S(2)}) collective-permute-start(f32[64,512]{1,0:T(8,128)S(1)} %get-tuple-element.35), channel_id=1, source_target_pairs={{0,8},{8,16},{16,24},{24,0},{1,9},{9,17},{17,25},{25,1},{2,10},{10... | collective-permute-start | bytes 393224 | tf_op jit(solution)/shard_map/ppermute | solution.py:414
  17.8 1.0 %join.1 = f32[1,16,128,128]{3,2,1,0:T(8,128)} custom-call(f32[8,128,128]{2,1,0:T(8,128)S(1)} %get-tuple-element.30.refs_0_, f32[8,128,128]{2,1,0:T(8,128)S(1)} %get-tuple-element.34.refs_1_), custom_call_target="tpu_custom_call" | custom-call | flops 10000000000 | bytes 1000000000 | tf_op jit(solution)/shard_map/join/pallas_call | solution.py:137
  18.8 0.7 %collective-permute-done.5.refs_0_ = f32[64,512]{1,0:T(8,128)S(1)} collective-permute-done((f32[64,512]{1,0:T(8,128)S(1)}, f32[64,512]{1,0:T(8,128)S(1)}, u32[]{:S(2)}, u32[]{:S(2)}) %collective-permute-start.5) | collective-permute-done | bytes 131104 | tf_op jit(solution)/shard_map/ppermute | solution.py:414
  19.5 1.0 %last.2.refs_8_ = f32[1,16,128,128]{3,2,1,0:T(8,128)} custom-call(f32[64,512]{1,0:T(8,128)S(1)} %collective-permute-done.5.refs_0_, bf16[128,192]{1,0:T(8,128)(2,1)S(1)} %copy-done.5, bf16[384,256]{1,0:T(8,128)(2,1)S(1)} %copy-done.4, f32[16,128,128]{2,1,0:T(8,128)S(1)} %bitcast.8, f32[64,640]{1,0:T(8,128)S(1)} %collective-permute-done.2.refs_5_.refs_4_, ...), custom_call_target="tpu_custom_call" | custom-call | flops 10000000000 | bytes 1000000000 | tf_op jit(solution)/shard_map/last/pallas_call | solution.py:137
  20.6 2.0 %collective-permute-done.4.refs_0_ = f32[64,512]{1,0:T(8,128)S(1)} collective-permute-done((f32[64,512]{1,0:T(8,128)S(1)}, f32[64,512]{1,0:T(8,128)S(1)}, u32[]{:S(2)}, u32[]{:S(2)}) %collective-permute-start.4) | collective-permute-done | bytes 131104 | tf_op jit(solution)/shard_map/ppermute | solution.py:414
  (11 shorter events, 0.1 us)
Async XLA Ops:
  0.6 4.2 %copy-start = (f32[16,128,128]{2,1,0:T(8,128)S(1)}, f32[16,128,128]{2,1,0:T(8,128)}, u32[]{:S(2)}) copy-start(f32[16,128,128]{2,1,0:T(8,128)} %refs_2_.5) | copy-start | bytes 3145732
  0.6 4.2 %copy-start.1 = (f32[1,16,128,128]{3,2,1,0:T(8,128)S(1)}, f32[1,16,128,128]{3,2,1,0:T(8,128)}, u32[]{:S(2)}) copy-start(f32[1,16,128,128]{3,2,1,0:T(8,128)} %param.6) | copy-start | bytes 3145732
  0.6 4.2 %copy-start.2 = (bf16[256,256]{1,0:T(8,128)(2,1)S(1)}, bf16[256,256]{1,0:T(8,128)(2,1)}, u32[]{:S(2)}) copy-start(bf16[256,256]{1,0:T(8,128)(2,1)} %constant.8.clone.fz_ref.refs_7_) | copy-start | bytes 393220
  0.7 4.1 %copy-start.3 = (bf16[128,256]{1,0:T(8,128)(2,1)S(1)}, bf16[128,256]{1,0:T(8,128)(2,1)}, u32[]{:S(2)}) copy-start(bf16[128,256]{1,0:T(8,128)(2,1)} %constant.9.clone.fy_ref.refs_8_) | copy-start | bytes 196612
  1.8 6.7 %collective-permute-start.1 = (f32[3,128,128]{2,1,0:T(8,128)S(1)}, f32[3,128,128]{2,1,0:T(8,128)S(1)}, u32[]{:S(2)}, u32[]{:S(2)}) collective-permute-start(f32[3,128,128]{2,1,0:T(8,128)S(1)} %pack.1.after), channel_id=1, source_target_pairs={{0,16},{1,2},{2,1},{3,4},{4,3},{5,6},{6,5},{7,23},{8,24},{9,10},{1... | collective-permute-start | bytes 589832 | tf_op jit(solution)/shard_map/ppermute | solution.py:419
  5.6 7.2 %collective-permute-start.2 = (f32[64,640]{1,0:T(8,128)S(1)}, f32[64,640]{1,0:T(8,128)S(1)}, u32[]{:S(2)}, u32[]{:S(2)}) collective-permute-start(f32[64,640]{1,0:T(8,128)S(1)} %get-tuple-element.28), channel_id=1, source_target_pairs={{0,8},{8,16},{16,24},{24,0},{1,9},{9,17},{17,25},{25,1},{2,10},{10... | collective-permute-start | bytes 491528 | tf_op jit(solution)/shard_map/ppermute | solution.py:414
  7.2 1.4 %collective-permute-start = (f32[3,128,128]{2,1,0:T(8,128)S(1)}, f32[3,128,128]{2,1,0:T(8,128)S(1)}, u32[]{:S(2)}, u32[]{:S(2)}) collective-permute-start(f32[3,128,128]{2,1,0:T(8,128)S(1)} %get-tuple-element.20), channel_id=1, source_target_pairs={{0,1},{1,0},{2,3},{3,2},{4,5},{5,4},{6,7},{7,6},{8,9},{9,8},{10,11... | collective-permute-start | bytes 589832 | tf_op jit(solution)/shard_map/ppermute | solution.py:431
  9.2 6.6 %collective-permute-start.3 = (f32[64,512]{1,0:T(8,128)S(1)}, f32[64,512]{1,0:T(8,128)S(1)}, u32[]{:S(2)}, u32[]{:S(2)}) collective-permute-start(f32[64,512]{1,0:T(8,128)S(1)} %get-tuple-element.31), channel_id=1, source_target_pairs={{0,8},{8,16},{16,24},{24,0},{1,9},{9,17},{17,25},{25,1},{2,10},{10... | collective-permute-start | bytes 393224 | tf_op jit(solution)/shard_map/ppermute | solution.py:414
  11.1 1.7 %copy-start.4 = (bf16[384,256]{1,0:T(8,128)(2,1)S(1)}, bf16[384,256]{1,0:T(8,128)(2,1)}, u32[]{:S(2)}) copy-start(bf16[384,256]{1,0:T(8,128)(2,1)} %constant.11.clone.refs_10_.refs_2_) | copy-start | bytes 589828
  11.1 1.7 %copy-start.5 = (bf16[128,192]{1,0:T(8,128)(2,1)S(1)}, bf16[128,192]{1,0:T(8,128)(2,1)}, u32[]{:S(2)}) copy-start(bf16[128,192]{1,0:T(8,128)(2,1)} %constant.10.clone.refs_9_.refs_1_) | copy-start | bytes 147460
  13.6 5.9 %collective-permute-start.5 = (f32[64,512]{1,0:T(8,128)S(1)}, f32[64,512]{1,0:T(8,128)S(1)}, u32[]{:S(2)}, u32[]{:S(2)}) collective-permute-start(f32[64,512]{1,0:T(8,128)S(1)} %get-tuple-element.37), channel_id=1, source_target_pairs={{0,8},{8,16},{16,24},{24,0},{1,9},{9,17},{17,25},{25,1},{2,10},{10... | collective-permute-start | bytes 393224 | tf_op jit(solution)/shard_map/ppermute | solution.py:414
  16.6 5.9 %collective-permute-start.4 = (f32[64,512]{1,0:T(8,128)S(1)}, f32[64,512]{1,0:T(8,128)S(1)}, u32[]{:S(2)}, u32[]{:S(2)}) collective-permute-start(f32[64,512]{1,0:T(8,128)S(1)} %get-tuple-element.35), channel_id=1, source_target_pairs={{0,8},{8,16},{16,24},{24,0},{1,9},{9,17},{17,25},{25,1},{2,10},{10... | collective-permute-start | bytes 393224 | tf_op jit(solution)/shard_map/ppermute | solution.py:414

commit v8 on v7

--- a/solution.py
+++ b/solution.py
@@ -98,6 +98,17 @@
 
 def rate(below, v, above, mobility):
     return mobility * (neighbours(v) + (below + above) - v * (5.0 + v * v))
+
+
+def analyse_small(pairs, fz_ref, fy_ref):
+    ny = pairs[0][0].shape[0]
+    width = 2 * KZ
+    rows = [jnp.concatenate([first.astype(BF16), second.astype(BF16)], axis=1) for first, second in pairs]
+    half = dot(jnp.concatenate(rows, axis=0), fz_ref[...])
+    half = (half[:, :width] + half[:, width:]).astype(BF16)
+    columns = [half[i * ny : (i + 1) * ny] for i in range(len(pairs))]
+    coeffs = dot(fy_ref[:, :ny], jnp.concatenate(columns, axis=1))
+    return coeffs[:KY] + coeffs[KY:]
 
 
 def analyse(pairs, fz_ref, fy_ref):
@@ -222,30 +233,34 @@
     return h * (W[0] * g + mobility * (h * W[1] * laplace - cube))
 
 
-def middle_kernel(a_ref, mu_ref, fz_ref, fy_ref, *refs):
+def middle_kernel(a_ref, mu_ref, fz_ref, fy_ref, after, g_ref, c_ref, *own_refs):
     nx = a_ref.shape[0]
     first = chunks(nx)[0]
-    early = [planes_of(part, -1) for part in first[:-1]]
-    g_refs, (g_ref, acc_ref), own_refs = refs[: len(early)], refs[len(early) : len(early) + 2], refs[len(early) + 2 :]
-    rest = planes_of(first[-1][1:-1], -1)
-    for i, p in enumerate(rest):
-        g_ref[i] = rate(a_ref[p - 1], a_ref[p], a_ref[p + 1], mu_ref[p])
-    rates = reader(*zip(g_refs, early), (g_ref, rest))
+    ends = []
+    for i, p in enumerate(planes_of(first[-1][1:-1], -1)):
+        g = rate(a_ref[p - 1], a_ref[p], a_ref[p + 1], mu_ref[p])
+        g_ref[i] = g
+        ends.append(a_ref[p] + time_step * g)
     inner = sum(first[:-1], []) + first[-1][1:-1]
-    coeffs = analyse([(a_ref[p - 1], a_ref[p]) for p in planes_of(inner, -1)[1::2]], fz_ref, fy_ref)
+    coeffs = analyse(by_pairs(ends) + [(a_ref[p - 1], a_ref[p]) for p in planes_of(inner, -1)[1::2]], fz_ref, fy_ref)
     start = 0
-    for ref in own_refs:
+    for ref in (c_ref, *own_refs):
         ref[...] = coeffs[:, start : start + ref.shape[1]]
         start += ref.shape[1]
-    for p in range(2, nx - 2):
-        acc_ref[p - 2] = later_part(rates(p - 1), rates(p), rates(p + 1), a_ref[p], mu_ref[p])
+
+
+def ends_between(c_ref, outer, rest_ref):
+    width = 2 * KZ
+    c_ref[:, :width] = outer[:, :width]
+    c_ref[:, width : c_ref.shape[1] - width] = rest_ref[...]
+    c_ref[:, c_ref.shape[1] - width :] = outer[:, width:]
 
 
 def mark_kernel(from_odd, after, out_ref):
     out_ref[...] = jnp.zeros_like(out_ref)
 
 
-def outer_kernel(a_ref, mu_ref, even_ref, odd_ref, g_ref, fz_ref, fy_ref, after, a_out, g_out, c_ref):
+def outer_kernel(a_ref, mu_ref, even_ref, odd_ref, rest_ref, fz_ref, fy_ref, after, a_out, g_out, c_ref):
     nx = a_ref.shape[0]
     even = is_even()
     place = lax.axis_index("gx")
@@ -267,24 +282,20 @@
         a_out[i] = values[i]
         g_out[i] = rates[i]
     outer = [v + time_step * g for v, g in zip(values, rates)]
-    rest = planes_of(chunks(nx)[0][-1][1:-1], -1)
-    inner = [a_ref[p] + time_step * g_ref[i] for i, p in enumerate(rest)]
-    c_ref[...] = analyse(by_pairs(outer[:2] + inner + outer[2:]), fz_ref, fy_ref)
-
-
-def later_kernel(a_ref, mu_ref, ab_ref, gb_ref, low_ref, high_ref, rest_ref, fz_ref, fy_ref, acc_ref, c_ref):
+    ends_between(c_ref, analyse(by_pairs(outer), fz_ref, fy_ref), rest_ref)
+
+
+def later_kernel(a_ref, mu_ref, ab_ref, gb_ref, rest_ref, fz_ref, fy_ref, *refs):
+    g_refs, (acc_ref, c_ref, cacc_ref) = refs[:-3], refs[-3:]
     nx = a_ref.shape[0]
     first = chunks(nx)[0]
-    rates = reader(
-        (gb_ref, outer_planes(nx)), (low_ref, planes_of(first[0], -1)), (high_ref, planes_of(first[-1][1:-1], -1))
-    )
-    own = analyse([(ab_ref[0], ab_ref[1]), (ab_ref[2], ab_ref[3])], fz_ref, fy_ref)
-    width = 2 * KZ
-    c_ref[:, :width] = own[:, :width]
-    c_ref[:, width : c_ref.shape[1] - width] = rest_ref[...]
-    c_ref[:, c_ref.shape[1] - width :] = own[:, width:]
-    for i, p in enumerate((0, 1, nx - 2, nx - 1)):
-        acc_ref[i] = later_part(rates(p - 1), rates(p), rates(p + 1), a_ref[p], mu_ref[p])
+    inner = [planes_of(part, -1) for part in (*first[:-1], first[-1][1:-1])]
+    rates = reader((gb_ref, outer_planes(nx)), *zip(g_refs, inner))
+    ends_between(c_ref, analyse([(ab_ref[0], ab_ref[1]), (ab_ref[2], ab_ref[3])], fz_ref, fy_ref), rest_ref)
+    for p in range(nx):
+        acc_ref[p] = later_part(rates(p - 1), rates(p), rates(p + 1), a_ref[p], mu_ref[p])
+    planes = planes_of(chunks(nx)[1][-1], 0)
+    cacc_ref[...] = analyse(by_pairs([acc_ref[p] for p in planes]), fz_ref, fy_ref)
 
 
 def received(c, own):
@@ -292,8 +303,10 @@
 
 
 def second_kernel(stage, *refs):
-    a_ref, ab_ref, mu_ref, acc_ref, accb_ref, c1_ref, own_ref, fz_ref, fy_ref, by_ref, bz_ref = refs[:11]
-    earlier, (a1_ref, e_ref, c2_ref) = refs[11:-3], refs[-3:]
+    a_ref, ab_ref, mu_ref, acc_ref, c1_ref, own_ref, fz_ref, fy_ref, by_ref, bz_ref = refs[:10]
+    earlier, (a1_ref, e_ref, c2_ref) = refs[10:-3], refs[-3:]
+    if stage == 1:
+        earlier, (cacc_ref, c1_first_ref, own_first_ref) = earlier[:1], earlier[1:]
     nx, ny, nz = mu_ref.shape
     first, second = chunks(nx)
     before = reader((a_ref, range(nx)), (ab_ref, outer_planes(nx)))
@@ -311,14 +324,22 @@
             a1_ref[i] = before(p)
 
     values = reader(*[(ref, planes_of(part, -1)) for ref, part in zip((*earlier, a1_ref), first)])
-    parts = reader((acc_ref, range(2, nx - 2)), (accb_ref, (0, 1, nx - 2, nx - 1)))
-    ends = []
-    for i, p in enumerate(planes_of(second[stage], 0)):
-        v = values(p)
-        e = v + time_step * LAST_ROW[0] * rate(values(p - 1), v, values(p + 1), mu_ref[p]) + parts(p)
+    planes = planes_of(second[stage], 0)
+    fresh = [rate(values(p - 1), values(p), values(p + 1), mu_ref[p]) for p in planes]
+    weight = time_step * LAST_ROW[0]
+    ends = [values(p) + weight * f + acc_ref[p] for p, f in zip(planes, fresh)]
+    for i, e in enumerate(ends):
         e_ref[i] = e
-        ends.append(e)
-    c2_ref[...] = analyse(by_pairs(ends), fz_ref, fy_ref)
+    if stage == 0:
+        c2_ref[...] = analyse(by_pairs(ends), fz_ref, fy_ref)
+        return
+    where = {}
+    for c, own, part in ((c1_first_ref, own_first_ref, first[0]), (c1_ref, own_ref, first[1])):
+        own_start = jnp.where(receives, c[...], own[...])
+        for i, p in enumerate(planes_of(part, -1)):
+            where[p] = own_start[:, i * KZ : (i + 1) * KZ]
+    known = jnp.concatenate([where[p] for p in planes], axis=1) + cacc_ref[...]
+    c2_ref[...] = known + weight * analyse_small(by_pairs(fresh), fz_ref, fy_ref)
 
 
 def last_kernel(stage, count, *refs):
@@ -407,7 +428,7 @@
             if 0 <= other < slabs:
                 odd_pairs.append((s * slabs + g, s * slabs + other))
             else:
-                odd_pairs.append((s * slabs + g, (s ^ 2) * slabs + g))
+                odd_pairs.append((s * slabs + g, (s ^ (1 if g else 2)) * slabs + g))
     ring = [(s, (s + 1) % slices) for s in range(slices)]
 
     def onward(c):
@@ -430,19 +451,20 @@
         if stage == 0:
             from_even = lax.ppermute(to_even[0], ("tm", "gx"), even_pairs)
     rest = first[-1][1:-1]
-    g_rest, acc, *own, own_rest = call(
+    g_rest, c_rest, *own, own_rest = call(
         middle_kernel,
-        [grid(2 * len(rest)), grid(nx - 4), *[modes(part) for part in first[:-1]], modes(rest)],
+        [grid(2 * len(rest)), modes(rest), *[modes(part) for part in first[:-1]], modes(rest)],
         "middle",
+        specs=[VMEM] * 4 + [ANY],
         cost=0,
-    )(a, mu, fz, fy, *g)
-    mark = call(mark_kernel, jax.ShapeDtypeStruct((8, 128), F32), "mark", specs=[ANY, ANY])(from_odd, acc)
+    )(a, mu, fz, fy, g[-1])
+    mark = call(mark_kernel, jax.ShapeDtypeStruct((8, 128), F32), "mark", specs=[ANY, ANY])(from_odd, own_rest)
     ab, gb, c = call(outer_kernel, [grid(4), grid(4), modes(first[-1])], "outer", specs=[VMEM] * 7 + [ANY])(
-        a, mu, from_even, from_odd, g_rest, fz, fy, mark
+        a, mu, from_even, from_odd, c_rest, fz, fy, mark
     )
     c1.append(onward(c))
-    accb, own_last = call(later_kernel, [grid(4), modes(first[-1])], "later")(
-        a, mu, ab, gb, g[0], g_rest, own_rest, fz, fy
+    acc, own_last, cacc = call(later_kernel, [grid(nx), modes(first[-1]), modes(second[-1])], "later")(
+        a, mu, ab, gb, own_rest, fz, fy, *g, g_rest
     )
     own.append(own_last)
     a1, e, c2 = [], [], []
@@ -451,7 +473,7 @@
             functools.partial(second_kernel, stage),
             [grid(2 * len(first[stage])), grid(2 * len(second[stage])), modes(second[stage])],
             "second",
-        )(a, ab, mu, acc, accb, c1[stage], own[stage], fz, fy, by, bz, *a1)
+        )(a, ab, mu, acc, c1[stage], own[stage], fz, fy, by, bz, *a1, *([cacc, c1[0], own[0]] if stage else []))
         a1.append(values)
         e.append(end)
         c2.append(onward(c))

time: 22.7 us -> 22.7 us (level)
  waiting for transfers between devices: 5.24 us -> 4.33 us
  starting transfers between devices: 8.85 us -> 9.38 us
    ppermute x4, waiting for transfers between devices: 4.98 us -> 3.65 us  [onward(): return lax.ppermute(c, 'tm', ring)]
    ppermute x4, starting transfers between devices: 5.82 us -> 6.35 us  [onward(): return lax.ppermute(c, 'tm', ring)]
    ppermute x1, waiting for transfers between devices: 0.1 us -> 0.54 us  [body(): from_odd = lax.ppermute(to_odd, ('tm', 'gx'), odd_pairs)]
  transfers between devices with their start and end apart: 6 -> 6, of which waited for: 6 -> 6; matrix products, arithmetic and copies ran while one was open for 0% -> 0% of each run, Pallas kernels for 29% -> 30%
where the time goes in v8:
time: 22.7 us; the launch traced here: 22.4 us
  starting transfers between devices  9.38 us (41%)
  Pallas kernels  7.91 us (35%)
  waiting for transfers between devices  4.33 us (19%)
  between operations  0.73 us (3%)
    pallas_call x11, Pallas kernels, run(): pl.pallas_call(kernel, out_shape=outs, in_specs=specs or [VMEM] * len(arg...  7.91 us
    ppermute x4, starting transfers between devices, onward(): return lax.ppermute(c, 'tm', ring)  6.35 us
    ppermute x4, waiting for transfers between devices, onward(): return lax.ppermute(c, 'tm', ring)  3.65 us
    ppermute x1, starting transfers between devices, body(): from_odd = lax.ppermute(to_odd, ('tm', 'gx'), odd_pairs)  3.03 us
    ppermute x1, waiting for transfers between devices, body(): from_odd = lax.ppermute(to_odd, ('tm', 'gx'), odd_pairs)  0.54 us
  transfers between devices with their start and end apart: 6, of which 6 were waited for; matrix products, arithmetic and copies ran while one was open for 0% of the time, Pallas kernels for 30%

profile of v8, /device:TPU:0, one launch (start us, length us, event | category | flops | bytes accessed | tf_op | source)
XLA Modules:
  0.0 22.4 jit_solution(2247702754677174590)
XLA Ops:
  0.6 0.0 copy-start.2
  0.7 0.0 copy-start.3
  0.7 1.1 %pack.1.after = f32[3,128,128]{2,1,0:T(8,128)S(1)} custom-call(f32[16,128,128]{2,1,0:T(8,128)} %bitcast.1, f32[16,128,128]{2,1,0:T(8,128)} %refs_2_.5), custom_call_target="tpu_custom_call" | custom-call | flops 10000000000 | bytes 1000000000 | tf_op jit(solution)/shard_map/pack/pallas_call | solution.py:148
  1.8 3.0 %collective-permute-start.1 = (f32[3,128,128]{2,1,0:T(8,128)S(1)}, f32[3,128,128]{2,1,0:T(8,128)S(1)}, u32[]{:S(2)}, u32[]{:S(2)}) collective-permute-start(f32[3,128,128]{2,1,0:T(8,128)S(1)} %pack.1.after), channel_id=1, source_target_pairs={{0,16},{1,2},{2,1},{3,4},{4,3},{5,6},{6,5},{7,15},{8,24},{9,10},{1... | collective-permute-start | bytes 589832 | tf_op jit(solution)/shard_map/ppermute | solution.py:440
  4.8 0.0 copy-done
  4.8 0.8 %inner.1 = (f32[10,128,128]{2,1,0:T(8,128)S(1)}, f32[64,640]{1,0:T(8,128)S(1)}, f32[3,128,128]{2,1,0:T(8,128)S(1)}) custom-call(f32[16,128,128]{2,1,0:T(8,128)S(1)} %bitcast.2, f32[16,128,128]{2,1,0:T(8,128)S(1)} %copy-done, bf16[256,256]{1,0:T(8,128)(2,1)S(1)} %copy-done.2, bf16[128,256]{1,0:T(8,128)(2,1)S(1)} %copy-done.3, f32[3,128,128]{2,1,0:T(8,128)S(1)} %pack.1.after), custom_call_target="tpu_custom_call" | custom-call | flops 10000000000 | bytes 1000000000 | tf_op jit(solution)/shard_map/inner/pallas_call | solution.py:148
  5.6 1.5 %collective-permute-start.2 = (f32[64,640]{1,0:T(8,128)S(1)}, f32[64,640]{1,0:T(8,128)S(1)}, u32[]{:S(2)}, u32[]{:S(2)}) collective-permute-start(f32[64,640]{1,0:T(8,128)S(1)} %get-tuple-element.29), channel_id=1, source_target_pairs={{0,8},{8,16},{16,24},{24,0},{1,9},{9,17},{17,25},{25,1},{2,10},{10... | collective-permute-start | bytes 491528 | tf_op jit(solution)/shard_map/ppermute | solution.py:435
  7.2 0.0 collective-permute-start
  7.2 0.7 %middle.1 = (f32[4,128,128]{2,1,0:T(8,128)S(1)}, f32[64,256]{1,0:T(8,128)S(1)}, f32[64,640]{1,0:T(8,128)S(1)}, f32[64,256]{1,0:T(8,128)S(1)}) custom-call(f32[16,128,128]{2,1,0:T(8,128)S(1)} %bitcast.3, f32[16,128,128]{2,1,0:T(8,128)S(1)} %copy-done, bf16[256,256]{1,0:T(8,128)(2,1)S(1)} %copy-done.2, bf16[128,256]{1,0:T(8,128)(2,1)S(1)} %copy-done.3, ...), custom_call_target="tpu_custom_call" | custom-call | tf_op jit(solution)/shard_map/middle/pallas_call | solution.py:148
  7.9 0.5 %collective-permute-done.1.from_odd.odd_ref = f32[3,128,128]{2,1,0:T(8,128)S(1)} collective-permute-done((f32[3,128,128]{2,1,0:T(8,128)S(1)}, f32[3,128,128]{2,1,0:T(8,128)S(1)}, u32[]{:S(2)}, u32[]{:S(2)}) %collective-permute-start.1) | collective-permute-done | bytes 196640 | tf_op jit(solution)/shard_map/ppermute | solution.py:440
  8.5 0.1 collective-permute-done.even_ref
  8.6 0.5 %outer.1 = (f32[4,128,128]{2,1,0:T(8,128)S(1)}, f32[4,128,128]{2,1,0:T(8,128)S(1)}, f32[64,512]{1,0:T(8,128)S(1)}) custom-call(f32[16,128,128]{2,1,0:T(8,128)S(1)} %bitcast.4, f32[16,128,128]{2,1,0:T(8,128)S(1)} %copy-done, f32[3,128,128]{2,1,0:T(8,128)S(1)} %collective-permute-done.even_ref, f32[3,128,128]{2,1,0:T(8,128)S(1)} %collective-permute-done.1.from_odd.odd_ref, ...), custom_call_target="tpu_custom_call" | custom-call | flops 10000000000 | bytes 1000000000 | tf_op jit(solution)/shard_map/outer/pallas_call | solution.py:148
  9.2 1.9 %collective-permute-start.3 = (f32[64,512]{1,0:T(8,128)S(1)}, f32[64,512]{1,0:T(8,128)S(1)}, u32[]{:S(2)}, u32[]{:S(2)}) collective-permute-start(f32[64,512]{1,0:T(8,128)S(1)} %get-tuple-element.32), channel_id=1, source_target_pairs={{0,8},{8,16},{16,24},{24,0},{1,9},{9,17},{17,25},{25,1},{2,10},{10... | collective-permute-start | bytes 393224 | tf_op jit(solution)/shard_map/ppermute | solution.py:435
  11.1 1.2 %later.1 = (f32[16,128,128]{2,1,0:T(8,128)S(1)}, f32[64,512]{1,0:T(8,128)S(1)}, f32[64,512]{1,0:T(8,128)S(1)}) custom-call(f32[16,128,128]{2,1,0:T(8,128)S(1)} %bitcast.5, f32[16,128,128]{2,1,0:T(8,128)S(1)} %copy-done, f32[4,128,128]{2,1,0:T(8,128)S(1)} %get-tuple-element.25.ab_ref.refs_1_, f32[4,128,128]{2,1,0:T(8,128)S(1)} %get-tuple-element.26.gb_ref, ...), custom_call_target="tpu_custom_call" | custom-call | flops 10000000000 | bytes 1000000000 | tf_op jit(solution)/shard_map/later/pallas_call | solution.py:148
  12.3 0.6 %collective-permute-done.2.refs_4_.refs_12_ = f32[64,640]{1,0:T(8,128)S(1)} collective-permute-done((f32[64,640]{1,0:T(8,128)S(1)}, f32[64,640]{1,0:T(8,128)S(1)}, u32[]{:S(2)}, u32[]{:S(2)}) %collective-permute-start.2) | collective-permute-done | bytes 163872 | tf_op jit(solution)/shard_map/ppermute | solution.py:435
  12.8 0.8 %second.2 = (f32[10,128,128]{2,1,0:T(8,128)S(1)}, f32[8,128,128]{2,1,0:T(8,128)S(1)}, f32[64,512]{1,0:T(8,128)S(1)}) custom-call(f32[16,128,128]{2,1,0:T(8,128)S(1)} %bitcast.6, f32[4,128,128]{2,1,0:T(8,128)S(1)} %get-tuple-element.25.ab_ref.refs_1_, f32[16,128,128]{2,1,0:T(8,128)S(1)} %copy-done, f32[16,128,128]{2,1,0:T(8,128)S(1)} %get-tuple-element.28.refs_3_, ...), custom_call_target="tpu_custom_call" | custom-call | flops 10000000000 | bytes 1000000000 | tf_op jit(solution)/shard_map/second/pallas_call | solution.py:148
  13.6 1.5 %collective-permute-start.5 = (f32[64,512]{1,0:T(8,128)S(1)}, f32[64,512]{1,0:T(8,128)S(1)}, u32[]{:S(2)}, u32[]{:S(2)}) collective-permute-start(f32[64,512]{1,0:T(8,128)S(1)} %get-tuple-element.39), channel_id=1, source_target_pairs={{0,8},{8,16},{16,24},{24,0},{1,9},{9,17},{17,25},{25,1},{2,10},{10... | collective-permute-start | bytes 393224 | tf_op jit(solution)/shard_map/ppermute | solution.py:435
  15.1 0.5 %collective-permute-done.3.refs_4_.refs_5_ = f32[64,512]{1,0:T(8,128)S(1)} collective-permute-done((f32[64,512]{1,0:T(8,128)S(1)}, f32[64,512]{1,0:T(8,128)S(1)}, u32[]{:S(2)}, u32[]{:S(2)}) %collective-permute-start.3) | collective-permute-done | bytes 131104 | tf_op jit(solution)/shard_map/ppermute | solution.py:435
  15.7 0.7 %second.3 = (f32[8,128,128]{2,1,0:T(8,128)S(1)}, f32[8,128,128]{2,1,0:T(8,128)S(1)}, f32[64,512]{1,0:T(8,128)S(1)}) custom-call(f32[16,128,128]{2,1,0:T(8,128)S(1)} %bitcast.7, f32[4,128,128]{2,1,0:T(8,128)S(1)} %get-tuple-element.25.ab_ref.refs_1_, f32[16,128,128]{2,1,0:T(8,128)S(1)} %copy-done, f32[16,128,128]{2,1,0:T(8,128)S(1)} %get-tuple-element.28.refs_3_, ...), custom_call_target="tpu_custom_call" | custom-call | flops 10000000000 | bytes 1000000000 | tf_op jit(solution)/shard_map/second/pallas_call | solution.py:148
  16.4 1.4 %collective-permute-start.4 = (f32[64,512]{1,0:T(8,128)S(1)}, f32[64,512]{1,0:T(8,128)S(1)}, u32[]{:S(2)}, u32[]{:S(2)}) collective-permute-start(f32[64,512]{1,0:T(8,128)S(1)} %get-tuple-element.37), channel_id=1, source_target_pairs={{0,8},{8,16},{16,24},{24,0},{1,9},{9,17},{17,25},{25,1},{2,10},{10... | collective-permute-start | bytes 393224 | tf_op jit(solution)/shard_map/ppermute | solution.py:435
  17.8 1.0 %join.1 = f32[1,16,128,128]{3,2,1,0:T(8,128)} custom-call(f32[8,128,128]{2,1,0:T(8,128)S(1)} %get-tuple-element.31.refs_0_, f32[8,128,128]{2,1,0:T(8,128)S(1)} %get-tuple-element.36.refs_1_), custom_call_target="tpu_custom_call" | custom-call | flops 10000000000 | bytes 1000000000 | tf_op jit(solution)/shard_map/join/pallas_call | solution.py:148
  18.8 1.1 %collective-permute-done.5.refs_0_ = f32[64,512]{1,0:T(8,128)S(1)} collective-permute-done((f32[64,512]{1,0:T(8,128)S(1)}, f32[64,512]{1,0:T(8,128)S(1)}, u32[]{:S(2)}, u32[]{:S(2)}) %collective-permute-start.5) | collective-permute-done | bytes 131104 | tf_op jit(solution)/shard_map/ppermute | solution.py:435
  19.9 1.0 %last.2.refs_8_ = f32[1,16,128,128]{3,2,1,0:T(8,128)} custom-call(f32[64,512]{1,0:T(8,128)S(1)} %collective-permute-done.5.refs_0_, bf16[128,192]{1,0:T(8,128)(2,1)S(1)} %copy-done.5, bf16[384,256]{1,0:T(8,128)(2,1)S(1)} %copy-done.4, f32[16,128,128]{2,1,0:T(8,128)S(1)} %bitcast.8, f32[64,640]{1,0:T(8,128)S(1)} %collective-permute-done.2.refs_4_.refs_12_, ...), custom_call_target="tpu_custom_call" | custom-call | flops 10000000000 | bytes 1000000000 | tf_op jit(solution)/shard_map/last/pallas_call | solution.py:148
  20.9 1.5 %collective-permute-done.4.refs_0_ = f32[64,512]{1,0:T(8,128)S(1)} collective-permute-done((f32[64,512]{1,0:T(8,128)S(1)}, f32[64,512]{1,0:T(8,128)S(1)}, u32[]{:S(2)}, u32[]{:S(2)}) %collective-permute-start.4) | collective-permute-done | bytes 131104 | tf_op jit(solution)/shard_map/ppermute | solution.py:435
  (11 shorter events, 0.1 us)
Async XLA Ops:
  0.6 4.2 %copy-start = (f32[16,128,128]{2,1,0:T(8,128)S(1)}, f32[16,128,128]{2,1,0:T(8,128)}, u32[]{:S(2)}) copy-start(f32[16,128,128]{2,1,0:T(8,128)} %refs_2_.5) | copy-start | bytes 3145732
  0.6 4.2 %copy-start.1 = (f32[1,16,128,128]{3,2,1,0:T(8,128)S(1)}, f32[1,16,128,128]{3,2,1,0:T(8,128)}, u32[]{:S(2)}) copy-start(f32[1,16,128,128]{3,2,1,0:T(8,128)} %param.6) | copy-start | bytes 3145732
  0.6 4.2 %copy-start.2 = (bf16[256,256]{1,0:T(8,128)(2,1)S(1)}, bf16[256,256]{1,0:T(8,128)(2,1)}, u32[]{:S(2)}) copy-start(bf16[256,256]{1,0:T(8,128)(2,1)} %constant.8.clone.fz_ref.refs_6_) | copy-start | bytes 393220
  0.7 4.1 %copy-start.3 = (bf16[128,256]{1,0:T(8,128)(2,1)S(1)}, bf16[128,256]{1,0:T(8,128)(2,1)}, u32[]{:S(2)}) copy-start(bf16[128,256]{1,0:T(8,128)(2,1)} %constant.9.clone.fy_ref.refs_7_) | copy-start | bytes 196612
  1.8 6.7 %collective-permute-start.1 = (f32[3,128,128]{2,1,0:T(8,128)S(1)}, f32[3,128,128]{2,1,0:T(8,128)S(1)}, u32[]{:S(2)}, u32[]{:S(2)}) collective-permute-start(f32[3,128,128]{2,1,0:T(8,128)S(1)} %pack.1.after), channel_id=1, source_target_pairs={{0,16},{1,2},{2,1},{3,4},{4,3},{5,6},{6,5},{7,15},{8,24},{9,10},{1... | collective-permute-start | bytes 589832 | tf_op jit(solution)/shard_map/ppermute | solution.py:440
  5.6 7.2 %collective-permute-start.2 = (f32[64,640]{1,0:T(8,128)S(1)}, f32[64,640]{1,0:T(8,128)S(1)}, u32[]{:S(2)}, u32[]{:S(2)}) collective-permute-start(f32[64,640]{1,0:T(8,128)S(1)} %get-tuple-element.29), channel_id=1, source_target_pairs={{0,8},{8,16},{16,24},{24,0},{1,9},{9,17},{17,25},{25,1},{2,10},{10... | collective-permute-start | bytes 491528 | tf_op jit(solution)/shard_map/ppermute | solution.py:435
  7.2 1.4 %collective-permute-start = (f32[3,128,128]{2,1,0:T(8,128)S(1)}, f32[3,128,128]{2,1,0:T(8,128)S(1)}, u32[]{:S(2)}, u32[]{:S(2)}) collective-permute-start(f32[3,128,128]{2,1,0:T(8,128)S(1)} %get-tuple-element.21), channel_id=1, source_target_pairs={{0,1},{1,0},{2,3},{3,2},{4,5},{5,4},{6,7},{7,6},{8,9},{9,8},{10,11... | collective-permute-start | bytes 589832 | tf_op jit(solution)/shard_map/ppermute | solution.py:452
  9.2 6.5 %collective-permute-start.3 = (f32[64,512]{1,0:T(8,128)S(1)}, f32[64,512]{1,0:T(8,128)S(1)}, u32[]{:S(2)}, u32[]{:S(2)}) collective-permute-start(f32[64,512]{1,0:T(8,128)S(1)} %get-tuple-element.32), channel_id=1, source_target_pairs={{0,8},{8,16},{16,24},{24,0},{1,9},{9,17},{17,25},{25,1},{2,10},{10... | collective-permute-start | bytes 393224 | tf_op jit(solution)/shard_map/ppermute | solution.py:435
  11.1 1.8 %copy-start.4 = (bf16[384,256]{1,0:T(8,128)(2,1)S(1)}, bf16[384,256]{1,0:T(8,128)(2,1)}, u32[]{:S(2)}) copy-start(bf16[384,256]{1,0:T(8,128)(2,1)} %constant.11.clone.refs_9_.refs_2_) | copy-start | bytes 589828
  11.1 1.8 %copy-start.5 = (bf16[128,192]{1,0:T(8,128)(2,1)S(1)}, bf16[128,192]{1,0:T(8,128)(2,1)}, u32[]{:S(2)}) copy-start(bf16[128,192]{1,0:T(8,128)(2,1)} %constant.10.clone.refs_8_.refs_1_) | copy-start | bytes 147460
  13.6 6.2 %collective-permute-start.5 = (f32[64,512]{1,0:T(8,128)S(1)}, f32[64,512]{1,0:T(8,128)S(1)}, u32[]{:S(2)}, u32[]{:S(2)}) collective-permute-start(f32[64,512]{1,0:T(8,128)S(1)} %get-tuple-element.39), channel_id=1, source_target_pairs={{0,8},{8,16},{16,24},{24,0},{1,9},{9,17},{17,25},{25,1},{2,10},{10... | collective-permute-start | bytes 393224 | tf_op jit(solution)/shard_map/ppermute | solution.py:435
  16.4 6.0 %collective-permute-start.4 = (f32[64,512]{1,0:T(8,128)S(1)}, f32[64,512]{1,0:T(8,128)S(1)}, u32[]{:S(2)}, u32[]{:S(2)}) collective-permute-start(f32[64,512]{1,0:T(8,128)S(1)} %get-tuple-element.37), channel_id=1, source_target_pairs={{0,8},{8,16},{16,24},{24,0},{1,9},{9,17},{17,25},{25,1},{2,10},{10... | collective-permute-start | bytes 393224 | tf_op jit(solution)/shard_map/ppermute | solution.py:435

commit v9 on v7

--- a/solution.py
+++ b/solution.py
@@ -323,27 +323,17 @@
 
 def last_kernel(stage, count, *refs):
     c2_ref, by_ref, bz_ref, a_ref = refs[:4]
-    c1_refs, a1_refs = refs[4 : 4 + count], refs[4 + count : 4 + 2 * count]
+    before_ref, a1_refs = refs[4], refs[5 : 5 + count]
     out_ref, buffer, sems = refs[-3:]
     nx, ny, nz = out_ref.shape[1:]
     first, second = chunks(nx)
-    where = {}
-    for ref, part in zip(c1_refs, first):
-        for i, p in enumerate(planes_of(part, -1)):
-            where[p] = (ref, i)
-
-    def column(p):
-        ref, i = where[p]
-        return ref[:, i * KZ : (i + 1) * KZ]
-
     receives = lax.axis_index("tm") > 0
 
     @pl.when(receives)
     def _():
         values = reader(*[(ref, planes_of(part, -1)) for ref, part in zip(a1_refs, first)])
         planes = planes_of(second[stage], 0)
-        before = jnp.concatenate([column(p) for p in planes], axis=1)
-        change = synthesise(c2_ref[...] - before, by_ref, bz_ref)
+        change = synthesise(c2_ref[...] - before_ref[...], by_ref, bz_ref)
         copies = []
         for i in range(0, len(planes), 2):
             for k in (0, 1):
@@ -371,16 +361,24 @@
                 copy.wait()
 
 
-def join_kernel(*refs):
-    parts, out_ref, sems = refs[:-2], refs[-2], refs[-1]
+def join_kernel(count, *refs):
+    parts, c1_refs = refs[:count], refs[count : 2 * count]
+    out_ref, before_refs, sems = refs[2 * count], refs[2 * count + 1 : -1], refs[-1]
+    first, second = chunks(out_ref.shape[1])
     copies = []
-    for ref, part in zip(parts, chunks(out_ref.shape[1])[1]):
+    for ref, part in zip(parts, second):
         for i, p in enumerate(planes_of(part, 0)[::2]):
             copies.append(
                 pltpu.make_async_copy(ref.at[pl.ds(2 * i, 2)], out_ref.at[0, pl.ds(p, 2)], sems.at[len(copies)])
             )
     for copy in copies:
         copy.start()
+    columns = {}
+    for ref, part in zip(c1_refs, first):
+        for i, p in enumerate(planes_of(part, -1)):
+            columns[p] = ref[:, i * KZ : (i + 1) * KZ]
+    for ref, part in zip(before_refs, second):
+        ref[...] = jnp.concatenate([columns[p] for p in planes_of(part, 0)], axis=1)
     for copy in copies:
         copy.wait()
 
@@ -456,14 +454,14 @@
         e.append(end)
         c2.append(onward(c))
     whole = jax.ShapeDtypeStruct((1, nx, ny, nz), F32)
-    end_state = call(
-        join_kernel,
-        whole,
+    end_state, *before = call(
+        functools.partial(join_kernel, count),
+        [whole, *[modes(part) for part in second]],
         "join",
         scratch=[pltpu.SemaphoreType.DMA((nx // 2,))],
-        specs=[ANY] * count,
-        out_specs=ANY,
-    )(*e)
+        specs=[ANY] * count + [VMEM] * count,
+        out_specs=[ANY] + [VMEM] * count,
+    )(*e, *c1)
     result = []
     for stage, part in enumerate(second):
         result = [
@@ -472,10 +470,10 @@
                 whole,
                 "last",
                 scratch=[pltpu.VMEM((2 * len(part), ny, nz), F32), pltpu.SemaphoreType.DMA((len(part),))],
-                specs=[VMEM] * (4 + 2 * count) + [ANY] * len(result),
+                specs=[VMEM] * (5 + count) + [ANY] * len(result),
                 out_specs=ANY,
-                aliases={4 + 2 * count: 0} if result else {},
-            )(c2[stage], by, bz, a, *c1, *a1, *result)
+                aliases={5 + count: 0} if result else {},
+            )(c2[stage], by, bz, a, before[stage], *a1, *result)
         ]
     return end_state, result[0]
 

time: 22.7 us -> 22.7 us (level)
  no operation moved by 1% of the time
where the time goes in v9:
time: 22.7 us; the launch traced here: 22.6 us
  starting transfers between devices  8.84 us (39%)
  Pallas kernels  7.72 us (34%)
  waiting for transfers between devices  5.24 us (23%)
  between operations  0.73 us (3%)
    pallas_call x11, Pallas kernels, run(): pl.pallas_call(kernel, out_shape=outs, in_specs=specs or [VMEM] * len(arg...  7.72 us
    ppermute x4, starting transfers between devices, onward(): return lax.ppermute(c, 'tm', ring)  5.81 us
    ppermute x4, waiting for transfers between devices, onward(): return lax.ppermute(c, 'tm', ring)  4.99 us
    ppermute x1, starting transfers between devices, body(): from_odd = lax.ppermute(to_odd, ('tm', 'gx'), odd_pairs)  3.03 us
  transfers between devices with their start and end apart: 6, of which 6 were waited for; matrix products, arithmetic and copies ran while one was open for 0% of the time, Pallas kernels for 29%

profile of v9, /device:TPU:0, one launch (start us, length us, event | category | flops | bytes accessed | tf_op | source)
XLA Modules:
  0.0 22.6 jit_solution(7828501119471291258)
XLA Ops:
  0.6 0.0 copy-start.2
  0.7 0.0 copy-start.3
  0.7 1.1 %pack.1.after = f32[3,128,128]{2,1,0:T(8,128)S(1)} custom-call(f32[16,128,128]{2,1,0:T(8,128)} %bitcast.1, f32[16,128,128]{2,1,0:T(8,128)} %refs_2_.5), custom_call_target="tpu_custom_call" | custom-call | flops 10000000000 | bytes 1000000000 | tf_op jit(solution)/shard_map/pack/pallas_call | solution.py:137
  1.8 3.0 %collective-permute-start.1 = (f32[3,128,128]{2,1,0:T(8,128)S(1)}, f32[3,128,128]{2,1,0:T(8,128)S(1)}, u32[]{:S(2)}, u32[]{:S(2)}) collective-permute-start(f32[3,128,128]{2,1,0:T(8,128)S(1)} %pack.1.after), channel_id=1, source_target_pairs={{0,16},{1,2},{2,1},{3,4},{4,3},{5,6},{6,5},{7,23},{8,24},{9,10},{1... | collective-permute-start | bytes 589832 | tf_op jit(solution)/shard_map/ppermute | solution.py:417
  4.8 0.0 copy-done.3
  4.8 0.8 %inner.1 = (f32[10,128,128]{2,1,0:T(8,128)S(1)}, f32[64,640]{1,0:T(8,128)S(1)}, f32[3,128,128]{2,1,0:T(8,128)S(1)}) custom-call(f32[16,128,128]{2,1,0:T(8,128)S(1)} %bitcast.2, f32[16,128,128]{2,1,0:T(8,128)S(1)} %copy-done, bf16[256,256]{1,0:T(8,128)(2,1)S(1)} %copy-done.2, bf16[128,256]{1,0:T(8,128)(2,1)S(1)} %copy-done.3, f32[3,128,128]{2,1,0:T(8,128)S(1)} %pack.1.after), custom_call_target="tpu_custom_call" | custom-call | flops 10000000000 | bytes 1000000000 | tf_op jit(solution)/shard_map/inner/pallas_call | solution.py:137
  5.6 1.5 %collective-permute-start.2 = (f32[64,640]{1,0:T(8,128)S(1)}, f32[64,640]{1,0:T(8,128)S(1)}, u32[]{:S(2)}, u32[]{:S(2)}) collective-permute-start(f32[64,640]{1,0:T(8,128)S(1)} %get-tuple-element.31), channel_id=1, source_target_pairs={{0,8},{8,16},{16,24},{24,0},{1,9},{9,17},{17,25},{25,1},{2,10},{10... | collective-permute-start | bytes 491528 | tf_op jit(solution)/shard_map/ppermute | solution.py:412
  7.2 0.0 collective-permute-start
  7.2 1.2 %middle.1 = (f32[4,128,128]{2,1,0:T(8,128)S(1)}, f32[12,128,128]{2,1,0:T(8,128)S(1)}, f32[64,640]{1,0:T(8,128)S(1)}, f32[64,256]{1,0:T(8,128)S(1)}) custom-call(f32[16,128,128]{2,1,0:T(8,128)S(1)} %bitcast.3, f32[16,128,128]{2,1,0:T(8,128)S(1)} %copy-done, bf16[256,256]{1,0:T(8,128)(2,1)S(1)} %copy-done.2, bf16[128,256]{1,0:T(8,128)(2,1)S(1)} %copy-done.3, ...), custom_call_target="tpu_custom_call" | custom-call | tf_op jit(solution)/shard_map/middle/pallas_call | solution.py:137
  8.3 0.1 collective-permute-done.1.from_odd.odd_ref
  8.5 0.1 collective-permute-done.even_ref
  8.6 0.6 %outer.1 = (f32[4,128,128]{2,1,0:T(8,128)S(1)}, f32[4,128,128]{2,1,0:T(8,128)S(1)}, f32[64,512]{1,0:T(8,128)S(1)}) custom-call(f32[16,128,128]{2,1,0:T(8,128)S(1)} %bitcast.4, f32[16,128,128]{2,1,0:T(8,128)S(1)} %copy-done, f32[3,128,128]{2,1,0:T(8,128)S(1)} %collective-permute-done.even_ref, f32[3,128,128]{2,1,0:T(8,128)S(1)} %collective-permute-done.1.from_odd.odd_ref, ...), custom_call_target="tpu_custom_call" | custom-call | flops 10000000000 | bytes 1000000000 | tf_op jit(solution)/shard_map/outer/pallas_call | solution.py:137
  9.2 1.9 %collective-permute-start.3 = (f32[64,512]{1,0:T(8,128)S(1)}, f32[64,512]{1,0:T(8,128)S(1)}, u32[]{:S(2)}, u32[]{:S(2)}) collective-permute-start(f32[64,512]{1,0:T(8,128)S(1)} %get-tuple-element.34), channel_id=1, source_target_pairs={{0,8},{8,16},{16,24},{24,0},{1,9},{9,17},{17,25},{25,1},{2,10},{10... | collective-permute-start | bytes 393224 | tf_op jit(solution)/shard_map/ppermute | solution.py:412
  11.1 0.5 %later.1 = (f32[4,128,128]{2,1,0:T(8,128)S(1)}, f32[64,512]{1,0:T(8,128)S(1)}) custom-call(f32[16,128,128]{2,1,0:T(8,128)S(1)} %bitcast.5, f32[16,128,128]{2,1,0:T(8,128)S(1)} %copy-done, f32[4,128,128]{2,1,0:T(8,128)S(1)} %get-tuple-element.27.ab_ref.refs_1_, f32[4,128,128]{2,1,0:T(8,128)S(1)} %get-tuple-element.28.gb_ref, ...), custom_call_target="tpu_custom_call" | custom-call | flops 10000000000 | bytes 1000000000 | tf_op jit(solution)/shard_map/later/pallas_call | solution.py:137
  11.6 1.3 %collective-permute-done.2.refs_5_.refs_2_ = f32[64,640]{1,0:T(8,128)S(1)} collective-permute-done((f32[64,640]{1,0:T(8,128)S(1)}, f32[64,640]{1,0:T(8,128)S(1)}, u32[]{:S(2)}, u32[]{:S(2)}) %collective-permute-start.2) | collective-permute-done | bytes 163872 | tf_op jit(solution)/shard_map/ppermute | solution.py:412
  12.8 0.8 %second.2 = (f32[10,128,128]{2,1,0:T(8,128)S(1)}, f32[8,128,128]{2,1,0:T(8,128)S(1)}, f32[64,512]{1,0:T(8,128)S(1)}) custom-call(f32[16,128,128]{2,1,0:T(8,128)S(1)} %bitcast.6, f32[4,128,128]{2,1,0:T(8,128)S(1)} %get-tuple-element.27.ab_ref.refs_1_, f32[16,128,128]{2,1,0:T(8,128)S(1)} %copy-done, f32[12,128,128]{2,1,0:T(8,128)S(1)} %get-tuple-element.26.after.refs_3_, ...), custom_call_target="tpu_custom_call" | custom-call | flops 10000000000 | bytes 1000000000 | tf_op jit(solution)/shard_map/second/pallas_call | solution.py:137
  13.6 1.2 %collective-permute-start.5 = (f32[64,512]{1,0:T(8,128)S(1)}, f32[64,512]{1,0:T(8,128)S(1)}, u32[]{:S(2)}, u32[]{:S(2)}) collective-permute-start(f32[64,512]{1,0:T(8,128)S(1)} %get-tuple-element.42), channel_id=1, source_target_pairs={{0,8},{8,16},{16,24},{24,0},{1,9},{9,17},{17,25},{25,1},{2,10},{10... | collective-permute-start | bytes 393224 | tf_op jit(solution)/shard_map/ppermute | solution.py:412
  14.8 1.0 %collective-permute-done.3.refs_5_.refs_3_ = f32[64,512]{1,0:T(8,128)S(1)} collective-permute-done((f32[64,512]{1,0:T(8,128)S(1)}, f32[64,512]{1,0:T(8,128)S(1)}, u32[]{:S(2)}, u32[]{:S(2)}) %collective-permute-start.3) | collective-permute-done | bytes 131104 | tf_op jit(solution)/shard_map/ppermute | solution.py:412
  15.8 0.8 %second.3 = (f32[8,128,128]{2,1,0:T(8,128)S(1)}, f32[8,128,128]{2,1,0:T(8,128)S(1)}, f32[64,512]{1,0:T(8,128)S(1)}) custom-call(f32[16,128,128]{2,1,0:T(8,128)S(1)} %bitcast.7, f32[4,128,128]{2,1,0:T(8,128)S(1)} %get-tuple-element.27.ab_ref.refs_1_, f32[16,128,128]{2,1,0:T(8,128)S(1)} %copy-done, f32[12,128,128]{2,1,0:T(8,128)S(1)} %get-tuple-element.26.after.refs_3_, ...), custom_call_target="tpu_custom_call" | custom-call | flops 10000000000 | bytes 1000000000 | tf_op jit(solution)/shard_map/second/pallas_call | solution.py:137
  16.6 1.2 %collective-permute-start.4 = (f32[64,512]{1,0:T(8,128)S(1)}, f32[64,512]{1,0:T(8,128)S(1)}, u32[]{:S(2)}, u32[]{:S(2)}) collective-permute-start(f32[64,512]{1,0:T(8,128)S(1)} %get-tuple-element.39), channel_id=1, source_target_pairs={{0,8},{8,16},{16,24},{24,0},{1,9},{9,17},{17,25},{25,1},{2,10},{10... | collective-permute-start | bytes 393224 | tf_op jit(solution)/shard_map/ppermute | solution.py:412
  17.8 1.0 %join.1 = (f32[1,16,128,128]{3,2,1,0:T(8,128)}, f32[64,512]{1,0:T(8,128)S(1)}, f32[64,512]{1,0:T(8,128)S(1)}) custom-call(f32[8,128,128]{2,1,0:T(8,128)S(1)} %get-tuple-element.33.refs_0_, f32[8,128,128]{2,1,0:T(8,128)S(1)} %get-tuple-element.37.refs_1_, f32[64,640]{1,0:T(8,128)S(1)} %collective-permute-done.2.refs_5_.refs_2_, ...), custom_call_target="tpu_custom_call" | custom-call | flops 10000000000 | bytes 1000000000 | tf_op jit(solution)/shard_map/join/pallas_call | solution.py:137
  18.8 0.7 %collective-permute-done.5.refs_0_ = f32[64,512]{1,0:T(8,128)S(1)} collective-permute-done((f32[64,512]{1,0:T(8,128)S(1)}, f32[64,512]{1,0:T(8,128)S(1)}, u32[]{:S(2)}, u32[]{:S(2)}) %collective-permute-start.5) | collective-permute-done | bytes 131104 | tf_op jit(solution)/shard_map/ppermute | solution.py:412
  19.5 1.0 %last.2.refs_7_ = f32[1,16,128,128]{3,2,1,0:T(8,128)} custom-call(f32[64,512]{1,0:T(8,128)S(1)} %collective-permute-done.5.refs_0_, bf16[128,192]{1,0:T(8,128)(2,1)S(1)} %copy-done.5, bf16[384,256]{1,0:T(8,128)(2,1)S(1)} %copy-done.4, f32[16,128,128]{2,1,0:T(8,128)S(1)} %bitcast.8, f32[64,512]{1,0:T(8,128)S(1)} %get-tuple-element.43.refs_4_, ...), custom_call_target="tpu_custom_call" | custom-call | flops 10000000000 | bytes 1000000000 | tf_op jit(solution)/shard_map/last/pallas_call | solution.py:137
  20.6 2.0 %collective-permute-done.4.refs_0_ = f32[64,512]{1,0:T(8,128)S(1)} collective-permute-done((f32[64,512]{1,0:T(8,128)S(1)}, f32[64,512]{1,0:T(8,128)S(1)}, u32[]{:S(2)}, u32[]{:S(2)}) %collective-permute-start.4) | collective-permute-done | bytes 131104 | tf_op jit(solution)/shard_map/ppermute | solution.py:412
  (11 shorter events, 0.1 us)
Async XLA Ops:
  0.6 4.2 %copy-start = (f32[16,128,128]{2,1,0:T(8,128)S(1)}, f32[16,128,128]{2,1,0:T(8,128)}, u32[]{:S(2)}) copy-start(f32[16,128,128]{2,1,0:T(8,128)} %refs_2_.5) | copy-start | bytes 3145732
  0.6 4.2 %copy-start.1 = (f32[1,16,128,128]{3,2,1,0:T(8,128)S(1)}, f32[1,16,128,128]{3,2,1,0:T(8,128)}, u32[]{:S(2)}) copy-start(f32[1,16,128,128]{3,2,1,0:T(8,128)} %param.6) | copy-start | bytes 3145732
  0.6 4.2 %copy-start.2 = (bf16[256,256]{1,0:T(8,128)(2,1)S(1)}, bf16[256,256]{1,0:T(8,128)(2,1)}, u32[]{:S(2)}) copy-start(bf16[256,256]{1,0:T(8,128)(2,1)} %constant.8.clone.fz_ref.refs_7_) | copy-start | bytes 393220
  0.7 4.1 %copy-start.3 = (bf16[128,256]{1,0:T(8,128)(2,1)S(1)}, bf16[128,256]{1,0:T(8,128)(2,1)}, u32[]{:S(2)}) copy-start(bf16[128,256]{1,0:T(8,128)(2,1)} %constant.9.clone.fy_ref.refs_8_) | copy-start | bytes 196612
  1.8 6.7 %collective-permute-start.1 = (f32[3,128,128]{2,1,0:T(8,128)S(1)}, f32[3,128,128]{2,1,0:T(8,128)S(1)}, u32[]{:S(2)}, u32[]{:S(2)}) collective-permute-start(f32[3,128,128]{2,1,0:T(8,128)S(1)} %pack.1.after), channel_id=1, source_target_pairs={{0,16},{1,2},{2,1},{3,4},{4,3},{5,6},{6,5},{7,23},{8,24},{9,10},{1... | collective-permute-start | bytes 589832 | tf_op jit(solution)/shard_map/ppermute | solution.py:417
  5.6 7.2 %collective-permute-start.2 = (f32[64,640]{1,0:T(8,128)S(1)}, f32[64,640]{1,0:T(8,128)S(1)}, u32[]{:S(2)}, u32[]{:S(2)}) collective-permute-start(f32[64,640]{1,0:T(8,128)S(1)} %get-tuple-element.31), channel_id=1, source_target_pairs={{0,8},{8,16},{16,24},{24,0},{1,9},{9,17},{17,25},{25,1},{2,10},{10... | collective-permute-start | bytes 491528 | tf_op jit(solution)/shard_map/ppermute | solution.py:412
  7.2 1.4 %collective-permute-start = (f32[3,128,128]{2,1,0:T(8,128)S(1)}, f32[3,128,128]{2,1,0:T(8,128)S(1)}, u32[]{:S(2)}, u32[]{:S(2)}) collective-permute-start(f32[3,128,128]{2,1,0:T(8,128)S(1)} %get-tuple-element.23), channel_id=1, source_target_pairs={{0,1},{1,0},{2,3},{3,2},{4,5},{5,4},{6,7},{7,6},{8,9},{9,8},{10,11... | collective-permute-start | bytes 589832 | tf_op jit(solution)/shard_map/ppermute | solution.py:429
  9.2 6.6 %collective-permute-start.3 = (f32[64,512]{1,0:T(8,128)S(1)}, f32[64,512]{1,0:T(8,128)S(1)}, u32[]{:S(2)}, u32[]{:S(2)}) collective-permute-start(f32[64,512]{1,0:T(8,128)S(1)} %get-tuple-element.34), channel_id=1, source_target_pairs={{0,8},{8,16},{16,24},{24,0},{1,9},{9,17},{17,25},{25,1},{2,10},{10... | collective-permute-start | bytes 393224 | tf_op jit(solution)/shard_map/ppermute | solution.py:412
  11.1 1.7 %copy-start.4 = (bf16[384,256]{1,0:T(8,128)(2,1)S(1)}, bf16[384,256]{1,0:T(8,128)(2,1)}, u32[]{:S(2)}) copy-start(bf16[384,256]{1,0:T(8,128)(2,1)} %constant.11.clone.refs_10_.refs_2_) | copy-start | bytes 589828
  11.1 1.7 %copy-start.5 = (bf16[128,192]{1,0:T(8,128)(2,1)S(1)}, bf16[128,192]{1,0:T(8,128)(2,1)}, u32[]{:S(2)}) copy-start(bf16[128,192]{1,0:T(8,128)(2,1)} %constant.10.clone.refs_9_.refs_1_) | copy-start | bytes 147460
  13.6 5.9 %collective-permute-start.5 = (f32[64,512]{1,0:T(8,128)S(1)}, f32[64,512]{1,0:T(8,128)S(1)}, u32[]{:S(2)}, u32[]{:S(2)}) collective-permute-start(f32[64,512]{1,0:T(8,128)S(1)} %get-tuple-element.42), channel_id=1, source_target_pairs={{0,8},{8,16},{16,24},{24,0},{1,9},{9,17},{17,25},{25,1},{2,10},{10... | collective-permute-start | bytes 393224 | tf_op jit(solution)/shard_map/ppermute | solution.py:412
  16.6 5.9 %collective-permute-start.4 = (f32[64,512]{1,0:T(8,128)S(1)}, f32[64,512]{1,0:T(8,128)S(1)}, u32[]{:S(2)}, u32[]{:S(2)}) collective-permute-start(f32[64,512]{1,0:T(8,128)S(1)} %get-tuple-element.39), channel_id=1, source_target_pairs={{0,8},{8,16},{16,24},{24,0},{1,9},{9,17},{17,25},{25,1},{2,10},{10... | collective-permute-start | bytes 393224 | tf_op jit(solution)/shard_map/ppermute | solution.py:412

commit v10 on v8

--- a/solution.py
+++ b/solution.py
@@ -344,27 +344,17 @@
 
 def last_kernel(stage, count, *refs):
     c2_ref, by_ref, bz_ref, a_ref = refs[:4]
-    c1_refs, a1_refs = refs[4 : 4 + count], refs[4 + count : 4 + 2 * count]
+    before_ref, a1_refs = refs[4], refs[5 : 5 + count]
     out_ref, buffer, sems = refs[-3:]
     nx, ny, nz = out_ref.shape[1:]
     first, second = chunks(nx)
-    where = {}
-    for ref, part in zip(c1_refs, first):
-        for i, p in enumerate(planes_of(part, -1)):
-            where[p] = (ref, i)
-
-    def column(p):
-        ref, i = where[p]
-        return ref[:, i * KZ : (i + 1) * KZ]
-
     receives = lax.axis_index("tm") > 0
 
     @pl.when(receives)
     def _():
         values = reader(*[(ref, planes_of(part, -1)) for ref, part in zip(a1_refs, first)])
         planes = planes_of(second[stage], 0)
-        before = jnp.concatenate([column(p) for p in planes], axis=1)
-        change = synthesise(c2_ref[...] - before, by_ref, bz_ref)
+        change = synthesise(c2_ref[...] - before_ref[...], by_ref, bz_ref)
         copies = []
         for i in range(0, len(planes), 2):
             for k in (0, 1):
@@ -392,16 +382,24 @@
                 copy.wait()
 
 
-def join_kernel(*refs):
-    parts, out_ref, sems = refs[:-2], refs[-2], refs[-1]
+def join_kernel(count, *refs):
+    parts, c1_refs = refs[:count], refs[count : 2 * count]
+    out_ref, before_refs, sems = refs[2 * count], refs[2 * count + 1 : -1], refs[-1]
+    first, second = chunks(out_ref.shape[1])
     copies = []
-    for ref, part in zip(parts, chunks(out_ref.shape[1])[1]):
+    for ref, part in zip(parts, second):
         for i, p in enumerate(planes_of(part, 0)[::2]):
             copies.append(
                 pltpu.make_async_copy(ref.at[pl.ds(2 * i, 2)], out_ref.at[0, pl.ds(p, 2)], sems.at[len(copies)])
             )
     for copy in copies:
         copy.start()
+    columns = {}
+    for ref, part in zip(c1_refs, first):
+        for i, p in enumerate(planes_of(part, -1)):
+            columns[p] = ref[:, i * KZ : (i + 1) * KZ]
+    for ref, part in zip(before_refs, second):
+        ref[...] = jnp.concatenate([columns[p] for p in planes_of(part, 0)], axis=1)
     for copy in copies:
         copy.wait()
 
@@ -478,14 +476,14 @@
         e.append(end)
         c2.append(onward(c))
     whole = jax.ShapeDtypeStruct((1, nx, ny, nz), F32)
-    end_state = call(
-        join_kernel,
-        whole,
+    end_state, *before = call(
+        functools.partial(join_kernel, count),
+        [whole, *[modes(part) for part in second]],
         "join",
         scratch=[pltpu.SemaphoreType.DMA((nx // 2,))],
-        specs=[ANY] * count,
-        out_specs=ANY,
-    )(*e)
+        specs=[ANY] * count + [VMEM] * count,
+        out_specs=[ANY] + [VMEM] * count,
+    )(*e, *c1)
     result = []
     for stage, part in enumerate(second):
         result = [
@@ -494,10 +492,10 @@
                 whole,
                 "last",
                 scratch=[pltpu.VMEM((2 * len(part), ny, nz), F32), pltpu.SemaphoreType.DMA((len(part),))],
-                specs=[VMEM] * (4 + 2 * count) + [ANY] * len(result),
+                specs=[VMEM] * (5 + count) + [ANY] * len(result),
                 out_specs=ANY,
-                aliases={4 + 2 * count: 0} if result else {},
-            )(c2[stage], by, bz, a, *c1, *a1, *result)
+                aliases={5 + count: 0} if result else {},
+            )(c2[stage], by, bz, a, before[stage], *a1, *result)
         ]
     return end_state, result[0]
 

time: 22.7 us -> 22.6 us (level)
  no operation moved by 1% of the time
where the time goes in v10:
time: 22.6 us; the launch traced here: 22.4 us
  starting transfers between devices  9.35 us (41%)
  Pallas kernels  7.89 us (35%)
  waiting for transfers between devices  4.39 us (19%)
  between operations  0.73 us (3%)
    pallas_call x11, Pallas kernels, run(): pl.pallas_call(kernel, out_shape=outs, in_specs=specs or [VMEM] * len(arg...  7.89 us
    ppermute x4, starting transfers between devices, onward(): return lax.ppermute(c, 'tm', ring)  6.31 us
    ppermute x4, waiting for transfers between devices, onward(): return lax.ppermute(c, 'tm', ring)  3.7 us
    ppermute x1, starting transfers between devices, body(): from_odd = lax.ppermute(to_odd, ('tm', 'gx'), odd_pairs)  3.03 us
    ppermute x1, waiting for transfers between devices, body(): from_odd = lax.ppermute(to_odd, ('tm', 'gx'), odd_pairs)  0.54 us
  transfers between devices with their start and end apart: 6, of which 6 were waited for; matrix products, arithmetic and copies ran while one was open for 0% of the time, Pallas kernels for 30%

profile of v10, /device:TPU:0, one launch (start us, length us, event | category | flops | bytes accessed | tf_op | source)
XLA Modules:
  0.0 22.4 jit_solution(16900721934089217155)
XLA Ops:
  0.6 0.0 copy-start.2
  0.7 0.0 copy-start.3
  0.7 1.1 %pack.1.after = f32[3,128,128]{2,1,0:T(8,128)S(1)} custom-call(f32[16,128,128]{2,1,0:T(8,128)} %bitcast.1, f32[16,128,128]{2,1,0:T(8,128)} %refs_2_.5), custom_call_target="tpu_custom_call" | custom-call | flops 10000000000 | bytes 1000000000 | tf_op jit(solution)/shard_map/pack/pallas_call | solution.py:148
  1.8 3.0 %collective-permute-start.1 = (f32[3,128,128]{2,1,0:T(8,128)S(1)}, f32[3,128,128]{2,1,0:T(8,128)S(1)}, u32[]{:S(2)}, u32[]{:S(2)}) collective-permute-start(f32[3,128,128]{2,1,0:T(8,128)S(1)} %pack.1.after), channel_id=1, source_target_pairs={{0,16},{1,2},{2,1},{3,4},{4,3},{5,6},{6,5},{7,15},{8,24},{9,10},{1... | collective-permute-start | bytes 589832 | tf_op jit(solution)/shard_map/ppermute | solution.py:438
  4.8 0.0 copy-done.1
  4.8 0.8 %inner.1 = (f32[10,128,128]{2,1,0:T(8,128)S(1)}, f32[64,640]{1,0:T(8,128)S(1)}, f32[3,128,128]{2,1,0:T(8,128)S(1)}) custom-call(f32[16,128,128]{2,1,0:T(8,128)S(1)} %bitcast.2, f32[16,128,128]{2,1,0:T(8,128)S(1)} %copy-done, bf16[256,256]{1,0:T(8,128)(2,1)S(1)} %copy-done.2, bf16[128,256]{1,0:T(8,128)(2,1)S(1)} %copy-done.3, f32[3,128,128]{2,1,0:T(8,128)S(1)} %pack.1.after), custom_call_target="tpu_custom_call" | custom-call | flops 10000000000 | bytes 1000000000 | tf_op jit(solution)/shard_map/inner/pallas_call | solution.py:148
  5.6 1.5 %collective-permute-start.2 = (f32[64,640]{1,0:T(8,128)S(1)}, f32[64,640]{1,0:T(8,128)S(1)}, u32[]{:S(2)}, u32[]{:S(2)}) collective-permute-start(f32[64,640]{1,0:T(8,128)S(1)} %get-tuple-element.32), channel_id=1, source_target_pairs={{0,8},{8,16},{16,24},{24,0},{1,9},{9,17},{17,25},{25,1},{2,10},{10... | collective-permute-start | bytes 491528 | tf_op jit(solution)/shard_map/ppermute | solution.py:433
  7.2 0.0 collective-permute-start
  7.2 0.7 %middle.1 = (f32[4,128,128]{2,1,0:T(8,128)S(1)}, f32[64,256]{1,0:T(8,128)S(1)}, f32[64,640]{1,0:T(8,128)S(1)}, f32[64,256]{1,0:T(8,128)S(1)}) custom-call(f32[16,128,128]{2,1,0:T(8,128)S(1)} %bitcast.3, f32[16,128,128]{2,1,0:T(8,128)S(1)} %copy-done, bf16[256,256]{1,0:T(8,128)(2,1)S(1)} %copy-done.2, bf16[128,256]{1,0:T(8,128)(2,1)S(1)} %copy-done.3, ...), custom_call_target="tpu_custom_call" | custom-call | tf_op jit(solution)/shard_map/middle/pallas_call | solution.py:148
  7.9 0.5 %collective-permute-done.1.from_odd.odd_ref = f32[3,128,128]{2,1,0:T(8,128)S(1)} collective-permute-done((f32[3,128,128]{2,1,0:T(8,128)S(1)}, f32[3,128,128]{2,1,0:T(8,128)S(1)}, u32[]{:S(2)}, u32[]{:S(2)}) %collective-permute-start.1) | collective-permute-done | bytes 196640 | tf_op jit(solution)/shard_map/ppermute | solution.py:438
  8.5 0.1 collective-permute-done.even_ref
  8.6 0.5 %outer.1 = (f32[4,128,128]{2,1,0:T(8,128)S(1)}, f32[4,128,128]{2,1,0:T(8,128)S(1)}, f32[64,512]{1,0:T(8,128)S(1)}) custom-call(f32[16,128,128]{2,1,0:T(8,128)S(1)} %bitcast.4, f32[16,128,128]{2,1,0:T(8,128)S(1)} %copy-done, f32[3,128,128]{2,1,0:T(8,128)S(1)} %collective-permute-done.even_ref, f32[3,128,128]{2,1,0:T(8,128)S(1)} %collective-permute-done.1.from_odd.odd_ref, ...), custom_call_target="tpu_custom_call" | custom-call | flops 10000000000 | bytes 1000000000 | tf_op jit(solution)/shard_map/outer/pallas_call | solution.py:148
  9.1 1.9 %collective-permute-start.3 = (f32[64,512]{1,0:T(8,128)S(1)}, f32[64,512]{1,0:T(8,128)S(1)}, u32[]{:S(2)}, u32[]{:S(2)}) collective-permute-start(f32[64,512]{1,0:T(8,128)S(1)} %get-tuple-element.35), channel_id=1, source_target_pairs={{0,8},{8,16},{16,24},{24,0},{1,9},{9,17},{17,25},{25,1},{2,10},{10... | collective-permute-start | bytes 393224 | tf_op jit(solution)/shard_map/ppermute | solution.py:433
  11.0 1.2 %later.1 = (f32[16,128,128]{2,1,0:T(8,128)S(1)}, f32[64,512]{1,0:T(8,128)S(1)}, f32[64,512]{1,0:T(8,128)S(1)}) custom-call(f32[16,128,128]{2,1,0:T(8,128)S(1)} %bitcast.5, f32[16,128,128]{2,1,0:T(8,128)S(1)} %copy-done, f32[4,128,128]{2,1,0:T(8,128)S(1)} %get-tuple-element.28.ab_ref.refs_1_, f32[4,128,128]{2,1,0:T(8,128)S(1)} %get-tuple-element.29.gb_ref, ...), custom_call_target="tpu_custom_call" | custom-call | flops 10000000000 | bytes 1000000000 | tf_op jit(solution)/shard_map/later/pallas_call | solution.py:148
  12.3 0.6 %collective-permute-done.2.refs_4_.refs_12_.refs_2_ = f32[64,640]{1,0:T(8,128)S(1)} collective-permute-done((f32[64,640]{1,0:T(8,128)S(1)}, f32[64,640]{1,0:T(8,128)S(1)}, u32[]{:S(2)}, u32[]{:S(2)}) %collective-permute-start.2) | collective-permute-done | bytes 163872 | tf_op jit(solution)/shard_map/ppermute | solution.py:433
  12.8 0.8 %second.2 = (f32[10,128,128]{2,1,0:T(8,128)S(1)}, f32[8,128,128]{2,1,0:T(8,128)S(1)}, f32[64,512]{1,0:T(8,128)S(1)}) custom-call(f32[16,128,128]{2,1,0:T(8,128)S(1)} %bitcast.6, f32[4,128,128]{2,1,0:T(8,128)S(1)} %get-tuple-element.28.ab_ref.refs_1_, f32[16,128,128]{2,1,0:T(8,128)S(1)} %copy-done, f32[16,128,128]{2,1,0:T(8,128)S(1)} %get-tuple-element.31.refs_3_, ...), custom_call_target="tpu_custom_call" | custom-call | flops 10000000000 | bytes 1000000000 | tf_op jit(solution)/shard_map/second/pallas_call | solution.py:148
  13.6 1.5 %collective-permute-start.5 = (f32[64,512]{1,0:T(8,128)S(1)}, f32[64,512]{1,0:T(8,128)S(1)}, u32[]{:S(2)}, u32[]{:S(2)}) collective-permute-start(f32[64,512]{1,0:T(8,128)S(1)} %get-tuple-element.44), channel_id=1, source_target_pairs={{0,8},{8,16},{16,24},{24,0},{1,9},{9,17},{17,25},{25,1},{2,10},{10... | collective-permute-start | bytes 393224 | tf_op jit(solution)/shard_map/ppermute | solution.py:433
  15.1 0.6 %collective-permute-done.3.refs_4_.refs_3_ = f32[64,512]{1,0:T(8,128)S(1)} collective-permute-done((f32[64,512]{1,0:T(8,128)S(1)}, f32[64,512]{1,0:T(8,128)S(1)}, u32[]{:S(2)}, u32[]{:S(2)}) %collective-permute-start.3) | collective-permute-done | bytes 131104 | tf_op jit(solution)/shard_map/ppermute | solution.py:433
  15.7 0.7 %second.3 = (f32[8,128,128]{2,1,0:T(8,128)S(1)}, f32[8,128,128]{2,1,0:T(8,128)S(1)}, f32[64,512]{1,0:T(8,128)S(1)}) custom-call(f32[16,128,128]{2,1,0:T(8,128)S(1)} %bitcast.7, f32[4,128,128]{2,1,0:T(8,128)S(1)} %get-tuple-element.28.ab_ref.refs_1_, f32[16,128,128]{2,1,0:T(8,128)S(1)} %copy-done, f32[16,128,128]{2,1,0:T(8,128)S(1)} %get-tuple-element.31.refs_3_, ...), custom_call_target="tpu_custom_call" | custom-call | flops 10000000000 | bytes 1000000000 | tf_op jit(solution)/shard_map/second/pallas_call | solution.py:148
  16.4 1.4 %collective-permute-start.4 = (f32[64,512]{1,0:T(8,128)S(1)}, f32[64,512]{1,0:T(8,128)S(1)}, u32[]{:S(2)}, u32[]{:S(2)}) collective-permute-start(f32[64,512]{1,0:T(8,128)S(1)} %get-tuple-element.41), channel_id=1, source_target_pairs={{0,8},{8,16},{16,24},{24,0},{1,9},{9,17},{17,25},{25,1},{2,10},{10... | collective-permute-start | bytes 393224 | tf_op jit(solution)/shard_map/ppermute | solution.py:433
  17.7 1.0 %join.1 = (f32[1,16,128,128]{3,2,1,0:T(8,128)}, f32[64,512]{1,0:T(8,128)S(1)}, f32[64,512]{1,0:T(8,128)S(1)}) custom-call(f32[8,128,128]{2,1,0:T(8,128)S(1)} %get-tuple-element.34.refs_0_, f32[8,128,128]{2,1,0:T(8,128)S(1)} %get-tuple-element.39.refs_1_, f32[64,640]{1,0:T(8,128)S(1)} %collective-permute-done.2.refs_4_.refs_12_.refs_2_, ...), custom_call_target="tpu_custom_call" | custom-call | flops 10000000000 | bytes 1000000000 | tf_op jit(solution)/shard_map/join/pallas_call | solution.py:148
  18.8 1.1 %collective-permute-done.5.refs_0_ = f32[64,512]{1,0:T(8,128)S(1)} collective-permute-done((f32[64,512]{1,0:T(8,128)S(1)}, f32[64,512]{1,0:T(8,128)S(1)}, u32[]{:S(2)}, u32[]{:S(2)}) %collective-permute-start.5) | collective-permute-done | bytes 131104 | tf_op jit(solution)/shard_map/ppermute | solution.py:433
  19.8 1.0 %last.2.refs_7_ = f32[1,16,128,128]{3,2,1,0:T(8,128)} custom-call(f32[64,512]{1,0:T(8,128)S(1)} %collective-permute-done.5.refs_0_, bf16[128,192]{1,0:T(8,128)(2,1)S(1)} %copy-done.5, bf16[384,256]{1,0:T(8,128)(2,1)S(1)} %copy-done.4, f32[16,128,128]{2,1,0:T(8,128)S(1)} %bitcast.8, f32[64,512]{1,0:T(8,128)S(1)} %get-tuple-element.45.refs_4_, ...), custom_call_target="tpu_custom_call" | custom-call | flops 10000000000 | bytes 1000000000 | tf_op jit(solution)/shard_map/last/pallas_call | solution.py:148
  20.9 1.5 %collective-permute-done.4.refs_0_ = f32[64,512]{1,0:T(8,128)S(1)} collective-permute-done((f32[64,512]{1,0:T(8,128)S(1)}, f32[64,512]{1,0:T(8,128)S(1)}, u32[]{:S(2)}, u32[]{:S(2)}) %collective-permute-start.4) | collective-permute-done | bytes 131104 | tf_op jit(solution)/shard_map/ppermute | solution.py:433
  (11 shorter events, 0.1 us)
Async XLA Ops:
  0.6 4.2 %copy-start = (f32[16,128,128]{2,1,0:T(8,128)S(1)}, f32[16,128,128]{2,1,0:T(8,128)}, u32[]{:S(2)}) copy-start(f32[16,128,128]{2,1,0:T(8,128)} %refs_2_.5) | copy-start | bytes 3145732
  0.6 4.2 %copy-start.1 = (f32[1,16,128,128]{3,2,1,0:T(8,128)S(1)}, f32[1,16,128,128]{3,2,1,0:T(8,128)}, u32[]{:S(2)}) copy-start(f32[1,16,128,128]{3,2,1,0:T(8,128)} %param.6) | copy-start | bytes 3145732
  0.6 4.2 %copy-start.2 = (bf16[256,256]{1,0:T(8,128)(2,1)S(1)}, bf16[256,256]{1,0:T(8,128)(2,1)}, u32[]{:S(2)}) copy-start(bf16[256,256]{1,0:T(8,128)(2,1)} %constant.8.clone.fz_ref.refs_6_) | copy-start | bytes 393220
  0.7 4.1 %copy-start.3 = (bf16[128,256]{1,0:T(8,128)(2,1)S(1)}, bf16[128,256]{1,0:T(8,128)(2,1)}, u32[]{:S(2)}) copy-start(bf16[128,256]{1,0:T(8,128)(2,1)} %constant.9.clone.fy_ref.refs_7_) | copy-start | bytes 196612
  1.8 6.7 %collective-permute-start.1 = (f32[3,128,128]{2,1,0:T(8,128)S(1)}, f32[3,128,128]{2,1,0:T(8,128)S(1)}, u32[]{:S(2)}, u32[]{:S(2)}) collective-permute-start(f32[3,128,128]{2,1,0:T(8,128)S(1)} %pack.1.after), channel_id=1, source_target_pairs={{0,16},{1,2},{2,1},{3,4},{4,3},{5,6},{6,5},{7,15},{8,24},{9,10},{1... | collective-permute-start | bytes 589832 | tf_op jit(solution)/shard_map/ppermute | solution.py:438
  5.6 7.2 %collective-permute-start.2 = (f32[64,640]{1,0:T(8,128)S(1)}, f32[64,640]{1,0:T(8,128)S(1)}, u32[]{:S(2)}, u32[]{:S(2)}) collective-permute-start(f32[64,640]{1,0:T(8,128)S(1)} %get-tuple-element.32), channel_id=1, source_target_pairs={{0,8},{8,16},{16,24},{24,0},{1,9},{9,17},{17,25},{25,1},{2,10},{10... | collective-permute-start | bytes 491528 | tf_op jit(solution)/shard_map/ppermute | solution.py:433
  7.2 1.4 %collective-permute-start = (f32[3,128,128]{2,1,0:T(8,128)S(1)}, f32[3,128,128]{2,1,0:T(8,128)S(1)}, u32[]{:S(2)}, u32[]{:S(2)}) collective-permute-start(f32[3,128,128]{2,1,0:T(8,128)S(1)} %get-tuple-element.24), channel_id=1, source_target_pairs={{0,1},{1,0},{2,3},{3,2},{4,5},{5,4},{6,7},{7,6},{8,9},{9,8},{10,11... | collective-permute-start | bytes 589832 | tf_op jit(solution)/shard_map/ppermute | solution.py:450
  9.1 6.5 %collective-permute-start.3 = (f32[64,512]{1,0:T(8,128)S(1)}, f32[64,512]{1,0:T(8,128)S(1)}, u32[]{:S(2)}, u32[]{:S(2)}) collective-permute-start(f32[64,512]{1,0:T(8,128)S(1)} %get-tuple-element.35), channel_id=1, source_target_pairs={{0,8},{8,16},{16,24},{24,0},{1,9},{9,17},{17,25},{25,1},{2,10},{10... | collective-permute-start | bytes 393224 | tf_op jit(solution)/shard_map/ppermute | solution.py:433
  11.0 1.8 %copy-start.4 = (bf16[384,256]{1,0:T(8,128)(2,1)S(1)}, bf16[384,256]{1,0:T(8,128)(2,1)}, u32[]{:S(2)}) copy-start(bf16[384,256]{1,0:T(8,128)(2,1)} %constant.11.clone.refs_9_.refs_2_) | copy-start | bytes 589828
  11.0 1.8 %copy-start.5 = (bf16[128,192]{1,0:T(8,128)(2,1)S(1)}, bf16[128,192]{1,0:T(8,128)(2,1)}, u32[]{:S(2)}) copy-start(bf16[128,192]{1,0:T(8,128)(2,1)} %constant.10.clone.refs_8_.refs_1_) | copy-start | bytes 147460
  13.6 6.2 %collective-permute-start.5 = (f32[64,512]{1,0:T(8,128)S(1)}, f32[64,512]{1,0:T(8,128)S(1)}, u32[]{:S(2)}, u32[]{:S(2)}) collective-permute-start(f32[64,512]{1,0:T(8,128)S(1)} %get-tuple-element.44), channel_id=1, source_target_pairs={{0,8},{8,16},{16,24},{24,0},{1,9},{9,17},{17,25},{25,1},{2,10},{10... | collective-permute-start | bytes 393224 | tf_op jit(solution)/shard_map/ppermute | solution.py:433
  16.4 6.0 %collective-permute-start.4 = (f32[64,512]{1,0:T(8,128)S(1)}, f32[64,512]{1,0:T(8,128)S(1)}, u32[]{:S(2)}, u32[]{:S(2)}) collective-permute-start(f32[64,512]{1,0:T(8,128)S(1)} %get-tuple-element.41), channel_id=1, source_target_pairs={{0,8},{8,16},{16,24},{24,0},{1,9},{9,17},{17,25},{25,1},{2,10},{10... | collective-permute-start | bytes 393224 | tf_op jit(solution)/shard_map/ppermute | solution.py:433

commit v11 on v10

--- a/solution.py
+++ b/solution.py
@@ -426,7 +426,7 @@
             if 0 <= other < slabs:
                 odd_pairs.append((s * slabs + g, s * slabs + other))
             else:
-                odd_pairs.append((s * slabs + g, (s ^ (1 if g else 2)) * slabs + g))
+                odd_pairs.append((s * slabs + g, (s ^ 2) * slabs + g))
     ring = [(s, (s + 1) % slices) for s in range(slices)]
 
     def onward(c):

time: 22.6 us -> 22.6 us (level)
  no operation moved by 1% of the time
where the time goes in v11:
time: 22.6 us; the launch traced here: 22.4 us
  starting transfers between devices  9.35 us (41%)
  Pallas kernels  7.89 us (35%)
  waiting for transfers between devices  4.39 us (19%)
  between operations  0.73 us (3%)
    pallas_call x11, Pallas kernels, run(): pl.pallas_call(kernel, out_shape=outs, in_specs=specs or [VMEM] * len(arg...  7.89 us
    ppermute x4, starting transfers between devices, onward(): return lax.ppermute(c, 'tm', ring)  6.31 us
    ppermute x4, waiting for transfers between devices, onward(): return lax.ppermute(c, 'tm', ring)  3.7 us
    ppermute x1, starting transfers between devices, body(): from_odd = lax.ppermute(to_odd, ('tm', 'gx'), odd_pairs)  3.03 us
    ppermute x1, waiting for transfers between devices, body(): from_odd = lax.ppermute(to_odd, ('tm', 'gx'), odd_pairs)  0.54 us
  transfers between devices with their start and end apart: 6, of which 6 were waited for; matrix products, arithmetic and copies ran while one was open for 0% of the time, Pallas kernels for 30%

profile of v11, /device:TPU:0, one launch (start us, length us, event | category | flops | bytes accessed | tf_op | source)
XLA Modules:
  0.0 22.4 jit_solution(8033376494286240620)
XLA Ops:
  0.6 0.0 copy-start
  0.6 0.0 copy-start.2
  0.7 0.0 copy-start.3
  0.7 1.1 %pack.1.after = f32[3,128,128]{2,1,0:T(8,128)S(1)} custom-call(f32[16,128,128]{2,1,0:T(8,128)} %bitcast.1, f32[16,128,128]{2,1,0:T(8,128)} %refs_2_.5), custom_call_target="tpu_custom_call" | custom-call | flops 10000000000 | bytes 1000000000 | tf_op jit(solution)/shard_map/pack/pallas_call | solution.py:148
  1.8 3.0 %collective-permute-start.1 = (f32[3,128,128]{2,1,0:T(8,128)S(1)}, f32[3,128,128]{2,1,0:T(8,128)S(1)}, u32[]{:S(2)}, u32[]{:S(2)}) collective-permute-start(f32[3,128,128]{2,1,0:T(8,128)S(1)} %pack.1.after), channel_id=1, source_target_pairs={{0,16},{1,2},{2,1},{3,4},{4,3},{5,6},{6,5},{7,23},{8,24},{9,10},{1... | collective-permute-start | bytes 589832 | tf_op jit(solution)/shard_map/ppermute | solution.py:438
  4.8 0.8 %inner.1 = (f32[10,128,128]{2,1,0:T(8,128)S(1)}, f32[64,640]{1,0:T(8,128)S(1)}, f32[3,128,128]{2,1,0:T(8,128)S(1)}) custom-call(f32[16,128,128]{2,1,0:T(8,128)S(1)} %bitcast.2, f32[16,128,128]{2,1,0:T(8,128)S(1)} %copy-done, bf16[256,256]{1,0:T(8,128)(2,1)S(1)} %copy-done.2, bf16[128,256]{1,0:T(8,128)(2,1)S(1)} %copy-done.3, f32[3,128,128]{2,1,0:T(8,128)S(1)} %pack.1.after), custom_call_target="tpu_custom_call" | custom-call | flops 10000000000 | bytes 1000000000 | tf_op jit(solution)/shard_map/inner/pallas_call | solution.py:148
  5.6 1.5 %collective-permute-start.2 = (f32[64,640]{1,0:T(8,128)S(1)}, f32[64,640]{1,0:T(8,128)S(1)}, u32[]{:S(2)}, u32[]{:S(2)}) collective-permute-start(f32[64,640]{1,0:T(8,128)S(1)} %get-tuple-element.32), channel_id=1, source_target_pairs={{0,8},{8,16},{16,24},{24,0},{1,9},{9,17},{17,25},{25,1},{2,10},{10... | collective-permute-start | bytes 491528 | tf_op jit(solution)/shard_map/ppermute | solution.py:433
  7.2 0.0 collective-permute-start
  7.2 0.7 %middle.1 = (f32[4,128,128]{2,1,0:T(8,128)S(1)}, f32[64,256]{1,0:T(8,128)S(1)}, f32[64,640]{1,0:T(8,128)S(1)}, f32[64,256]{1,0:T(8,128)S(1)}) custom-call(f32[16,128,128]{2,1,0:T(8,128)S(1)} %bitcast.3, f32[16,128,128]{2,1,0:T(8,128)S(1)} %copy-done, bf16[256,256]{1,0:T(8,128)(2,1)S(1)} %copy-done.2, bf16[128,256]{1,0:T(8,128)(2,1)S(1)} %copy-done.3, ...), custom_call_target="tpu_custom_call" | custom-call | tf_op jit(solution)/shard_map/middle/pallas_call | solution.py:148
  7.9 0.5 %collective-permute-done.1.from_odd.odd_ref = f32[3,128,128]{2,1,0:T(8,128)S(1)} collective-permute-done((f32[3,128,128]{2,1,0:T(8,128)S(1)}, f32[3,128,128]{2,1,0:T(8,128)S(1)}, u32[]{:S(2)}, u32[]{:S(2)}) %collective-permute-start.1) | collective-permute-done | bytes 196640 | tf_op jit(solution)/shard_map/ppermute | solution.py:438
  8.5 0.1 collective-permute-done.even_ref
  8.6 0.5 %outer.1 = (f32[4,128,128]{2,1,0:T(8,128)S(1)}, f32[4,128,128]{2,1,0:T(8,128)S(1)}, f32[64,512]{1,0:T(8,128)S(1)}) custom-call(f32[16,128,128]{2,1,0:T(8,128)S(1)} %bitcast.4, f32[16,128,128]{2,1,0:T(8,128)S(1)} %copy-done, f32[3,128,128]{2,1,0:T(8,128)S(1)} %collective-permute-done.even_ref, f32[3,128,128]{2,1,0:T(8,128)S(1)} %collective-permute-done.1.from_odd.odd_ref, ...), custom_call_target="tpu_custom_call" | custom-call | flops 10000000000 | bytes 1000000000 | tf_op jit(solution)/shard_map/outer/pallas_call | solution.py:148
  9.1 1.9 %collective-permute-start.3 = (f32[64,512]{1,0:T(8,128)S(1)}, f32[64,512]{1,0:T(8,128)S(1)}, u32[]{:S(2)}, u32[]{:S(2)}) collective-permute-start(f32[64,512]{1,0:T(8,128)S(1)} %get-tuple-element.35), channel_id=1, source_target_pairs={{0,8},{8,16},{16,24},{24,0},{1,9},{9,17},{17,25},{25,1},{2,10},{10... | collective-permute-start | bytes 393224 | tf_op jit(solution)/shard_map/ppermute | solution.py:433
  11.0 1.2 %later.1 = (f32[16,128,128]{2,1,0:T(8,128)S(1)}, f32[64,512]{1,0:T(8,128)S(1)}, f32[64,512]{1,0:T(8,128)S(1)}) custom-call(f32[16,128,128]{2,1,0:T(8,128)S(1)} %bitcast.5, f32[16,128,128]{2,1,0:T(8,128)S(1)} %copy-done, f32[4,128,128]{2,1,0:T(8,128)S(1)} %get-tuple-element.28.ab_ref.refs_1_, f32[4,128,128]{2,1,0:T(8,128)S(1)} %get-tuple-element.29.gb_ref, ...), custom_call_target="tpu_custom_call" | custom-call | flops 10000000000 | bytes 1000000000 | tf_op jit(solution)/shard_map/later/pallas_call | solution.py:148
  12.3 0.6 %collective-permute-done.2.refs_4_.refs_12_.refs_2_ = f32[64,640]{1,0:T(8,128)S(1)} collective-permute-done((f32[64,640]{1,0:T(8,128)S(1)}, f32[64,640]{1,0:T(8,128)S(1)}, u32[]{:S(2)}, u32[]{:S(2)}) %collective-permute-start.2) | collective-permute-done | bytes 163872 | tf_op jit(solution)/shard_map/ppermute | solution.py:433
  12.8 0.8 %second.2 = (f32[10,128,128]{2,1,0:T(8,128)S(1)}, f32[8,128,128]{2,1,0:T(8,128)S(1)}, f32[64,512]{1,0:T(8,128)S(1)}) custom-call(f32[16,128,128]{2,1,0:T(8,128)S(1)} %bitcast.6, f32[4,128,128]{2,1,0:T(8,128)S(1)} %get-tuple-element.28.ab_ref.refs_1_, f32[16,128,128]{2,1,0:T(8,128)S(1)} %copy-done, f32[16,128,128]{2,1,0:T(8,128)S(1)} %get-tuple-element.31.refs_3_, ...), custom_call_target="tpu_custom_call" | custom-call | flops 10000000000 | bytes 1000000000 | tf_op jit(solution)/shard_map/second/pallas_call | solution.py:148
  13.6 1.5 %collective-permute-start.5 = (f32[64,512]{1,0:T(8,128)S(1)}, f32[64,512]{1,0:T(8,128)S(1)}, u32[]{:S(2)}, u32[]{:S(2)}) collective-permute-start(f32[64,512]{1,0:T(8,128)S(1)} %get-tuple-element.44), channel_id=1, source_target_pairs={{0,8},{8,16},{16,24},{24,0},{1,9},{9,17},{17,25},{25,1},{2,10},{10... | collective-permute-start | bytes 393224 | tf_op jit(solution)/shard_map/ppermute | solution.py:433
  15.1 0.6 %collective-permute-done.3.refs_4_.refs_3_ = f32[64,512]{1,0:T(8,128)S(1)} collective-permute-done((f32[64,512]{1,0:T(8,128)S(1)}, f32[64,512]{1,0:T(8,128)S(1)}, u32[]{:S(2)}, u32[]{:S(2)}) %collective-permute-start.3) | collective-permute-done | bytes 131104 | tf_op jit(solution)/shard_map/ppermute | solution.py:433
  15.7 0.7 %second.3 = (f32[8,128,128]{2,1,0:T(8,128)S(1)}, f32[8,128,128]{2,1,0:T(8,128)S(1)}, f32[64,512]{1,0:T(8,128)S(1)}) custom-call(f32[16,128,128]{2,1,0:T(8,128)S(1)} %bitcast.7, f32[4,128,128]{2,1,0:T(8,128)S(1)} %get-tuple-element.28.ab_ref.refs_1_, f32[16,128,128]{2,1,0:T(8,128)S(1)} %copy-done, f32[16,128,128]{2,1,0:T(8,128)S(1)} %get-tuple-element.31.refs_3_, ...), custom_call_target="tpu_custom_call" | custom-call | flops 10000000000 | bytes 1000000000 | tf_op jit(solution)/shard_map/second/pallas_call | solution.py:148
  16.4 1.4 %collective-permute-start.4 = (f32[64,512]{1,0:T(8,128)S(1)}, f32[64,512]{1,0:T(8,128)S(1)}, u32[]{:S(2)}, u32[]{:S(2)}) collective-permute-start(f32[64,512]{1,0:T(8,128)S(1)} %get-tuple-element.41), channel_id=1, source_target_pairs={{0,8},{8,16},{16,24},{24,0},{1,9},{9,17},{17,25},{25,1},{2,10},{10... | collective-permute-start | bytes 393224 | tf_op jit(solution)/shard_map/ppermute | solution.py:433
  17.7 1.0 %join.1 = (f32[1,16,128,128]{3,2,1,0:T(8,128)}, f32[64,512]{1,0:T(8,128)S(1)}, f32[64,512]{1,0:T(8,128)S(1)}) custom-call(f32[8,128,128]{2,1,0:T(8,128)S(1)} %get-tuple-element.34.refs_0_, f32[8,128,128]{2,1,0:T(8,128)S(1)} %get-tuple-element.39.refs_1_, f32[64,640]{1,0:T(8,128)S(1)} %collective-permute-done.2.refs_4_.refs_12_.refs_2_, ...), custom_call_target="tpu_custom_call" | custom-call | flops 10000000000 | bytes 1000000000 | tf_op jit(solution)/shard_map/join/pallas_call | solution.py:148
  18.8 1.1 %collective-permute-done.5.refs_0_ = f32[64,512]{1,0:T(8,128)S(1)} collective-permute-done((f32[64,512]{1,0:T(8,128)S(1)}, f32[64,512]{1,0:T(8,128)S(1)}, u32[]{:S(2)}, u32[]{:S(2)}) %collective-permute-start.5) | collective-permute-done | bytes 131104 | tf_op jit(solution)/shard_map/ppermute | solution.py:433
  19.8 1.0 %last.2.refs_7_ = f32[1,16,128,128]{3,2,1,0:T(8,128)} custom-call(f32[64,512]{1,0:T(8,128)S(1)} %collective-permute-done.5.refs_0_, bf16[128,192]{1,0:T(8,128)(2,1)S(1)} %copy-done.5, bf16[384,256]{1,0:T(8,128)(2,1)S(1)} %copy-done.4, f32[16,128,128]{2,1,0:T(8,128)S(1)} %bitcast.8, f32[64,512]{1,0:T(8,128)S(1)} %get-tuple-element.45.refs_4_, ...), custom_call_target="tpu_custom_call" | custom-call | flops 10000000000 | bytes 1000000000 | tf_op jit(solution)/shard_map/last/pallas_call | solution.py:148
  20.9 1.5 %collective-permute-done.4.refs_0_ = f32[64,512]{1,0:T(8,128)S(1)} collective-permute-done((f32[64,512]{1,0:T(8,128)S(1)}, f32[64,512]{1,0:T(8,128)S(1)}, u32[]{:S(2)}, u32[]{:S(2)}) %collective-permute-start.4) | collective-permute-done | bytes 131104 | tf_op jit(solution)/shard_map/ppermute | solution.py:433
  (11 shorter events, 0.1 us)
Async XLA Ops:
  0.6 4.2 %copy-start = (f32[16,128,128]{2,1,0:T(8,128)S(1)}, f32[16,128,128]{2,1,0:T(8,128)}, u32[]{:S(2)}) copy-start(f32[16,128,128]{2,1,0:T(8,128)} %refs_2_.5) | copy-start | bytes 3145732
  0.6 4.2 %copy-start.1 = (f32[1,16,128,128]{3,2,1,0:T(8,128)S(1)}, f32[1,16,128,128]{3,2,1,0:T(8,128)}, u32[]{:S(2)}) copy-start(f32[1,16,128,128]{3,2,1,0:T(8,128)} %param.6) | copy-start | bytes 3145732
  0.6 4.2 %copy-start.2 = (bf16[256,256]{1,0:T(8,128)(2,1)S(1)}, bf16[256,256]{1,0:T(8,128)(2,1)}, u32[]{:S(2)}) copy-start(bf16[256,256]{1,0:T(8,128)(2,1)} %constant.8.clone.fz_ref.refs_6_) | copy-start | bytes 393220
  0.7 4.1 %copy-start.3 = (bf16[128,256]{1,0:T(8,128)(2,1)S(1)}, bf16[128,256]{1,0:T(8,128)(2,1)}, u32[]{:S(2)}) copy-start(bf16[128,256]{1,0:T(8,128)(2,1)} %constant.9.clone.fy_ref.refs_7_) | copy-start | bytes 196612
  1.8 6.7 %collective-permute-start.1 = (f32[3,128,128]{2,1,0:T(8,128)S(1)}, f32[3,128,128]{2,1,0:T(8,128)S(1)}, u32[]{:S(2)}, u32[]{:S(2)}) collective-permute-start(f32[3,128,128]{2,1,0:T(8,128)S(1)} %pack.1.after), channel_id=1, source_target_pairs={{0,16},{1,2},{2,1},{3,4},{4,3},{5,6},{6,5},{7,23},{8,24},{9,10},{1... | collective-permute-start | bytes 589832 | tf_op jit(solution)/shard_map/ppermute | solution.py:438
  5.6 7.2 %collective-permute-start.2 = (f32[64,640]{1,0:T(8,128)S(1)}, f32[64,640]{1,0:T(8,128)S(1)}, u32[]{:S(2)}, u32[]{:S(2)}) collective-permute-start(f32[64,640]{1,0:T(8,128)S(1)} %get-tuple-element.32), channel_id=1, source_target_pairs={{0,8},{8,16},{16,24},{24,0},{1,9},{9,17},{17,25},{25,1},{2,10},{10... | collective-permute-start | bytes 491528 | tf_op jit(solution)/shard_map/ppermute | solution.py:433
  7.2 1.4 %collective-permute-start = (f32[3,128,128]{2,1,0:T(8,128)S(1)}, f32[3,128,128]{2,1,0:T(8,128)S(1)}, u32[]{:S(2)}, u32[]{:S(2)}) collective-permute-start(f32[3,128,128]{2,1,0:T(8,128)S(1)} %get-tuple-element.24), channel_id=1, source_target_pairs={{0,1},{1,0},{2,3},{3,2},{4,5},{5,4},{6,7},{7,6},{8,9},{9,8},{10,11... | collective-permute-start | bytes 589832 | tf_op jit(solution)/shard_map/ppermute | solution.py:450
  9.1 6.5 %collective-permute-start.3 = (f32[64,512]{1,0:T(8,128)S(1)}, f32[64,512]{1,0:T(8,128)S(1)}, u32[]{:S(2)}, u32[]{:S(2)}) collective-permute-start(f32[64,512]{1,0:T(8,128)S(1)} %get-tuple-element.35), channel_id=1, source_target_pairs={{0,8},{8,16},{16,24},{24,0},{1,9},{9,17},{17,25},{25,1},{2,10},{10... | collective-permute-start | bytes 393224 | tf_op jit(solution)/shard_map/ppermute | solution.py:433
  11.0 1.8 %copy-start.4 = (bf16[384,256]{1,0:T(8,128)(2,1)S(1)}, bf16[384,256]{1,0:T(8,128)(2,1)}, u32[]{:S(2)}) copy-start(bf16[384,256]{1,0:T(8,128)(2,1)} %constant.11.clone.refs_9_.refs_2_) | copy-start | bytes 589828
  11.0 1.8 %copy-start.5 = (bf16[128,192]{1,0:T(8,128)(2,1)S(1)}, bf16[128,192]{1,0:T(8,128)(2,1)}, u32[]{:S(2)}) copy-start(bf16[128,192]{1,0:T(8,128)(2,1)} %constant.10.clone.refs_8_.refs_1_) | copy-start | bytes 147460
  13.6 6.2 %collective-permute-start.5 = (f32[64,512]{1,0:T(8,128)S(1)}, f32[64,512]{1,0:T(8,128)S(1)}, u32[]{:S(2)}, u32[]{:S(2)}) collective-permute-start(f32[64,512]{1,0:T(8,128)S(1)} %get-tuple-element.44), channel_id=1, source_target_pairs={{0,8},{8,16},{16,24},{24,0},{1,9},{9,17},{17,25},{25,1},{2,10},{10... | collective-permute-start | bytes 393224 | tf_op jit(solution)/shard_map/ppermute | solution.py:433
  16.4 6.0 %collective-permute-start.4 = (f32[64,512]{1,0:T(8,128)S(1)}, f32[64,512]{1,0:T(8,128)S(1)}, u32[]{:S(2)}, u32[]{:S(2)}) collective-permute-start(f32[64,512]{1,0:T(8,128)S(1)} %get-tuple-element.41), channel_id=1, source_target_pairs={{0,8},{8,16},{16,24},{24,0},{1,9},{9,17},{17,25},{25,1},{2,10},{10... | collective-permute-start | bytes 393224 | tf_op jit(solution)/shard_map/ppermute | solution.py:433
